TPU v7x, 32 devices: a whole 2x2x4 slice. The times are simulated.
32 devices in a mesh: dp: 8 (over y, x, core), tensor: 4 (over z).
Axes of the slice: x: 2, y: 2, z: 4, core: 2. Of those that a mesh axis runs over, the one named last changes fastest.
Arguments:
- train_hidden: bfloat16 [64, 128, 14336], P('dp', None, 'tensor')
- train_grads: bfloat16 [64, 128, 4096], P('dp', None, 'tensor'), may hold values from -6 to 6
- train_ids: int32 [64, 128], P('dp'), may hold values from 0 to 128004, as said below
- query_hidden: bfloat16 [16, 128, 14336], P(None, 'dp', 'tensor')
- query_grads: bfloat16 [16, 128, 4096], P(None, 'dp', 'tensor'), may hold values from -6 to 6
- query_ids: int32 [16, 128], P(None, 'dp'), may hold values from 0 to 128004, as said below
- proj_in: bfloat16 [14336, 64], P('tensor'), may hold values from -0.046875 to 0.046875
- proj_out: bfloat16 [4096, 64], P('tensor'), may hold values from -0.09375 to 0.09375
Outputs:
- scores: float32 [16, 64], P(None, ('dp', 'tensor'))
Inputs may be any that keep to these rules, and one draw needn't show every extreme that they name: `train_ids`: id 128004 marks padding and appears only at the end of a sequence; the first 32 tokens of every training sequence are not padding; other ids lie below 128000. `query_ids`: id 128004 marks padding and appears only at the end of a query; the first 32 tokens of every query are not padding; other ids lie below 128000.
All inputs are finite; a program needn't handle non-finite values.
Results may differ from a plain program's by a relative error of at most 0.0003.
Values sent between devices are 32-bit elements; how exact they have to be, the bound alone decides.
No kernel may reach another device: no remote copies, remote signals or barrier semaphores. Data moves between devices by JAX's collectives and lax.ppermute only.
A program may use at most 128 MiB of HBM per device.

v0:
```python
import jax
import jax.numpy as jnp
from jax import lax
from jax.sharding import PartitionSpec as P

ITERS = 3


PAD_ID = 128004
DAMP = 0.1


def per_device(
    train_hidden, train_grads, train_ids, query_hidden, query_grads, query_ids, proj_in, proj_out
):
    tensor_size = lax.axis_size("tensor")
    tensor_at = lax.axis_index("tensor")
    seq_local, seq_len, ff_part = train_hidden.shape
    width_part = train_grads.shape[2]
    rank = proj_in.shape[1]
    nquery, qtok, unused_ff = query_hidden.shape
    total_train = seq_local * lax.axis_size("dp")
    seq_share = seq_local // tensor_size
    tok_share = qtok // tensor_size
    side_in = jnp.dot(
        train_hidden.reshape(-1, ff_part), proj_in, preferred_element_type=jnp.float32
    )
    side_out = jnp.dot(
        train_grads.reshape(-1, width_part), proj_out, preferred_element_type=jnp.float32
    )
    train_in = side_in.reshape(seq_local, seq_len, rank)
    train_out = side_out.reshape(seq_local, seq_len, rank)
    side_in = jnp.einsum("qtf,fr->tqr", query_hidden, proj_in, preferred_element_type=jnp.float32)
    side_out = jnp.einsum("qtd,dr->tqr", query_grads, proj_out, preferred_element_type=jnp.float32)
    query_in = side_in
    query_out = side_out
    train_in, train_out, query_in, query_out = (
        lax.psum_scatter(train_in, "tensor", scatter_dimension=0, tiled=True),
        lax.psum_scatter(train_out, "tensor", scatter_dimension=0, tiled=True),
        lax.psum_scatter(query_in, "tensor", scatter_dimension=0, tiled=True),
        lax.psum_scatter(query_out, "tensor", scatter_dimension=0, tiled=True),
    )
    local_ids = lax.dynamic_slice_in_dim(train_ids, tensor_at * seq_share, seq_share, 0)
    mask = (local_ids != PAD_ID).astype(jnp.float32)
    outer = jnp.einsum(
        "sta,stb->sab", train_in * mask[:, :, None], train_out, precision=lax.Precision.HIGHEST
    )
    examples = outer.reshape(seq_share, rank * rank) / jnp.sum(mask, axis=1)[:, None]
    local_ids = lax.dynamic_slice_in_dim(query_ids, tensor_at * tok_share, tok_share, 1)
    mask = (local_ids != PAD_ID).astype(jnp.float32)
    outer = jnp.einsum(
        "tqa,tqb->qab", query_in * mask.T[:, :, None], query_out, precision=lax.Precision.HIGHEST
    )
    partial_value = outer.reshape(nquery, rank * rank)
    counts = jnp.sum(mask, axis=1)
    partial_value, counts, trace = lax.psum(
        (partial_value, counts, jnp.sum(examples * examples)), ("dp", "tensor")
    )
    queries = partial_value / counts[:, None]
    damping = DAMP * (trace / total_train) / (rank * rank)
    solved = jnp.zeros_like(queries)
    residual = queries
    direction = queries
    norm_now = jnp.sum(residual * residual, axis=1)
    for step in range(ITERS):
        inner = jnp.dot(direction, examples.T, precision=lax.Precision.HIGHEST)
        term = jnp.dot(inner, examples, precision=lax.Precision.HIGHEST)
        image = direction + lax.psum(term, ("dp", "tensor")) / (total_train * damping)
        alpha = norm_now / jnp.sum(direction * image, axis=1)
        solved = solved + alpha[:, None] * direction
        residual = residual - alpha[:, None] * image
        fresh = jnp.sum(residual * residual, axis=1)
        direction = residual + (fresh / norm_now)[:, None] * direction
        norm_now = fresh
    return jnp.dot(solved, examples.T, precision=lax.Precision.HIGHEST)


def solution(mesh):
    return jax.shard_map(
        per_device,
        mesh=mesh,
        in_specs=(
            P("dp", None, "tensor"),
            P("dp", None, "tensor"),
            P("dp", None),
            P(None, "dp", "tensor"),
            P(None, "dp", "tensor"),
            P(None, "dp"),
            P("tensor", None),
            P("tensor", None),
        ),
        out_specs=P(None, ("dp", "tensor")),
        check_vma=False,
    )
```

profile of v0, /device:TPU:0, one launch (start us, length us, event | category | flops | bytes accessed | tf_op | source)
XLA Modules:
  0.0 618.6 jit_solution(8762879594878134548)
XLA Ops:
  6.5 0.0 copy-start
  6.5 0.0 copy-start.2
  6.5 0.0 copy-start.3
  6.5 0.0 copy-start.5
  6.5 0.0 reduce-scatter.5.cloned.1.call-start
  6.6 3.5 fusion.2
  10.1 0.0 reduce-scatter.5.cloned.1.call-update
  10.2 0.0 reduce-scatter.7.cloned.1.call-start
  10.2 0.0 copy-done.3
  10.2 0.0 copy-done.5
  10.2 1.1 convolution_bitcast_fusion
  11.3 0.0 reduce-scatter.7.cloned.1.call-update
  11.3 0.0 reduce-scatter.9.cloned.1.call-start
  11.4 0.0 copy-done.2
  11.4 6.1 fusion.6
  17.5 0.0 copy-start.4
  17.5 0.0 reduce-scatter.9.cloned.1.call-update
  17.5 0.0 reduce-scatter.11.cloned.1.call-start
  17.6 0.0 copy-done
  17.6 1.5 fusion.16
  19.0 0.0 reduce-scatter.11.cloned.1.call-update
  19.1 0.0 all-reduce.6.cloned.1.call-start
  19.1 0.0 copy-done.4
  19.1 0.2 convert_reduce_fusion
  19.3 0.1 copy.9
  19.4 0.8 fusion.34
  20.2 12.0 %reduce-scatter.5.cloned.1.call-done = f32[4,16,64]{2,1,0:T(8,128)} async-done(((f32[16,16,64]{2,1,0:T(8,128)}), f32[4,16,64]{2,1,0:T(8,128)}) %reduce-scatter.5.cloned.1.call-update) | async-done | bytes 16400 | tf_op jit(solution)/shard_map/reduce_scatter | solution.py:40
  32.2 0.8 broadcast_multiply_fusion
  33.1 18.9 %reduce-scatter.7.cloned.1.call-done = f32[4,16,64]{2,1,0:T(8,128)} async-done(((f32[16,16,64]{2,1,0:T(8,128)}), f32[4,16,64]{2,1,0:T(8,128)}) %reduce-scatter.7.cloned.1.call-update) | async-done | bytes 16400 | tf_op jit(solution)/shard_map/reduce_scatter | solution.py:41
  51.9 1.8 fusion.24
  53.7 0.9 reshape.47
  54.6 0.0 all-reduce.6.cloned.1.call-update
  54.6 0.0 all-reduce.8.cloned.1.call-start
  54.7 17.4 %reduce-scatter.9.cloned.1.call-done = f32[2,128,64]{1,2,0:T(8,128)} async-done(((f32[8,128,64]{1,2,0:T(8,128)}), f32[2,128,64]{1,2,0:T(8,128)}) %reduce-scatter.9.cloned.1.call-update) | async-done | bytes 65552 | tf_op jit(solution)/shard_map/reduce_scatter | solution.py:38
  72.1 20.1 %reduce-scatter.11.cloned.1.call-done = f32[2,128,64]{1,2,0:T(8,128)} async-done(((f32[8,128,64]{1,2,0:T(8,128)}), f32[2,128,64]{1,2,0:T(8,128)}) %reduce-scatter.11.cloned.1.call-update) | async-done | bytes 65552 | tf_op jit(solution)/shard_map/reduce_scatter | solution.py:39
  92.2 1.7 multiply_reduce_fusion.5
  93.9 38.8 %all-reduce = (f32[16]{0:T(128)S(1)}, f32[]{:T(128)}) all-reduce(f32[16]{0:T(128)S(1)} %get-tuple-element.13, f32[]{:T(128)} %get-tuple-element.17), channel_id=1, replica_groups=mesh['dp'=8,'tensor'=4] {'dp','tensor'}, use_global_device_ids=true, to_apply=%region_4.0 | all-reduce | flops 17 | bytes 136 | tf_op jit(solution)/shard_map/psum | solution.py:56
  132.7 0.1 reshape.48
  132.8 88.0 %all-reduce.6.cloned.1.call-done = f32[16,4096]{1,0:T(8,128)} async-done(((f32[16,4096]{1,0:T(8,128)}), f32[16,4096]{1,0:T(8,128)}) %all-reduce.6.cloned.1.call-update) | async-done | bytes 262160 | tf_op jit(solution)/shard_map/psum | solution.py:56
  220.8 0.0 copy-start.1
  220.8 1.5 fusion.33
  222.3 1.1 fusion.32
  223.5 0.0 all-reduce.8.cloned.1.call-update
  223.5 0.0 all-reduce.10.cloned.1.call-start
  224.2 126.1 %all-reduce.8.cloned.1.call-done = f32[16,4096]{1,0:T(8,128)} async-done(((f32[16,4096]{1,0:T(8,128)}), f32[16,4096]{1,0:T(8,128)}) %all-reduce.8.cloned.1.call-update) | async-done | bytes 262160 | tf_op jit(solution)/shard_map/psum | solution.py:68
  350.3 0.0 copy-done.1
  350.3 1.2 multiply_reduce_fusion.3
  351.5 1.2 multiply_reduce_fusion.2
  352.7 0.1 multiply_add_fusion.1
  352.8 0.5 fusion.31
  353.3 1.1 fusion.30
  354.5 0.0 all-reduce.10.cloned.1.call-update
  354.5 0.0 all-reduce.12.cloned.1.call-start
  354.5 125.4 %all-reduce.10.cloned.1.call-done = f32[16,4096]{1,0:T(8,128)} async-done(((f32[16,4096]{1,0:T(8,128)}), f32[16,4096]{1,0:T(8,128)}) %all-reduce.10.cloned.1.call-update) | async-done | bytes 262160 | tf_op jit(solution)/shard_map/psum | solution.py:68
  479.9 1.1 multiply_reduce_fusion.1
  481.0 1.2 multiply_reduce_fusion
  482.2 0.5 fusion.28
  482.7 1.1 fusion.29
  483.9 0.0 all-reduce.12.cloned.1.call-update
  483.9 125.6 %all-reduce.12.cloned.1.call-done = f32[16,4096]{1,0:T(8,128)} async-done(((f32[16,4096]{1,0:T(8,128)}), f32[16,4096]{1,0:T(8,128)}) %all-reduce.12.cloned.1.call-update) | async-done | bytes 262160 | tf_op jit(solution)/shard_map/psum | solution.py:68
  609.5 1.2 fusion.9
  610.7 1.1 fusion.10
  (6 shorter events, 0.0 us)
Async XLA Ops:
  6.5 11.0 %copy-start = (bf16[8,128,1024]{2,1,0:T(8,128)(2,1)S(1)}, bf16[8,128,1024]{2,1,0:T(8,128)(2,1)}, u32[]{:S(2)}) copy-start(bf16[8,128,1024]{2,1,0:T(8,128)(2,1)} %param.9) | copy-start | bytes 6291460
  6.5 4.8 copy-start.2
  6.5 3.7 copy-start.3
  6.5 3.7 copy-start.5
  6.5 25.7 %reduce-scatter.5.cloned.1.call-start = ((), (), s32[]{:S(2)}) async-start(), calls=%async_computation.4 | async-start | bytes 163840 | tf_op jit(solution)/shard_map/reduce_scatter | solution.py:40
  10.2 41.8 %reduce-scatter.7.cloned.1.call-start = ((), (), s32[]{:S(2)}) async-start(), calls=%async_computation.5 | async-start | bytes 163840 | tf_op jit(solution)/shard_map/reduce_scatter | solution.py:41
  11.3 60.7 %reduce-scatter.9.cloned.1.call-start = ((), (), s32[]{:S(2)}) async-start(), calls=%async_computation.7 | async-start | bytes 327680 | tf_op jit(solution)/shard_map/reduce_scatter | solution.py:38
  17.5 1.6 copy-start.4
  17.5 74.7 %reduce-scatter.11.cloned.1.call-start = ((), (), s32[]{:S(2)}) async-start(), calls=%async_computation.8 | async-start | bytes 327680 | tf_op jit(solution)/shard_map/reduce_scatter | solution.py:39
  19.1 201.7 %all-reduce.6.cloned.1.call-start = ((), (), s32[]{:S(2)}) async-start(), calls=%async_computation.6 | async-start | bytes 524288 | tf_op jit(solution)/shard_map/psum | solution.py:56
  54.6 295.7 %all-reduce.8.cloned.1.call-start = ((), (), s32[]{:S(2)}) async-start(), calls=%async_computation.9 | async-start | bytes 524288 | tf_op jit(solution)/shard_map/psum | solution.py:68
  220.8 129.5 %copy-start.1 = (f32[16,4096]{1,0:T(8,128)S(1)}, f32[16,4096]{1,0:T(8,128)}, u32[]{:S(2)}) copy-start(f32[16,4096]{1,0:T(8,128)} %all-reduce.6.cloned.1.call-done) | copy-start | bytes 786436
  223.5 256.4 %all-reduce.10.cloned.1.call-start = ((), (), s32[]{:S(2)}) async-start(), calls=%async_computation.10 | async-start | bytes 524288 | tf_op jit(solution)/shard_map/psum | solution.py:68
  354.5 255.0 %all-reduce.12.cloned.1.call-start = ((), (), s32[]{:S(2)}) async-start(), calls=%async_computation.11 | async-start | bytes 524288 | tf_op jit(solution)/shard_map/psum | solution.py:68
Sparse Core Ops, SparseCore 0:
  10.3 21.8 reduce-scatter.4
  34.6 17.3 reduce-scatter.6
  54.2 17.8 reduce-scatter.8
  74.3 17.8 reduce-scatter.10
  97.5 123.1 all-reduce.5
  226.1 124.1 all-reduce.7
  355.8 124.0 all-reduce.9
  485.4 124.0 all-reduce.11
where the time goes:
time: 619 us
  waiting for transfers between devices  534 us (86%)
  blocking collectives  38.8 us (6%)
  matrix products  22.8 us (4%)
  between operations  14.2 us (2%)
  other arithmetic  7.8 us (1%)
    psum x3, waiting for transfers between devices, per_device(): lax.psum(term, ('dp', 'tensor')) / (total_train * damping)  377 us
    psum x1, waiting for transfers between devices, per_device(): lax.psum((partial_value, counts, jnp.sum(examples * examples)), ('dp', 't...  88 us
    psum x1, blocking collectives, per_device(): lax.psum((partial_value, counts, jnp.sum(examples * examples)), ('dp', 't...  38.8 us
    reduce_scatter x1, waiting for transfers between devices, per_device(): lax.psum_scatter(train_out, 'tensor', scatter_dimension=0, tiled=True)  20.1 us
    reduce_scatter x1, waiting for transfers between devices, per_device(): lax.psum_scatter(query_out, 'tensor', scatter_dimension=0, tiled=True)  18.9 us
    reduce_scatter x1, waiting for transfers between devices, per_device(): lax.psum_scatter(train_in, 'tensor', scatter_dimension=0, tiled=True)  17.4 us
  transfers between devices with their start and end apart: 8, of which 8 were waited for; matrix products, arithmetic and copies ran while one was open for 2% of the time, Pallas kernels for 0%

commit v1 on v0

v1 whole, which is shorter than its diff:
```python
import functools

import jax
import jax.numpy as jnp
from jax import lax
from jax.experimental import pallas as pl
from jax.experimental.pallas import tpu as pltpu
from jax.sharding import PartitionSpec as P

ITERS = 3
PAD_ID = 128004
DAMP = 0.1
HIGHEST = lax.Precision.HIGHEST
F32 = jnp.float32
VMEM_LIMIT = 32 * 1024 * 1024
NT = (((1,), (1,)), ((), ()))
SMEM_SPEC = pl.BlockSpec(memory_space=pltpu.SMEM)
VMEM_SPEC = pl.BlockSpec(memory_space=pltpu.VMEM)
HBM_SPEC = pl.BlockSpec(memory_space=pltpu.HBM)


def call(kernel, out_shape, name, **kwargs):
    return pl.pallas_call(
        kernel,
        out_shape=out_shape,
        name=name,
        compiler_params=pltpu.CompilerParams(vmem_limit_bytes=VMEM_LIMIT),
        **kwargs,
    )


def swap(value, dp_flip, tensor_flip):
    groups, parts = lax.axis_size("dp"), lax.axis_size("tensor")
    flip = dp_flip * parts + tensor_flip
    return lax.ppermute(value, ("dp", "tensor"), [(i, i ^ flip) for i in range(groups * parts)])


def project_kernel(mesh, parts, hops, tile, at_ref, th_ref, tg_ref, qh_ref, qg_ref, pin_ref, pout_ref, *refs):
    out_refs = refs[: len(hops)]
    hid, grad, pin, pout, sems = refs[len(hops) :]
    at = at_ref[0]
    trows = th_ref.shape[0] // parts
    qrows = qh_ref.shape[0] // parts
    rows = trows + qrows
    rank = pin_ref.shape[0]
    sides = ((th_ref, qh_ref, hid, pin_ref, pin), (tg_ref, qg_ref, grad, pout_ref, pout))
    chunks = []
    for side, (_, _, buf, _, _) in enumerate(sides):
        start = 0
        while start < buf.shape[1]:
            size = min(2 * tile if not chunks else 4 * tile, buf.shape[1] - start)
            chunks.append((side, start, size))
            start += size
    copies = []
    for chunk, (side, start, size) in enumerate(chunks):
        train, query, buf, weight, held = sides[side]
        cols = pl.ds(start, size)
        pairs = [(weight.at[:, cols], held.at[:, cols])]
        for slot, hop in enumerate(hops):
            to = at ^ hop
            tsrc = pl.ds(pl.multiple_of(to * trows, trows), trows)
            qsrc = pl.ds(pl.multiple_of(to * qrows, qrows), qrows)
            pairs.append((train.at[tsrc, cols], buf.at[pl.ds(slot * rows, trows), cols]))
            pairs.append((query.at[qsrc, cols], buf.at[pl.ds(slot * rows + trows, qrows), cols]))
        copies.append(
            [pltpu.make_async_copy(src, dst, sems.at[chunk, k]) for k, (src, dst) in enumerate(pairs)]
        )
        for copy in copies[-1]:
            copy.start()

    def multiply(*sums):
        count = 0
        for (side, start, size), waits in zip(chunks, copies):
            _, _, buf, _, held = sides[side]
            for copy in waits:
                copy.wait()
            for col in range(start, start + size, tile):
                unit, turn = count % len(sums), count // len(sums)
                count += 1
                weight = [held[:, col : col + tile]]
                if side:
                    weight.insert(0, jnp.zeros((side * rank, tile), held.dtype))
                weight.append(jnp.zeros((tile - (side + 1) * rank, tile), held.dtype))
                weight = jnp.concatenate(weight, axis=0)
                pltpu.matmul_push_rhs(weight, turn % 2, unit, transpose=True)
                pltpu.matmul_acc_lhs(sums[unit], buf[:, col : col + tile], load_staged_rhs=turn % 2)
        total = pltpu.matmul_pop(sums[0])[:, : 2 * rank]
        for unit in sums[1:]:
            total = total + pltpu.matmul_pop(unit)[:, : 2 * rank]
        for slot, ref in enumerate(out_refs):
            ref[...] = total[slot * rows : (slot + 1) * rows]

    with jax.sharding.use_abstract_mesh(mesh.abstract_mesh):
        sums = [pltpu.ACC(unit)((hid.shape[0], tile), F32) for unit in range(2)]
        pl.run_scoped(multiply, *sums)


def project(mesh, at, arrays, parts, hops):
    train, _, query, _, pin, pout = arrays
    rank, ff = pin.shape
    width = pout.shape[1]
    rows = (train.shape[0] + query.shape[0]) // parts
    held = rows * len(hops)
    bf16 = jnp.bfloat16
    tile = 256
    return call(
        functools.partial(project_kernel, mesh, parts, hops, tile),
        [jax.ShapeDtypeStruct((rows, 2 * rank), F32)] * len(hops),
        "project_" + "_".join(str(hop) for hop in hops),
        in_specs=[SMEM_SPEC] + [HBM_SPEC] * 6,
        out_specs=[VMEM_SPEC] * len(hops),
        scratch_shapes=[
            pltpu.VMEM((held, ff), bf16),
            pltpu.VMEM((held, width), bf16),
            pltpu.VMEM((rank, ff), bf16),
            pltpu.VMEM((rank, width), bf16),
            pltpu.SemaphoreType.DMA((8, 1 + 2 * len(hops))),
        ],
        cost_estimate=pl.CostEstimate(
            flops=2 * held * (ff + width) * rank,
            bytes_accessed=2 * (held + rank) * (ff + width),
            transcendentals=0,
        ),
    )(at, *[pltpu.with_memory_space_constraint(array, pltpu.HBM) for array in arrays])


def fold(outer, start, half):
    return jnp.concatenate([outer[start : start + half], outer[start + half : start + 2 * half]], axis=1)


def outer_kernel(share, qshare, at_ref, quarter_ref, ids_ref, qids_ref, *refs):
    tok_refs, (keep_ref, send_ref, scratch) = refs[:-3], refs[-3:]
    at, mine = at_ref[0], quarter_ref[0]
    seq_len = ids_ref.shape[1]
    rank = tok_refs[0].shape[1] // 2
    qtok = qids_ref.shape[1]
    half = rank // 8

    def product(tokens, left):
        return jnp.dot(left, tokens[:, rank:], precision=HIGHEST, preferred_element_type=F32)

    def total(start, rows):
        value = tok_refs[0][start : start + rows, :]
        for ref in tok_refs[1:]:
            value = value + ref[start : start + rows, :]
        return value

    def store(slot, outer):
        for quarter in range(4):
            scratch[quarter, slot] = fold(outer, quarter * 2 * half, half)

    for seq in range(share):
        tokens = total(seq * seq_len, seq_len)
        mask = (ids_ref[pl.ds(at * share + seq, 1), :] != PAD_ID).astype(F32)
        outer = product(tokens, tokens.T[:rank] * mask)
        store(seq, outer / jnp.sum(mask, axis=1, keepdims=True))
    for quarter in range(4):
        scratch[quarter, share + qshare] = jnp.ones((half, 2 * rank), F32)
    for query in range(qshare):
        tokens = total(share * seq_len + query * qtok, qtok)
        mask = (qids_ref[pl.ds(at * qshare + query, 1), :] != PAD_ID).astype(F32)
        store(share + query, product(tokens, tokens.T[:rank] * mask))
        count = jnp.broadcast_to(jnp.sum(mask, axis=1, keepdims=True), (1, 2 * rank))
        for quarter in range(4):
            scratch[quarter, share + qshare, query : query + 1, :] = count
    for flip in range(2):
        keep_ref[flip] = scratch[mine ^ flip]
        send_ref[flip] = scratch[mine ^ 2 ^ flip]


def gram_kernel(qshare, at_ref, *refs):
    piece_refs, (out_ref, scratch) = refs[:-2], refs[-2:]
    at = at_ref[0]
    rows, half, lanes = piece_refs[0].shape
    nex = rows - qshare - 1
    ntrain = nex * len(piece_refs)
    nquery = scratch.shape[0]
    for hop, ref in enumerate(piece_refs):
        counts = ref[nex + qshare]
        for query in range(qshare):
            scratch[(at ^ hop) * qshare + query] = ref[nex + query] / counts[query : query + 1, :]
    total = None
    for row in range(half):
        both = jnp.concatenate(
            [ref[:nex, row, :] for ref in piece_refs] + [scratch[:, row, :]], axis=0
        )
        high = both.astype(jnp.bfloat16)
        low = (both - high.astype(F32)).astype(jnp.bfloat16)
        left = jnp.concatenate([high, low], axis=0)
        product = lax.dot_general(left, high, NT, preferred_element_type=F32)
        product = product + lax.dot_general(left, low, NT, preferred_element_type=F32)
        total = product if total is None else total + product
    size = ntrain + nquery
    total = total[:size] + total[size:]
    if folds(ntrain):
        half = ntrain // 2
        out_ref[:half, :] = jnp.concatenate([total[:half, :ntrain], total[half:ntrain, :ntrain]], axis=1)
        out_ref[half:, :size] = total[ntrain:]
        out_ref[half:, size:] = jnp.zeros((nquery, 2 * ntrain - size), F32)
    else:
        out_ref[...] = total


def folds(ntrain):
    return 2 * ntrain <= 128


def solve_kernel(ntrain, feat, share, low_ref, one_ref, two_ref, out_ref):
    nquery = out_ref.shape[0]
    whole = one_ref[...] + two_ref[...]
    if folds(ntrain):
        half = ntrain // 2
        gram = jnp.concatenate([whole[:half, :ntrain], whole[:half, ntrain:]], axis=0)
        rest = whole[half:]
    else:
        gram = whole[:ntrain, :ntrain]
        rest = whole[ntrain:]
    cross = rest[:, :ntrain]
    square = rest[:, ntrain : ntrain + nquery]

    def rowsum(v):
        return jnp.sum(v, axis=1, keepdims=True)

    def diagonal(v):
        rows = lax.broadcasted_iota(jnp.int32, v.shape, 0)
        cols = lax.broadcasted_iota(jnp.int32, v.shape, 1)
        return jnp.where(rows == cols, v, 0.0)

    norm = rowsum(diagonal(square))
    trace = jnp.sum(diagonal(gram)) / ntrain
    scale = 1.0 / (ntrain * (DAMP * trace / feat))

    res_a, res_x, res_p = jnp.ones_like(norm), jnp.zeros_like(cross), cross
    dir_a, dir_x, dir_p = res_a, res_x, res_p
    solved = jnp.zeros_like(cross)
    now = norm
    for step in range(ITERS):
        square = dir_a * dir_a * norm + dir_a * rowsum(dir_x * cross) + rowsum(dir_x * dir_p)
        alpha = now / (square + rowsum(dir_p * dir_p) * scale)
        solved = solved + alpha * dir_p
        if step == ITERS - 1:
            break
        res_a = res_a - alpha * dir_a
        res_x = res_x - alpha * (dir_x + dir_p * scale)
        res_p = res_a * cross + jnp.dot(
            res_x, gram, precision=HIGHEST, preferred_element_type=F32
        )
        fresh = res_a * res_a * norm + res_a * rowsum(res_x * cross) + rowsum(res_x * res_p)
        beta = fresh / now
        dir_a = res_a + beta * dir_a
        dir_x = res_x + beta * dir_x
        dir_p = res_p + beta * dir_p
        now = fresh
    low = low_ref[0]
    cols = lax.broadcasted_iota(jnp.int32, solved.shape, 1)
    mine = [rowsum(jnp.where(cols == low * share + seq, solved, 0.0)) for seq in range(share)]
    out_ref[...] = jnp.concatenate(mine, axis=1)


def per_device(
    mesh, train_hidden, train_grads, train_ids, query_hidden, query_grads, query_ids, proj_in, proj_out
):
    parts = lax.axis_size("tensor")
    groups = lax.axis_size("dp")
    at = lax.axis_index("tensor").astype(jnp.int32).reshape(1)
    group = lax.axis_index("dp").astype(jnp.int32)
    low = (group & 3).reshape(1)
    steady = at[0] >> 1
    for bit in range((groups - 1).bit_length()):
        steady = steady ^ (group >> bit)
    quarter = ((steady & 1) * 2 + (low >> 1)).reshape(1)
    nseq, seq_len, ff = train_hidden.shape
    width = train_grads.shape[2]
    rank = proj_in.shape[1]
    nquery, qtok, _ = query_hidden.shape
    ntrain = nseq * groups
    share = nseq // parts
    qshare = nquery // parts
    half = rank // 8

    arrays = (
        train_hidden.reshape(nseq * seq_len, ff),
        train_grads.reshape(nseq * seq_len, width),
        query_hidden.reshape(nquery * qtok, ff),
        query_grads.reshape(nquery * qtok, width),
        proj_in.T,
        proj_out.T,
    )
    pieces = {}
    turn = at
    for hops in ((3,), (2, 1, 0)):
        values = project(mesh, turn, arrays, parts, hops)
        turn, *values = lax.optimization_barrier((turn, *values))
        for hop, value in zip(hops, values):
            pieces[hop] = swap(value, 0, hop) if hop else value

    early = pieces[3] + pieces[0]
    rows = share + qshare + 1
    keep, send = call(
        functools.partial(outer_kernel, share, qshare),
        [jax.ShapeDtypeStruct((2, rows, half, 2 * rank), F32)] * 2,
        "outer",
        in_specs=[SMEM_SPEC] * 2 + [VMEM_SPEC] * 5,
        scratch_shapes=[pltpu.VMEM((4, rows, half, 2 * rank), F32)],
    )(at, quarter, train_ids, query_ids, early, pieces[2], pieces[1])

    def ordered(bit, mine, other):
        nex = mine.shape[-3] - qshare - 1
        first = jnp.where(bit == 0, mine, other)[..., :nex, :, :]
        second = jnp.where(bit == 0, other, mine)[..., :nex, :, :]
        return jnp.concatenate([first, second, (mine + other)[..., nex:, :, :]], axis=-3)

    both = ordered(low[0] & 1, keep, swap(send, 1, 0))
    block = ordered(low[0] >> 1, both[0], swap(both[1], 3, 0))
    flip = 4
    while flip < groups:
        block = ordered(0, block, swap(block, flip | 1, 0))
        flip *= 2
    blocks = [block] + [swap(block, hop >> 1, hop) for hop in range(1, parts)]
    size = ntrain + nquery
    shape = (ntrain // 2 + nquery, 2 * ntrain) if folds(ntrain) else (size, size)
    gram = call(
        functools.partial(gram_kernel, qshare),
        jax.ShapeDtypeStruct(shape, F32),
        "gram",
        in_specs=[SMEM_SPEC] + [VMEM_SPEC] * parts,
        scratch_shapes=[pltpu.VMEM((nquery, half, 2 * rank), F32)],
    )(at, *blocks)
    gram = gram + swap(gram, 3, 0)
    return call(
        functools.partial(solve_kernel, ntrain, rank * rank, share),
        jax.ShapeDtypeStruct((nquery, share), F32),
        "solve",
        in_specs=[SMEM_SPEC] + [VMEM_SPEC] * 2,
    )(low, gram, swap(gram, 1, 0))


def solution(mesh):
    return jax.shard_map(
        functools.partial(per_device, mesh),
        mesh=mesh,
        in_specs=(
            P("dp", None, "tensor"),
            P("dp", None, "tensor"),
            P("dp", None),
            P(None, "dp", "tensor"),
            P(None, "dp", "tensor"),
            P(None, "dp"),
            P("tensor", None),
            P("tensor", None),
        ),
        out_specs=P(None, ("dp", "tensor")),
        check_vma=False,
    )
```

time: 619 us -> 47.6 us (0.08)
  waiting for transfers between devices: 534 us -> 23 us
  blocking collectives: 38.8 us -> 0 us
  matrix products: 22.8 us -> 0 us
  between operations: 14.2 us -> 0.12 us
  starting transfers between devices: 0.33 us -> 14.1 us
  Pallas kernels: 0 us -> 9.52 us
  other arithmetic: 7.8 us -> 0.08 us
    psum x4 -> x0, waiting for transfers between devices: 465 us -> none  [the longest x3 377 us: per_device(): lax.psum(term, ('dp', 'tensor')) / (total_train * damping)]
    reduce_scatter x4 -> x0, waiting for transfers between devices: 68.4 us -> none  [the longest x1 20.1 us: per_device(): lax.psum_scatter(train_out, 'tensor', scatter_dimension=0, tiled=True)]
    psum x1 -> x0, blocking collectives: 38.8 us -> none  [per_device(): lax.psum((partial_value, counts, jnp.sum(examples * examples)), ('dp', 't...]
    ppermute x0 -> x11, waiting for transfers between devices: none -> 23 us  [swap(): lax.ppermute(value, ('dp', 'tensor'), [(i, i ^ flip) for i in range(group...]
    dot_general x13 -> x0, matrix products: 22.8 us -> none  [the longest x1 6.09 us: per_device(): jnp.dot(train_hidden.reshape(-1, ff_part), proj_in, preferred_element_typ...]
    ppermute x0 -> x11, starting transfers between devices: none -> 14.1 us  [swap(): lax.ppermute(value, ('dp', 'tensor'), [(i, i ^ flip) for i in range(group...]
    pallas_call x0 -> x5, Pallas kernels: none -> 9.52 us  [the longest x2 7.53 us: project(): call(functools.partial(project_kernel, mesh, parts, hops, tile), [jax.Sha...]
    reduce_sum x7 -> x0, other arithmetic: 6.82 us -> none  [the longest x3 3.46 us: per_device(): alpha = norm_now / jnp.sum(direction * image, axis=1)]
  transfers between devices with their start and end apart: 8 -> 11, of which waited for: 8 -> 9; matrix products, arithmetic and copies ran while one was open for 2% -> 0% of each run, Pallas kernels for 0% -> 10%
where the time goes in v1:
time: 47.6 us; the launch traced here: 47.5 us
  waiting for transfers between devices  23 us (48%)
  starting transfers between devices  14.1 us (30%)
  Pallas kernels  9.52 us (20%)
  local copies, waits for them, and re-layouts  0.67 us (1%)
    ppermute x11, waiting for transfers between devices, swap(): lax.ppermute(value, ('dp', 'tensor'), [(i, i ^ flip) for i in range(group...  23 us
    ppermute x11, starting transfers between devices, swap(): lax.ppermute(value, ('dp', 'tensor'), [(i, i ^ flip) for i in range(group...  14.1 us
    pallas_call x2, Pallas kernels, project(): call(functools.partial(project_kernel, mesh, parts, hops, tile), [jax.Sha...  7.53 us
    pallas_call x1, Pallas kernels, per_device(): call(functools.partial(solve_kernel, ntrain, rank * rank, share), jax.Sha...  0.98 us
  transfers between devices with their start and end apart: 11, of which 9 were waited for; matrix products, arithmetic and copies ran while one was open for 0% of the time, Pallas kernels for 10%

profile of v1, /device:TPU:0, one launch (start us, length us, event | category | flops | bytes accessed | tf_op | source)
XLA Modules:
  0.0 47.5 jit_solution(3694695834379048506)
XLA Ops:
  0.0 2.6 %project_3.1 = f32[320,128]{1,0:T(8,128)S(1)} custom-call(s32[1]{0:T(128)} %bitcast.1.at_ref, bf16[1024,3584]{1,0:T(8,128)(2,1)} %bitcast.13, bf16[1024,1024]{1,0:T(8,128)(2,1)} %bitcast.15, bf16[256,3584]{1,0:T(8,128)(2,1)} %bitcast.17, bf16[256,1024]{1,0:T(8,128)(2,1)} %bitcast.19, bf16[64,3584]{1,0:T(8,128)(2,1)} %bitcast.21, bf16[64,1024]{1,0:T(8,128)(2,1)} %bitcast.23), custom_call_target="tpu_custom_call" | custom-call | flops 188743680 | bytes 3538944 | tf_op jit(solution)/shard_map/project_3/pallas_call | solution.py:106
  2.6 0.0 copy-start
  2.6 0.0 copy-start.1
  2.7 5.1 %collective-permute-start = (f32[320,128]{1,0:T(8,128)S(1)}, f32[320,128]{1,0:T(8,128)S(1)}, u32[]{:S(2)}, u32[]{:S(2)}) collective-permute-start(f32[320,128]{1,0:T(8,128)S(1)} %project_3.1), channel_id=1, source_target_pairs={{0,3},{1,2},{2,1},{3,0},{4,7},{5,6},{6,5},{7,4},{8,11},{9,10},{10,... | collective-permute-start | bytes 491528 | tf_op jit(solution)/shard_map/ppermute | solution.py:35
  7.8 4.9 %project_2_1_0.1 = (f32[320,128]{1,0:T(8,128)S(1)}, f32[320,128]{1,0:T(8,128)S(1)}, f32[320,128]{1,0:T(8,128)S(1)}) custom-call(s32[1]{0:T(128)} %bitcast.1.at_ref, bf16[1024,3584]{1,0:T(8,128)(2,1)} %bitcast.14, bf16[1024,1024]{1,0:T(8,128)(2,1)} %bitcast.16, bf16[256,3584]{1,0:T(8,128)(2,1)} %bitcast.18, bf16[256,1024]{1,0:T(8,128)(2,1)} %bitcast.20, ...), custom_call_target="tpu_custom_call" | custom-call | flops 566231040 | bytes 9437184 | tf_op jit(solution)/shard_map/project_2_1_0/pallas_call | solution.py:106
  12.7 0.1 collective-permute-start.1
  12.8 0.6 %collective-permute-start.2 = (f32[320,128]{1,0:T(8,128)S(1)}, f32[320,128]{1,0:T(8,128)S(1)}, u32[]{:S(2)}, u32[]{:S(2)}) collective-permute-start(f32[320,128]{1,0:T(8,128)S(1)} %get-tuple-element.22), channel_id=1, source_target_pairs={{0,1},{1,0},{2,3},{3,2},{4,5},{5,4},{6,7},{7,6},{8,9},{9,8},{10,11... | collective-permute-start | bytes 491528 | tf_op jit(solution)/shard_map/ppermute | solution.py:35
  13.3 0.0 collective-permute-done
  13.3 8.6 %collective-permute-done.1.refs_1_ = f32[320,128]{1,0:T(8,128)S(1)} collective-permute-done((f32[320,128]{1,0:T(8,128)S(1)}, f32[320,128]{1,0:T(8,128)S(1)}, u32[]{:S(2)}, u32[]{:S(2)}) %collective-permute-start.1) | collective-permute-done | bytes 163872 | tf_op jit(solution)/shard_map/ppermute | solution.py:35
  21.9 0.1 collective-permute-done.2.refs_2_
  22.0 0.0 copy-done
  22.0 0.0 copy-done.1
  22.0 0.6 %outer.1 = (f32[2,7,8,128]{3,2,1,0:T(8,128)S(1)}, f32[2,7,8,128]{3,2,1,0:T(8,128)S(1)}) custom-call(s32[1]{0:T(128)} %bitcast.1.at_ref, s32[1]{0:T(128)S(6)} %add.22.quarter_ref, s32[8,128]{1,0:T(8,128)S(1)} %copy-done.1, s32[16,16]{1,0:T(8,128)S(1)} %copy-done, f32[320,128]{1,0:T(8,128)S(1)} %add.23.refs_0_, f32[320,128]{1,0:T(8,128)S(1)} %collective-permute-done.1.refs_1_, ...), custom_call_target="tpu_custom_call" | custom-call | tf_op jit(solution)/shard_map/outer/pallas_call | solution.py:299
  22.5 0.1 collective-permute-start.3
  22.6 1.2 %collective-permute-done.3 = f32[2,7,8,128]{3,2,1,0:T(8,128)S(1)} collective-permute-done((f32[2,7,8,128]{3,2,1,0:T(8,128)S(1)}, f32[2,7,8,128]{3,2,1,0:T(8,128)S(1)}, u32[]{:S(2)}, u32[]{:S(2)}) %collective-permute-start.3) | collective-permute-done | bytes 57376 | tf_op jit(solution)/shard_map/ppermute | solution.py:35
  23.9 1.3 %collective-permute-start.4 = (f32[9,8,128]{2,1,0:T(8,128)S(1)}, f32[9,8,128]{2,1,0:T(8,128)S(1)}, u32[]{:S(2)}, u32[]{:S(2)}) collective-permute-start(f32[9,8,128]{2,1,0:T(8,128)S(1)} %get-tuple-element.30), channel_id=1, source_target_pairs={{0,12},{1,13},{2,14},{3,15},{4,8},{5,9},{6,10},{7,11},{8,4},{9,5},... | collective-permute-start | bytes 110600 | tf_op jit(solution)/shard_map/ppermute | solution.py:35
  25.3 2.2 %collective-permute-done.4 = f32[9,8,128]{2,1,0:T(8,128)S(1)} collective-permute-done((f32[9,8,128]{2,1,0:T(8,128)S(1)}, f32[9,8,128]{2,1,0:T(8,128)S(1)}, u32[]{:S(2)}, u32[]{:S(2)}) %collective-permute-start.4) | collective-permute-done | bytes 36896 | tf_op jit(solution)/shard_map/ppermute | solution.py:35
  27.4 1.4 %collective-permute-start.5 = (f32[13,8,128]{2,1,0:T(8,128)S(1)}, f32[13,8,128]{2,1,0:T(8,128)S(1)}, u32[]{:S(2)}, u32[]{:S(2)}) collective-permute-start(f32[13,8,128]{2,1,0:T(8,128)S(1)} %pad_maximum_fusion.2), channel_id=1, source_target_pairs={{0,20},{1,21},{2,22},{3,23},{4,16},{5,17},{6,18},{7,19},{8,28},{9,... | collective-permute-start | bytes 159752 | tf_op jit(solution)/shard_map/ppermute | solution.py:35
  28.8 2.5 %collective-permute-done.5 = f32[13,8,128]{2,1,0:T(8,128)S(1)} collective-permute-done((f32[13,8,128]{2,1,0:T(8,128)S(1)}, f32[13,8,128]{2,1,0:T(8,128)S(1)}, u32[]{:S(2)}, u32[]{:S(2)}) %collective-permute-start.5) | collective-permute-done | bytes 53280 | tf_op jit(solution)/shard_map/ppermute | solution.py:35
  31.3 0.3 collective-permute-start.6
  31.6 2.0 %collective-permute-start.7 = (f32[21,8,128]{2,1,0:T(8,128)S(1)}, f32[21,8,128]{2,1,0:T(8,128)S(1)}, u32[]{:S(2)}, u32[]{:S(2)}) collective-permute-start(f32[21,8,128]{2,1,0:T(8,128)S(1)} %pad_maximum_fusion.refs_0_), channel_id=1, source_target_pairs={{0,6},{1,7},{2,4},{3,5},{4,2},{5,3},{6,0},{7,1},{8,14},{9,15},{10,... | collective-permute-start | bytes 258056 | tf_op jit(solution)/shard_map/ppermute | solution.py:35
  33.6 1.9 %collective-permute-start.8 = (f32[21,8,128]{2,1,0:T(8,128)S(1)}, f32[21,8,128]{2,1,0:T(8,128)S(1)}, u32[]{:S(2)}, u32[]{:S(2)}) collective-permute-start(f32[21,8,128]{2,1,0:T(8,128)S(1)} %pad_maximum_fusion.refs_0_), channel_id=1, source_target_pairs={{0,7},{1,6},{2,5},{3,4},{4,3},{5,2},{6,1},{7,0},{8,15},{9,14},{10,... | collective-permute-start | bytes 258056 | tf_op jit(solution)/shard_map/ppermute | solution.py:35
  35.5 1.8 %collective-permute-done.6.refs_1_ = f32[21,8,128]{2,1,0:T(8,128)S(1)} collective-permute-done((f32[21,8,128]{2,1,0:T(8,128)S(1)}, f32[21,8,128]{2,1,0:T(8,128)S(1)}, u32[]{:S(2)}, u32[]{:S(2)}) %collective-permute-start.6) | collective-permute-done | bytes 86048 | tf_op jit(solution)/shard_map/ppermute | solution.py:35
  37.2 3.7 %collective-permute-done.7.refs_2_ = f32[21,8,128]{2,1,0:T(8,128)S(1)} collective-permute-done((f32[21,8,128]{2,1,0:T(8,128)S(1)}, f32[21,8,128]{2,1,0:T(8,128)S(1)}, u32[]{:S(2)}, u32[]{:S(2)}) %collective-permute-start.7) | collective-permute-done | bytes 86048 | tf_op jit(solution)/shard_map/ppermute | solution.py:35
  40.9 0.0 collective-permute-done.8.refs_3_
  40.9 0.5 gram.1
  41.4 1.3 %collective-permute-start.9 = (f32[48,128]{1,0:T(8,128)S(1)}, f32[48,128]{1,0:T(8,128)S(1)}, u32[]{:S(2)}, u32[]{:S(2)}) collective-permute-start(f32[48,128]{1,0:T(8,128)S(1)} %gram.1), channel_id=1, source_target_pairs={{0,12},{1,13},{2,14},{3,15},{4,8},{5,9},{6,10},{7,11},{8,4},{9,5},... | collective-permute-start | bytes 73736 | tf_op jit(solution)/shard_map/ppermute | solution.py:35
  42.7 2.0 %collective-permute-done.9 = f32[48,128]{1,0:T(8,128)S(1)} collective-permute-done((f32[48,128]{1,0:T(8,128)S(1)}, f32[48,128]{1,0:T(8,128)S(1)}, u32[]{:S(2)}, u32[]{:S(2)}) %collective-permute-start.9) | collective-permute-done | bytes 24608 | tf_op jit(solution)/shard_map/ppermute | solution.py:35
  44.7 0.2 collective-permute-start.10
  44.8 1.0 %collective-permute-done.10.two_ref = f32[48,128]{1,0:T(8,128)S(1)} collective-permute-done((f32[48,128]{1,0:T(8,128)S(1)}, f32[48,128]{1,0:T(8,128)S(1)}, u32[]{:S(2)}, u32[]{:S(2)}) %collective-permute-start.10) | collective-permute-done | bytes 24608 | tf_op jit(solution)/shard_map/ppermute | solution.py:35
  45.9 1.0 %solve.1 = f32[16,2]{1,0:T(8,128)S(1)} custom-call(s32[1]{0:T(128)} %bitcast.low_ref, f32[48,128]{1,0:T(8,128)S(1)} %add.27.one_ref, f32[48,128]{1,0:T(8,128)S(1)} %collective-permute-done.10.two_ref), custom_call_target="tpu_custom_call" | custom-call | tf_op jit(solution)/shard_map/solve/pallas_call | solution.py:330
  46.8 0.7 %copy.9 = f32[16,2]{0,1:T(2,128)} copy(f32[16,2]{1,0:T(8,128)S(1)} %solve.1) | data formatting | bytes 256 | tf_op jit(solution)/shard_map/solve/pallas_call | solution.py:330
  (12 shorter events, 0.1 us)
Async XLA Ops:
  2.6 19.4 %copy-start = (s32[16,16]{1,0:T(8,128)S(1)}, s32[16,16]{1,0:T(8,128)}, u32[]{:S(2)}) copy-start(s32[16,16]{1,0:T(8,128)} %qids_ref.1) | copy-start | bytes 3076
  2.6 19.3 %copy-start.1 = (s32[8,128]{1,0:T(8,128)S(1)}, s32[8,128]{1,0:T(8,128)}, u32[]{:S(2)}) copy-start(s32[8,128]{1,0:T(8,128)} %ids_ref.1) | copy-start | bytes 12292
  2.7 10.7 %collective-permute-start = (f32[320,128]{1,0:T(8,128)S(1)}, f32[320,128]{1,0:T(8,128)S(1)}, u32[]{:S(2)}, u32[]{:S(2)}) collective-permute-start(f32[320,128]{1,0:T(8,128)S(1)} %project_3.1), channel_id=1, source_target_pairs={{0,3},{1,2},{2,1},{3,0},{4,7},{5,6},{6,5},{7,4},{8,11},{9,10},{10,... | collective-permute-start | bytes 491528 | tf_op jit(solution)/shard_map/ppermute | solution.py:35
  12.7 9.2 %collective-permute-start.1 = (f32[320,128]{1,0:T(8,128)S(1)}, f32[320,128]{1,0:T(8,128)S(1)}, u32[]{:S(2)}, u32[]{:S(2)}) collective-permute-start(f32[320,128]{1,0:T(8,128)S(1)} %get-tuple-element.21), channel_id=1, source_target_pairs={{0,2},{1,3},{2,0},{3,1},{4,6},{5,7},{6,4},{7,5},{8,10},{9,11},{10,... | collective-permute-start | bytes 491528 | tf_op jit(solution)/shard_map/ppermute | solution.py:35
  12.8 9.2 %collective-permute-start.2 = (f32[320,128]{1,0:T(8,128)S(1)}, f32[320,128]{1,0:T(8,128)S(1)}, u32[]{:S(2)}, u32[]{:S(2)}) collective-permute-start(f32[320,128]{1,0:T(8,128)S(1)} %get-tuple-element.22), channel_id=1, source_target_pairs={{0,1},{1,0},{2,3},{3,2},{4,5},{5,4},{6,7},{7,6},{8,9},{9,8},{10,11... | collective-permute-start | bytes 491528 | tf_op jit(solution)/shard_map/ppermute | solution.py:35
  22.5 1.3 %collective-permute-start.3 = (f32[2,7,8,128]{3,2,1,0:T(8,128)S(1)}, f32[2,7,8,128]{3,2,1,0:T(8,128)S(1)}, u32[]{:S(2)}, u32[]{:S(2)}) collective-permute-start(f32[2,7,8,128]{3,2,1,0:T(8,128)S(1)} %get-tuple-element.24), channel_id=1, source_target_pairs={{0,4},{1,5},{2,6},{3,7},{4,0},{5,1},{6,2},{7,3},{8,12},{9,13},{10,... | collective-permute-start | bytes 172040 | tf_op jit(solution)/shard_map/ppermute | solution.py:35
  23.9 3.5 %collective-permute-start.4 = (f32[9,8,128]{2,1,0:T(8,128)S(1)}, f32[9,8,128]{2,1,0:T(8,128)S(1)}, u32[]{:S(2)}, u32[]{:S(2)}) collective-permute-start(f32[9,8,128]{2,1,0:T(8,128)S(1)} %get-tuple-element.30), channel_id=1, source_target_pairs={{0,12},{1,13},{2,14},{3,15},{4,8},{5,9},{6,10},{7,11},{8,4},{9,5},... | collective-permute-start | bytes 110600 | tf_op jit(solution)/shard_map/ppermute | solution.py:35
  27.4 3.9 %collective-permute-start.5 = (f32[13,8,128]{2,1,0:T(8,128)S(1)}, f32[13,8,128]{2,1,0:T(8,128)S(1)}, u32[]{:S(2)}, u32[]{:S(2)}) collective-permute-start(f32[13,8,128]{2,1,0:T(8,128)S(1)} %pad_maximum_fusion.2), channel_id=1, source_target_pairs={{0,20},{1,21},{2,22},{3,23},{4,16},{5,17},{6,18},{7,19},{8,28},{9,... | collective-permute-start | bytes 159752 | tf_op jit(solution)/shard_map/ppermute | solution.py:35
  31.3 5.9 %collective-permute-start.6 = (f32[21,8,128]{2,1,0:T(8,128)S(1)}, f32[21,8,128]{2,1,0:T(8,128)S(1)}, u32[]{:S(2)}, u32[]{:S(2)}) collective-permute-start(f32[21,8,128]{2,1,0:T(8,128)S(1)} %pad_maximum_fusion.refs_0_), channel_id=1, source_target_pairs={{0,1},{1,0},{2,3},{3,2},{4,5},{5,4},{6,7},{7,6},{8,9},{9,8},{10,11... | collective-permute-start | bytes 258056 | tf_op jit(solution)/shard_map/ppermute | solution.py:35
  31.6 9.3 %collective-permute-start.7 = (f32[21,8,128]{2,1,0:T(8,128)S(1)}, f32[21,8,128]{2,1,0:T(8,128)S(1)}, u32[]{:S(2)}, u32[]{:S(2)}) collective-permute-start(f32[21,8,128]{2,1,0:T(8,128)S(1)} %pad_maximum_fusion.refs_0_), channel_id=1, source_target_pairs={{0,6},{1,7},{2,4},{3,5},{4,2},{5,3},{6,0},{7,1},{8,14},{9,15},{10,... | collective-permute-start | bytes 258056 | tf_op jit(solution)/shard_map/ppermute | solution.py:35
  33.6 7.3 %collective-permute-start.8 = (f32[21,8,128]{2,1,0:T(8,128)S(1)}, f32[21,8,128]{2,1,0:T(8,128)S(1)}, u32[]{:S(2)}, u32[]{:S(2)}) collective-permute-start(f32[21,8,128]{2,1,0:T(8,128)S(1)} %pad_maximum_fusion.refs_0_), channel_id=1, source_target_pairs={{0,7},{1,6},{2,5},{3,4},{4,3},{5,2},{6,1},{7,0},{8,15},{9,14},{10,... | collective-permute-start | bytes 258056 | tf_op jit(solution)/shard_map/ppermute | solution.py:35
  41.4 3.3 %collective-permute-start.9 = (f32[48,128]{1,0:T(8,128)S(1)}, f32[48,128]{1,0:T(8,128)S(1)}, u32[]{:S(2)}, u32[]{:S(2)}) collective-permute-start(f32[48,128]{1,0:T(8,128)S(1)} %gram.1), channel_id=1, source_target_pairs={{0,12},{1,13},{2,14},{3,15},{4,8},{5,9},{6,10},{7,11},{8,4},{9,5},... | collective-permute-start | bytes 73736 | tf_op jit(solution)/shard_map/ppermute | solution.py:35
  44.7 1.2 %collective-permute-start.10 = (f32[48,128]{1,0:T(8,128)S(1)}, f32[48,128]{1,0:T(8,128)S(1)}, u32[]{:S(2)}, u32[]{:S(2)}) collective-permute-start(f32[48,128]{1,0:T(8,128)S(1)} %add.27.one_ref), channel_id=1, source_target_pairs={{0,4},{1,5},{2,6},{3,7},{4,0},{5,1},{6,2},{7,3},{8,12},{9,13},{10,... | collective-permute-start | bytes 73736 | tf_op jit(solution)/shard_map/ppermute | solution.py:35

commit v2 on v1

--- a/solution.py
+++ b/solution.py
@@ -45,34 +45,34 @@
     rank = pin_ref.shape[0]
     sides = ((th_ref, qh_ref, hid, pin_ref, pin), (tg_ref, qg_ref, grad, pout_ref, pout))
     chunks = []
-    for side, (_, _, buf, _, _) in enumerate(sides):
-        start = 0
-        while start < buf.shape[1]:
-            size = min(2 * tile if not chunks else 4 * tile, buf.shape[1] - start)
-            chunks.append((side, start, size))
-            start += size
-    copies = []
-    for chunk, (side, start, size) in enumerate(chunks):
-        train, query, buf, weight, held = sides[side]
-        cols = pl.ds(start, size)
-        pairs = [(weight.at[:, cols], held.at[:, cols])]
-        for slot, hop in enumerate(hops):
-            to = at ^ hop
-            tsrc = pl.ds(pl.multiple_of(to * trows, trows), trows)
-            qsrc = pl.ds(pl.multiple_of(to * qrows, qrows), qrows)
-            pairs.append((train.at[tsrc, cols], buf.at[pl.ds(slot * rows, trows), cols]))
-            pairs.append((query.at[qsrc, cols], buf.at[pl.ds(slot * rows + trows, qrows), cols]))
-        copies.append(
-            [pltpu.make_async_copy(src, dst, sems.at[chunk, k]) for k, (src, dst) in enumerate(pairs)]
-        )
-        for copy in copies[-1]:
-            copy.start()
+    started = 0
+    for side, (train, query, buf, weight, held) in enumerate(sides):
+        first = 4 * tile if side == 0 else buf.shape[1]
+        for start, size in ((0, first), (first, buf.shape[1] - first)):
+            if not size:
+                continue
+            cols = pl.ds(start, size)
+            pairs = [] if start else [(weight, held)]
+            for slot, hop in enumerate(hops):
+                to = at ^ hop
+                tsrc = pl.ds(pl.multiple_of(to * trows, trows), trows)
+                pairs.append((train.at[tsrc, cols], buf.at[pl.ds(slot * rows, trows), cols]))
+            for slot, hop in enumerate(() if start else hops):
+                to = at ^ hop
+                qsrc = pl.ds(pl.multiple_of(to * qrows, qrows), qrows)
+                pairs.append((query.at[qsrc, :], buf.at[pl.ds(slot * rows + trows, qrows), :]))
+            copies = []
+            for src, dst in pairs:
+                copies.append(pltpu.make_async_copy(src, dst, sems.at[started]))
+                copies[-1].start()
+                started += 1
+            chunks.append((side, start, size, copies))
 
     def multiply(*sums):
         count = 0
-        for (side, start, size), waits in zip(chunks, copies):
+        for side, start, size, copies in chunks:
             _, _, buf, _, held = sides[side]
-            for copy in waits:
+            for copy in copies:
                 copy.wait()
             for col in range(start, start + size, tile):
                 unit, turn = count % len(sums), count // len(sums)
@@ -114,7 +114,7 @@
             pltpu.VMEM((held, width), bf16),
             pltpu.VMEM((rank, ff), bf16),
             pltpu.VMEM((rank, width), bf16),
-            pltpu.SemaphoreType.DMA((8, 1 + 2 * len(hops))),
+            pltpu.SemaphoreType.DMA((2 + 5 * len(hops),)),
         ],
         cost_estimate=pl.CostEstimate(
             flops=2 * held * (ff + width) * rank,
@@ -124,8 +124,9 @@
     )(at, *[pltpu.with_memory_space_constraint(array, pltpu.HBM) for array in arrays])
 
 
-def fold(outer, start, half):
-    return jnp.concatenate([outer[start : start + half], outer[start + half : start + 2 * half]], axis=1)
+def halves(value):
+    high = value.astype(jnp.bfloat16)
+    return high, (value - high.astype(F32)).astype(jnp.bfloat16)
 
 
 def outer_kernel(share, qshare, at_ref, quarter_ref, ids_ref, qids_ref, *refs):
@@ -136,62 +137,87 @@
     qtok = qids_ref.shape[1]
     half = rank // 8
 
-    def product(tokens, left):
-        return jnp.dot(left, tokens[:, rank:], precision=HIGHEST, preferred_element_type=F32)
-
     def total(start, rows):
         value = tok_refs[0][start : start + rows, :]
         for ref in tok_refs[1:]:
             value = value + ref[start : start + rows, :]
         return value
 
+    def product(lefts, tokens):
+        left = jnp.concatenate([part for value in lefts for part in halves(value)], axis=0)
+        right = jnp.concatenate(halves(tokens), axis=1)
+        out = jnp.dot(left, right, preferred_element_type=F32)
+        out = out[:, : 2 * rank] + out[:, 2 * rank :]
+        sums = []
+        for index in range(len(lefts)):
+            start = 2 * rank * index
+            sums.append(out[start : start + rank] + out[start + rank : start + 2 * rank])
+        return sums
+
     def store(slot, outer):
         for quarter in range(4):
-            scratch[quarter, slot] = fold(outer, quarter * 2 * half, half)
+            start = quarter * 2 * half
+            scratch[quarter, slot] = jnp.concatenate(
+                [outer[start : start + half, rank:], outer[start + half : start + 2 * half, rank:]],
+                axis=1,
+            )
 
     for seq in range(share):
         tokens = total(seq * seq_len, seq_len)
         mask = (ids_ref[pl.ds(at * share + seq, 1), :] != PAD_ID).astype(F32)
-        outer = product(tokens, tokens.T[:rank] * mask)
+        (outer,) = product([tokens.T[:rank] * mask], tokens)
         store(seq, outer / jnp.sum(mask, axis=1, keepdims=True))
+
     for quarter in range(4):
         scratch[quarter, share + qshare] = jnp.ones((half, 2 * rank), F32)
+    tokens = total(share * seq_len, qshare * qtok)
+    left = tokens.T[:rank]
+    owner = lax.broadcasted_iota(jnp.int32, (1, qshare * qtok), 1) // qtok
+    lefts = []
     for query in range(qshare):
-        tokens = total(share * seq_len + query * qtok, qtok)
         mask = (qids_ref[pl.ds(at * qshare + query, 1), :] != PAD_ID).astype(F32)
-        store(share + query, product(tokens, tokens.T[:rank] * mask))
+        lefts.append(left * jnp.where(owner == query, jnp.concatenate([mask] * qshare, axis=1), 0.0))
         count = jnp.broadcast_to(jnp.sum(mask, axis=1, keepdims=True), (1, 2 * rank))
         for quarter in range(4):
             scratch[quarter, share + qshare, query : query + 1, :] = count
+    for query, outer in enumerate(product(lefts, tokens)):
+        store(share + query, outer)
     for flip in range(2):
         keep_ref[flip] = scratch[mine ^ flip]
         send_ref[flip] = scratch[mine ^ 2 ^ flip]
 
 
-def gram_kernel(qshare, at_ref, *refs):
+def gram_kernel(qshare, hops, at_ref, *refs):
     piece_refs, (out_ref, scratch) = refs[:-2], refs[-2:]
     at = at_ref[0]
-    rows, half, lanes = piece_refs[0].shape
-    nex = rows - qshare - 1
-    ntrain = nex * len(piece_refs)
+    _, half, lanes = piece_refs[0].shape
     nquery = scratch.shape[0]
-    for hop, ref in enumerate(piece_refs):
-        counts = ref[nex + qshare]
-        for query in range(qshare):
-            scratch[(at ^ hop) * qshare + query] = ref[nex + query] / counts[query : query + 1, :]
-    total = None
-    for row in range(half):
-        both = jnp.concatenate(
-            [ref[:nex, row, :] for ref in piece_refs] + [scratch[:, row, :]], axis=0
-        )
-        high = both.astype(jnp.bfloat16)
-        low = (both - high.astype(F32)).astype(jnp.bfloat16)
-        left = jnp.concatenate([high, low], axis=0)
-        product = lax.dot_general(left, high, NT, preferred_element_type=F32)
-        product = product + lax.dot_general(left, low, NT, preferred_element_type=F32)
-        total = product if total is None else total + product
+    examples = []
+    for hop, pieces in hops:
+        for piece in pieces[:-1]:
+            examples.append((piece_refs[piece], piece_refs[piece].shape[0]))
+        last = piece_refs[pieces[-1]]
+        nex = last.shape[0] - qshare
+        examples.append((last, nex))
+        scratch[pl.ds((at ^ hop) * qshare, qshare)] = last[nex:]
+    ntrain = sum(nex for _, nex in examples)
+    both = jnp.concatenate(
+        [
+            jnp.concatenate(
+                [ref[:nex, row, :] for ref, nex in examples] + [scratch[:, row, :]], axis=0
+            )
+            for row in range(half)
+        ],
+        axis=1,
+    )
     size = ntrain + nquery
+    high, low = halves(both)
+    gap = jnp.zeros((-size % 128, half * lanes), high.dtype)
+    left = jnp.concatenate([high, low], axis=0)
+    right = jnp.concatenate([high, gap, low], axis=0)
+    total = lax.dot_general(left, right, NT, preferred_element_type=F32)
     total = total[:size] + total[size:]
+    total = total[:, :size] + total[:, size + gap.shape[0] :]
     if folds(ntrain):
         half = ntrain // 2
         out_ref[:half, :] = jnp.concatenate([total[:half, :ntrain], total[half:ntrain, :ntrain]], axis=1)
@@ -205,8 +231,8 @@
     return 2 * ntrain <= 128
 
 
-def solve_kernel(ntrain, feat, share, low_ref, one_ref, two_ref, out_ref):
-    nquery = out_ref.shape[0]
+def solve_kernel(ntrain, feat, share, low_ref, one_ref, two_ref, out_ref, columns):
+    nquery = out_ref.shape[1]
     whole = one_ref[...] + two_ref[...]
     if folds(ntrain):
         half = ntrain // 2
@@ -230,31 +256,41 @@
     trace = jnp.sum(diagonal(gram)) / ntrain
     scale = 1.0 / (ntrain * (DAMP * trace / feat))
 
+    def thirds(value):
+        high, rest = halves(value)
+        low = value - high.astype(F32) - rest.astype(F32)
+        return high, rest, low.astype(jnp.bfloat16)
+
+    gram_parts = thirds(gram)
+
+    def times_gram(value):
+        left = jnp.concatenate(thirds(value), axis=0)
+        out = sum(jnp.dot(left, part, preferred_element_type=F32) for part in gram_parts[::-1])
+        return out[2 * nquery :] + out[nquery : 2 * nquery] + out[:nquery]
+
     res_a, res_x, res_p = jnp.ones_like(norm), jnp.zeros_like(cross), cross
     dir_a, dir_x, dir_p = res_a, res_x, res_p
     solved = jnp.zeros_like(cross)
     now = norm
     for step in range(ITERS):
-        square = dir_a * dir_a * norm + dir_a * rowsum(dir_x * cross) + rowsum(dir_x * dir_p)
-        alpha = now / (square + rowsum(dir_p * dir_p) * scale)
+        inner = dir_p * dir_p * scale
+        if step:
+            inner = inner + dir_x * (dir_a * cross + dir_p)
+        alpha = now / (dir_a * dir_a * norm + rowsum(inner))
         solved = solved + alpha * dir_p
         if step == ITERS - 1:
             break
         res_a = res_a - alpha * dir_a
         res_x = res_x - alpha * (dir_x + dir_p * scale)
-        res_p = res_a * cross + jnp.dot(
-            res_x, gram, precision=HIGHEST, preferred_element_type=F32
-        )
-        fresh = res_a * res_a * norm + res_a * rowsum(res_x * cross) + rowsum(res_x * res_p)
+        res_p = res_a * cross + times_gram(res_x)
+        fresh = res_a * res_a * norm + rowsum(res_x * (res_a * cross + res_p))
         beta = fresh / now
         dir_a = res_a + beta * dir_a
         dir_x = res_x + beta * dir_x
         dir_p = res_p + beta * dir_p
         now = fresh
-    low = low_ref[0]
-    cols = lax.broadcasted_iota(jnp.int32, solved.shape, 1)
-    mine = [rowsum(jnp.where(cols == low * share + seq, solved, 0.0)) for seq in range(share)]
-    out_ref[...] = jnp.concatenate(mine, axis=1)
+    columns[...] = solved.T
+    out_ref[...] = columns[pl.ds(low_ref[0] * share, share), :]
 
 
 def per_device(
@@ -265,8 +301,8 @@
     at = lax.axis_index("tensor").astype(jnp.int32).reshape(1)
     group = lax.axis_index("dp").astype(jnp.int32)
     low = (group & 3).reshape(1)
-    steady = at[0] >> 1
-    for bit in range((groups - 1).bit_length()):
+    steady = group
+    for bit in range(1, (groups - 1).bit_length()):
         steady = steady ^ (group >> bit)
     quarter = ((steady & 1) * 2 + (low >> 1)).reshape(1)
     nseq, seq_len, ff = train_hidden.shape
@@ -288,7 +324,7 @@
     )
     pieces = {}
     turn = at
-    for hops in ((3,), (2, 1, 0)):
+    for hops in ((3,), (2, 1), (0,)):
         values = project(mesh, turn, arrays, parts, hops)
         turn, *values = lax.optimization_barrier((turn, *values))
         for hop, value in zip(hops, values):
@@ -313,26 +349,38 @@
     both = ordered(low[0] & 1, keep, swap(send, 1, 0))
     block = ordered(low[0] >> 1, both[0], swap(both[1], 3, 0))
     flip = 4
-    while flip < groups:
+    while 2 * flip < groups:
         block = ordered(0, block, swap(block, flip | 1, 0))
         flip *= 2
-    blocks = [block] + [swap(block, hop >> 1, hop) for hop in range(1, parts)]
+    nex = block.shape[0] - qshare - 1
+    own = block[:nex]
+    other = swap(block, flip | 1, 0)
+    early = swap(own, 0, 3)
+    rest = (block + other)[nex:]
+    after = jnp.concatenate([other[:nex], rest[:qshare] / rest[qshare, :qshare, None, :]], axis=0)
+    whole = jnp.concatenate([own, after], axis=0)
+    far = swap(whole, 0, 2)
+    late = swap(lax.optimization_barrier((after, early))[0], 0, 3)
+    near = swap(whole, 0, 1)
+    blocks = [whole, early, late, far, near]
+    hops = ((0, (0,)), (3, (1, 2)), (2, (3,)), (1, (4,)))
     size = ntrain + nquery
     shape = (ntrain // 2 + nquery, 2 * ntrain) if folds(ntrain) else (size, size)
     gram = call(
-        functools.partial(gram_kernel, qshare),
+        functools.partial(gram_kernel, qshare, hops),
         jax.ShapeDtypeStruct(shape, F32),
         "gram",
-        in_specs=[SMEM_SPEC] + [VMEM_SPEC] * parts,
+        in_specs=[SMEM_SPEC] + [VMEM_SPEC] * len(blocks),
         scratch_shapes=[pltpu.VMEM((nquery, half, 2 * rank), F32)],
     )(at, *blocks)
     gram = gram + swap(gram, 3, 0)
     return call(
         functools.partial(solve_kernel, ntrain, rank * rank, share),
-        jax.ShapeDtypeStruct((nquery, share), F32),
+        jax.ShapeDtypeStruct((share, nquery), F32),
         "solve",
         in_specs=[SMEM_SPEC] + [VMEM_SPEC] * 2,
-    )(low, gram, swap(gram, 1, 0))
+        scratch_shapes=[pltpu.VMEM((ntrain, nquery), F32)],
+    )(low, gram, swap(gram, 1, 0)).T
 
 
 def solution(mesh):

time: 47.6 us -> 47 us (0.987)
  waiting for transfers between devices: 23 us -> 17.7 us
  starting transfers between devices: 14.1 us -> 17 us
  Pallas kernels: 9.52 us -> 11.9 us
  local copies, waits for them, and re-layouts: 0.67 us -> 0.02 us
    ppermute x11 -> x12, waiting for transfers between devices: 23 us -> 17.7 us  [swap(): lax.ppermute(value, ('dp', 'tensor'), [(i, i ^ flip) for i in range(group...]
    ppermute x11 -> x12, starting transfers between devices: 14.1 us -> 17 us  [swap(): lax.ppermute(value, ('dp', 'tensor'), [(i, i ^ flip) for i in range(group...]
    pallas_call x2 -> x3, Pallas kernels: 7.53 us -> 9.42 us  [project(): call(functools.partial(project_kernel, mesh, parts, hops, tile), [jax.Sha...]
    pallas_call x1 -> x0, local copies, waits for them, and re-layouts: 0.65 us -> none  [per_device(): call(functools.partial(solve_kernel, ntrain, rank * rank, share), jax.Sha...]
    pallas_call x1, Pallas kernels: 0.98 us -> 1.61 us  [per_device(): call(functools.partial(solve_kernel, ntrain, rank * rank, share), jax.Sha...]
  transfers between devices with their start and end apart: 11 -> 12, of which waited for: 9 -> 6; matrix products, arithmetic and copies ran while one was open for 0% -> 0% of each run, Pallas kernels for 10% -> 14%
where the time goes in v2:
time: 47 us; the launch traced here: 46.9 us
  waiting for transfers between devices  17.7 us (38%)
  starting transfers between devices  17 us (36%)
  Pallas kernels  11.9 us (25%)
    ppermute x12, waiting for transfers between devices, swap(): lax.ppermute(value, ('dp', 'tensor'), [(i, i ^ flip) for i in range(group...  17.7 us
    ppermute x12, starting transfers between devices, swap(): lax.ppermute(value, ('dp', 'tensor'), [(i, i ^ flip) for i in range(group...  17 us
    pallas_call x3, Pallas kernels, project(): call(functools.partial(project_kernel, mesh, parts, hops, tile), [jax.Sha...  9.42 us
    pallas_call x1, Pallas kernels, per_device(): call(functools.partial(solve_kernel, ntrain, rank * rank, share), jax.Sha...  1.61 us
  transfers between devices with their start and end apart: 12, of which 6 were waited for; matrix products, arithmetic and copies ran while one was open for 0% of the time, Pallas kernels for 14%

profile of v2, /device:TPU:0, one launch (start us, length us, event | category | flops | bytes accessed | tf_op | source)
XLA Modules:
  0.0 46.9 jit_solution(3569475714545685929)
XLA Ops:
  0.0 2.7 %project_3.1 = f32[320,128]{1,0:T(8,128)S(1)} custom-call(s32[1]{0:T(128)} %bitcast.1.at_ref, bf16[1024,3584]{1,0:T(8,128)(2,1)} %bitcast.16, bf16[1024,1024]{1,0:T(8,128)(2,1)} %bitcast.19, bf16[256,3584]{1,0:T(8,128)(2,1)} %bitcast.22, bf16[256,1024]{1,0:T(8,128)(2,1)} %bitcast.25, bf16[64,3584]{1,0:T(8,128)(2,1)} %bitcast.28, bf16[64,1024]{1,0:T(8,128)(2,1)} %bitcast.31), custom_call_target="tpu_custom_call" | custom-call | flops 188743680 | bytes 3538944 | tf_op jit(solution)/shard_map/project_3/pallas_call | solution.py:106
  2.7 5.1 %collective-permute-start = (f32[320,128]{1,0:T(8,128)S(1)}, f32[320,128]{1,0:T(8,128)S(1)}, u32[]{:S(2)}, u32[]{:S(2)}) collective-permute-start(f32[320,128]{1,0:T(8,128)S(1)} %project_3.1), channel_id=1, source_target_pairs={{0,3},{1,2},{2,1},{3,0},{4,7},{5,6},{6,5},{7,4},{8,11},{9,10},{10,... | collective-permute-start | bytes 491528 | tf_op jit(solution)/shard_map/ppermute | solution.py:35
  7.8 4.0 %project_2_1.1 = (f32[320,128]{1,0:T(8,128)S(1)}, f32[320,128]{1,0:T(8,128)S(1)}) custom-call(s32[1]{0:T(128)} %bitcast.1.at_ref, bf16[1024,3584]{1,0:T(8,128)(2,1)} %bitcast.17, bf16[1024,1024]{1,0:T(8,128)(2,1)} %bitcast.20, bf16[256,3584]{1,0:T(8,128)(2,1)} %bitcast.23, bf16[256,1024]{1,0:T(8,128)(2,1)} %bitcast.26, bf16[64,3584]{1,0:T(8,128)(2,1)} %bitcast.29, ...), custom_call_target="tpu_custom_call" | custom-call | flops 377487360 | bytes 6488064 | tf_op jit(solution)/shard_map/project_2_1/pallas_call | solution.py:106
  11.8 0.1 collective-permute-start.1
  11.9 0.6 %collective-permute-start.2 = (f32[320,128]{1,0:T(8,128)S(1)}, f32[320,128]{1,0:T(8,128)S(1)}, u32[]{:S(2)}, u32[]{:S(2)}) collective-permute-start(f32[320,128]{1,0:T(8,128)S(1)} %get-tuple-element.23), channel_id=1, source_target_pairs={{0,1},{1,0},{2,3},{3,2},{4,5},{5,4},{6,7},{7,6},{8,9},{9,8},{10,11... | collective-permute-start | bytes 491528 | tf_op jit(solution)/shard_map/ppermute | solution.py:35
  12.5 0.0 copy-start
  12.5 0.0 copy-start.1
  12.5 2.7 %project_0.1 = f32[320,128]{1,0:T(8,128)S(1)} custom-call(s32[1]{0:T(128)} %bitcast.1.at_ref, bf16[1024,3584]{1,0:T(8,128)(2,1)} %bitcast.18, bf16[1024,1024]{1,0:T(8,128)(2,1)} %bitcast.21, bf16[256,3584]{1,0:T(8,128)(2,1)} %bitcast.24, bf16[256,1024]{1,0:T(8,128)(2,1)} %bitcast.27, bf16[64,3584]{1,0:T(8,128)(2,1)} %bitcast.30, bf16[64,1024]{1,0:T(8,128)(2,1)} %bitcast.33), custom_call_target="tpu_custom_call" | custom-call | flops 188743680 | bytes 3538944 | tf_op jit(solution)/shard_map/project_0/pallas_call | solution.py:106
  15.2 0.0 collective-permute-done
  15.3 6.4 %collective-permute-done.1.refs_1_ = f32[320,128]{1,0:T(8,128)S(1)} collective-permute-done((f32[320,128]{1,0:T(8,128)S(1)}, f32[320,128]{1,0:T(8,128)S(1)}, u32[]{:S(2)}, u32[]{:S(2)}) %collective-permute-start.1) | collective-permute-done | bytes 163872 | tf_op jit(solution)/shard_map/ppermute | solution.py:35
  21.7 0.0 collective-permute-done.2.refs_2_
  21.7 0.0 copy-done
  21.7 0.0 copy-done.1
  21.7 0.4 outer.1
  22.2 0.1 collective-permute-start.3
  22.2 1.2 %collective-permute-done.3 = f32[2,7,8,128]{3,2,1,0:T(8,128)S(1)} collective-permute-done((f32[2,7,8,128]{3,2,1,0:T(8,128)S(1)}, f32[2,7,8,128]{3,2,1,0:T(8,128)S(1)}, u32[]{:S(2)}, u32[]{:S(2)}) %collective-permute-start.3) | collective-permute-done | bytes 57376 | tf_op jit(solution)/shard_map/ppermute | solution.py:35
  23.5 1.3 %collective-permute-start.4 = (f32[9,8,128]{2,1,0:T(8,128)S(1)}, f32[9,8,128]{2,1,0:T(8,128)S(1)}, u32[]{:S(2)}, u32[]{:S(2)}) collective-permute-start(f32[9,8,128]{2,1,0:T(8,128)S(1)} %get-tuple-element.32), channel_id=1, source_target_pairs={{0,12},{1,13},{2,14},{3,15},{4,8},{5,9},{6,10},{7,11},{8,4},{9,5},... | collective-permute-start | bytes 110600 | tf_op jit(solution)/shard_map/ppermute | solution.py:35
  24.8 2.2 %collective-permute-done.4 = f32[9,8,128]{2,1,0:T(8,128)S(1)} collective-permute-done((f32[9,8,128]{2,1,0:T(8,128)S(1)}, f32[9,8,128]{2,1,0:T(8,128)S(1)}, u32[]{:S(2)}, u32[]{:S(2)}) %collective-permute-start.4) | collective-permute-done | bytes 36896 | tf_op jit(solution)/shard_map/ppermute | solution.py:35
  27.0 1.4 %collective-permute-start.5 = (f32[13,8,128]{2,1,0:T(8,128)S(1)}, f32[13,8,128]{2,1,0:T(8,128)S(1)}, u32[]{:S(2)}, u32[]{:S(2)}) collective-permute-start(f32[13,8,128]{2,1,0:T(8,128)S(1)} %pad_maximum_fusion.2), channel_id=1, source_target_pairs={{0,20},{1,21},{2,22},{3,23},{4,16},{5,17},{6,18},{7,19},{8,28},{9,... | collective-permute-start | bytes 159752 | tf_op jit(solution)/shard_map/ppermute | solution.py:35
  28.4 2.5 %collective-permute-start.6 = (f32[8,8,128]{2,1,0:T(8,128)S(1)}, f32[8,8,128]{2,1,0:T(8,128)S(1)}, u32[]{:S(2)}, u32[]{:S(2)}) collective-permute-start(f32[8,8,128]{2,1,0:T(8,128)S(1)} %pad_maximum_fusion.4), channel_id=1, source_target_pairs={{0,3},{1,2},{2,1},{3,0},{4,7},{5,6},{6,5},{7,4},{8,11},{9,10},{10,... | collective-permute-start | bytes 98312 | tf_op jit(solution)/shard_map/ppermute | solution.py:35
  30.9 0.0 collective-permute-done.5
  31.0 0.1 collective-permute-start.8
  31.0 3.0 %collective-permute-start.9 = (f32[20,8,128]{2,1,0:T(8,128)S(1)}, f32[20,8,128]{2,1,0:T(8,128)S(1)}, u32[]{:S(2)}, u32[]{:S(2)}) collective-permute-start(f32[20,8,128]{2,1,0:T(8,128)S(1)} %pad_maximum_fusion.refs_0_), channel_id=1, source_target_pairs={{0,1},{1,0},{2,3},{3,2},{4,5},{5,4},{6,7},{7,6},{8,9},{9,8},{10,11... | collective-permute-start | bytes 245768 | tf_op jit(solution)/shard_map/ppermute | solution.py:35
  34.1 0.0 collective-permute-done.6.refs_1_
  34.1 2.8 %collective-permute-start.7 = (f32[12,8,128]{2,1,0:T(8,128)S(1)}, f32[12,8,128]{2,1,0:T(8,128)S(1)}, u32[]{:S(2)}, u32[]{:S(2)}) collective-permute-start(f32[12,8,128]{2,1,0:T(8,128)S(1)} %pad_maximum_fusion.3), channel_id=1, source_target_pairs={{0,3},{1,2},{2,1},{3,0},{4,7},{5,6},{6,5},{7,4},{8,11},{9,10},{10,... | collective-permute-start | bytes 147464 | tf_op jit(solution)/shard_map/ppermute | solution.py:35
  36.9 3.3 %collective-permute-done.7.refs_2_ = f32[12,8,128]{2,1,0:T(8,128)S(1)} collective-permute-done((f32[12,8,128]{2,1,0:T(8,128)S(1)}, f32[12,8,128]{2,1,0:T(8,128)S(1)}, u32[]{:S(2)}, u32[]{:S(2)}) %collective-permute-start.7) | collective-permute-done | bytes 49184 | tf_op jit(solution)/shard_map/ppermute | solution.py:35
  40.1 0.0 collective-permute-done.8.refs_3_
  40.1 0.0 collective-permute-done.9.refs_4_
  40.1 0.5 gram.1
  40.6 0.0 collective-permute-start.10
  40.6 3.5 %collective-permute-done.10 = f32[48,128]{1,0:T(8,128)S(1)} collective-permute-done((f32[48,128]{1,0:T(8,128)S(1)}, f32[48,128]{1,0:T(8,128)S(1)}, u32[]{:S(2)}, u32[]{:S(2)}) %collective-permute-start.10) | collective-permute-done | bytes 24608 | tf_op jit(solution)/shard_map/ppermute | solution.py:35
  44.1 0.1 collective-permute-start.11
  44.2 1.1 %collective-permute-done.11.two_ref = f32[48,128]{1,0:T(8,128)S(1)} collective-permute-done((f32[48,128]{1,0:T(8,128)S(1)}, f32[48,128]{1,0:T(8,128)S(1)}, u32[]{:S(2)}, u32[]{:S(2)}) %collective-permute-start.11) | collective-permute-done | bytes 24608 | tf_op jit(solution)/shard_map/ppermute | solution.py:35
  45.3 1.6 %solve.1 = f32[2,16]{1,0:T(2,128)} custom-call(s32[1]{0:T(128)} %bitcast.low_ref, f32[48,128]{1,0:T(8,128)S(1)} %add.27.one_ref, f32[48,128]{1,0:T(8,128)S(1)} %collective-permute-done.11.two_ref), custom_call_target="tpu_custom_call" | custom-call | tf_op jit(solution)/shard_map/solve/pallas_call | solution.py:377
  (16 shorter events, 0.1 us)
Async XLA Ops:
  2.7 12.5 %collective-permute-start = (f32[320,128]{1,0:T(8,128)S(1)}, f32[320,128]{1,0:T(8,128)S(1)}, u32[]{:S(2)}, u32[]{:S(2)}) collective-permute-start(f32[320,128]{1,0:T(8,128)S(1)} %project_3.1), channel_id=1, source_target_pairs={{0,3},{1,2},{2,1},{3,0},{4,7},{5,6},{6,5},{7,4},{8,11},{9,10},{10,... | collective-permute-start | bytes 491528 | tf_op jit(solution)/shard_map/ppermute | solution.py:35
  11.8 9.9 %collective-permute-start.1 = (f32[320,128]{1,0:T(8,128)S(1)}, f32[320,128]{1,0:T(8,128)S(1)}, u32[]{:S(2)}, u32[]{:S(2)}) collective-permute-start(f32[320,128]{1,0:T(8,128)S(1)} %get-tuple-element.22), channel_id=1, source_target_pairs={{0,2},{1,3},{2,0},{3,1},{4,6},{5,7},{6,4},{7,5},{8,10},{9,11},{10,... | collective-permute-start | bytes 491528 | tf_op jit(solution)/shard_map/ppermute | solution.py:35
  11.9 9.8 %collective-permute-start.2 = (f32[320,128]{1,0:T(8,128)S(1)}, f32[320,128]{1,0:T(8,128)S(1)}, u32[]{:S(2)}, u32[]{:S(2)}) collective-permute-start(f32[320,128]{1,0:T(8,128)S(1)} %get-tuple-element.23), channel_id=1, source_target_pairs={{0,1},{1,0},{2,3},{3,2},{4,5},{5,4},{6,7},{7,6},{8,9},{9,8},{10,11... | collective-permute-start | bytes 491528 | tf_op jit(solution)/shard_map/ppermute | solution.py:35
  12.5 9.2 %copy-start = (s32[16,16]{1,0:T(8,128)S(1)}, s32[16,16]{1,0:T(8,128)}, u32[]{:S(2)}) copy-start(s32[16,16]{1,0:T(8,128)} %qids_ref.1) | copy-start | bytes 3076
  12.5 9.2 %copy-start.1 = (s32[8,128]{1,0:T(8,128)S(1)}, s32[8,128]{1,0:T(8,128)}, u32[]{:S(2)}) copy-start(s32[8,128]{1,0:T(8,128)} %ids_ref.1) | copy-start | bytes 12292
  22.2 1.3 %collective-permute-start.3 = (f32[2,7,8,128]{3,2,1,0:T(8,128)S(1)}, f32[2,7,8,128]{3,2,1,0:T(8,128)S(1)}, u32[]{:S(2)}, u32[]{:S(2)}) collective-permute-start(f32[2,7,8,128]{3,2,1,0:T(8,128)S(1)} %get-tuple-element.25), channel_id=1, source_target_pairs={{0,4},{1,5},{2,6},{3,7},{4,0},{5,1},{6,2},{7,3},{8,12},{9,13},{10,... | collective-permute-start | bytes 172040 | tf_op jit(solution)/shard_map/ppermute | solution.py:35
  23.5 3.5 %collective-permute-start.4 = (f32[9,8,128]{2,1,0:T(8,128)S(1)}, f32[9,8,128]{2,1,0:T(8,128)S(1)}, u32[]{:S(2)}, u32[]{:S(2)}) collective-permute-start(f32[9,8,128]{2,1,0:T(8,128)S(1)} %get-tuple-element.32), channel_id=1, source_target_pairs={{0,12},{1,13},{2,14},{3,15},{4,8},{5,9},{6,10},{7,11},{8,4},{9,5},... | collective-permute-start | bytes 110600 | tf_op jit(solution)/shard_map/ppermute | solution.py:35
  27.0 3.9 %collective-permute-start.5 = (f32[13,8,128]{2,1,0:T(8,128)S(1)}, f32[13,8,128]{2,1,0:T(8,128)S(1)}, u32[]{:S(2)}, u32[]{:S(2)}) collective-permute-start(f32[13,8,128]{2,1,0:T(8,128)S(1)} %pad_maximum_fusion.2), channel_id=1, source_target_pairs={{0,20},{1,21},{2,22},{3,23},{4,16},{5,17},{6,18},{7,19},{8,28},{9,... | collective-permute-start | bytes 159752 | tf_op jit(solution)/shard_map/ppermute | solution.py:35
  28.4 5.7 %collective-permute-start.6 = (f32[8,8,128]{2,1,0:T(8,128)S(1)}, f32[8,8,128]{2,1,0:T(8,128)S(1)}, u32[]{:S(2)}, u32[]{:S(2)}) collective-permute-start(f32[8,8,128]{2,1,0:T(8,128)S(1)} %pad_maximum_fusion.4), channel_id=1, source_target_pairs={{0,3},{1,2},{2,1},{3,0},{4,7},{5,6},{6,5},{7,4},{8,11},{9,10},{10,... | collective-permute-start | bytes 98312 | tf_op jit(solution)/shard_map/ppermute | solution.py:35
  31.0 9.2 %collective-permute-start.8 = (f32[20,8,128]{2,1,0:T(8,128)S(1)}, f32[20,8,128]{2,1,0:T(8,128)S(1)}, u32[]{:S(2)}, u32[]{:S(2)}) collective-permute-start(f32[20,8,128]{2,1,0:T(8,128)S(1)} %pad_maximum_fusion.refs_0_), channel_id=1, source_target_pairs={{0,2},{1,3},{2,0},{3,1},{4,6},{5,7},{6,4},{7,5},{8,10},{9,11},{10,... | collective-permute-start | bytes 245768 | tf_op jit(solution)/shard_map/ppermute | solution.py:35
  31.0 9.1 %collective-permute-start.9 = (f32[20,8,128]{2,1,0:T(8,128)S(1)}, f32[20,8,128]{2,1,0:T(8,128)S(1)}, u32[]{:S(2)}, u32[]{:S(2)}) collective-permute-start(f32[20,8,128]{2,1,0:T(8,128)S(1)} %pad_maximum_fusion.refs_0_), channel_id=1, source_target_pairs={{0,1},{1,0},{2,3},{3,2},{4,5},{5,4},{6,7},{7,6},{8,9},{9,8},{10,11... | collective-permute-start | bytes 245768 | tf_op jit(solution)/shard_map/ppermute | solution.py:35
  34.1 6.0 %collective-permute-start.7 = (f32[12,8,128]{2,1,0:T(8,128)S(1)}, f32[12,8,128]{2,1,0:T(8,128)S(1)}, u32[]{:S(2)}, u32[]{:S(2)}) collective-permute-start(f32[12,8,128]{2,1,0:T(8,128)S(1)} %pad_maximum_fusion.3), channel_id=1, source_target_pairs={{0,3},{1,2},{2,1},{3,0},{4,7},{5,6},{6,5},{7,4},{8,11},{9,10},{10,... | collective-permute-start | bytes 147464 | tf_op jit(solution)/shard_map/ppermute | solution.py:35
  40.6 3.5 %collective-permute-start.10 = (f32[48,128]{1,0:T(8,128)S(1)}, f32[48,128]{1,0:T(8,128)S(1)}, u32[]{:S(2)}, u32[]{:S(2)}) collective-permute-start(f32[48,128]{1,0:T(8,128)S(1)} %gram.1), channel_id=1, source_target_pairs={{0,12},{1,13},{2,14},{3,15},{4,8},{5,9},{6,10},{7,11},{8,4},{9,5},... | collective-permute-start | bytes 73736 | tf_op jit(solution)/shard_map/ppermute | solution.py:35
  44.1 1.2 %collective-permute-start.11 = (f32[48,128]{1,0:T(8,128)S(1)}, f32[48,128]{1,0:T(8,128)S(1)}, u32[]{:S(2)}, u32[]{:S(2)}) collective-permute-start(f32[48,128]{1,0:T(8,128)S(1)} %add.27.one_ref), channel_id=1, source_target_pairs={{0,4},{1,5},{2,6},{3,7},{4,0},{5,1},{6,2},{7,3},{8,12},{9,13},{10,... | collective-permute-start | bytes 73736 | tf_op jit(solution)/shard_map/ppermute | solution.py:35

commit v3 on v2

--- a/solution.py
+++ b/solution.py
@@ -46,9 +46,12 @@
     sides = ((th_ref, qh_ref, hid, pin_ref, pin), (tg_ref, qg_ref, grad, pout_ref, pout))
     chunks = []
     started = 0
-    for side, (train, query, buf, weight, held) in enumerate(sides):
-        first = 4 * tile if side == 0 else buf.shape[1]
-        for start, size in ((0, first), (first, buf.shape[1] - first)):
+    for side in (1, 0):
+        train, query, buf, weight, held = sides[side]
+        wide = buf.shape[1]
+        first = wide if side else 4 * tile
+        second = (wide - first + tile) // (2 * tile) * tile
+        for start, size in ((0, first), (first, second), (first + second, wide - first - second)):
             if not size:
                 continue
             cols = pl.ds(start, size)
@@ -114,7 +117,7 @@
             pltpu.VMEM((held, width), bf16),
             pltpu.VMEM((rank, ff), bf16),
             pltpu.VMEM((rank, width), bf16),
-            pltpu.SemaphoreType.DMA((2 + 5 * len(hops),)),
+            pltpu.SemaphoreType.DMA((2 + 6 * len(hops),)),
         ],
         cost_estimate=pl.CostEstimate(
             flops=2 * held * (ff + width) * rank,
@@ -221,8 +224,9 @@
     if folds(ntrain):
         half = ntrain // 2
         out_ref[:half, :] = jnp.concatenate([total[:half, :ntrain], total[half:ntrain, :ntrain]], axis=1)
-        out_ref[half:, :size] = total[ntrain:]
-        out_ref[half:, size:] = jnp.zeros((nquery, 2 * ntrain - size), F32)
+        rest = [total[start : start + nquery, ntrain:] for start in range(0, size, nquery)]
+        rest.append(jnp.zeros((nquery, 2 * ntrain - size), F32))
+        out_ref[half:, :] = jnp.concatenate(rest, axis=1)
     else:
         out_ref[...] = total
 
@@ -238,22 +242,24 @@
         half = ntrain // 2
         gram = jnp.concatenate([whole[:half, :ntrain], whole[:half, ntrain:]], axis=0)
         rest = whole[half:]
+        cross = [rest[:, start : start + nquery] for start in range(0, ntrain, nquery)]
+        cross = jnp.concatenate(cross, axis=0)
+        square = rest[:, ntrain : ntrain + nquery]
     else:
         gram = whole[:ntrain, :ntrain]
-        rest = whole[ntrain:]
-    cross = rest[:, :ntrain]
-    square = rest[:, ntrain : ntrain + nquery]
-
-    def rowsum(v):
-        return jnp.sum(v, axis=1, keepdims=True)
+        cross = whole[:ntrain, ntrain:]
+        square = whole[ntrain:, ntrain:]
+
+    def colsum(v):
+        return jnp.sum(v, axis=0, keepdims=True)
 
     def diagonal(v):
         rows = lax.broadcasted_iota(jnp.int32, v.shape, 0)
         cols = lax.broadcasted_iota(jnp.int32, v.shape, 1)
         return jnp.where(rows == cols, v, 0.0)
 
-    norm = rowsum(diagonal(square))
-    trace = jnp.sum(diagonal(gram)) / ntrain
+    norm = colsum(diagonal(square))
+    trace = jnp.sum(colsum(diagonal(gram)), axis=1, keepdims=True) / ntrain
     scale = 1.0 / (ntrain * (DAMP * trace / feat))
 
     def thirds(value):
@@ -261,12 +267,13 @@
         low = value - high.astype(F32) - rest.astype(F32)
         return high, rest, low.astype(jnp.bfloat16)
 
-    gram_parts = thirds(gram)
+    gram_parts = jnp.concatenate(thirds(gram), axis=0)
 
     def times_gram(value):
-        left = jnp.concatenate(thirds(value), axis=0)
-        out = sum(jnp.dot(left, part, preferred_element_type=F32) for part in gram_parts[::-1])
-        return out[2 * nquery :] + out[nquery : 2 * nquery] + out[:nquery]
+        out = sum(
+            jnp.dot(gram_parts, part, preferred_element_type=F32) for part in thirds(value)[::-1]
+        )
+        return out[2 * ntrain :] + out[ntrain : 2 * ntrain] + out[:ntrain]
 
     res_a, res_x, res_p = jnp.ones_like(norm), jnp.zeros_like(cross), cross
     dir_a, dir_x, dir_p = res_a, res_x, res_p
@@ -276,20 +283,20 @@
         inner = dir_p * dir_p * scale
         if step:
             inner = inner + dir_x * (dir_a * cross + dir_p)
-        alpha = now / (dir_a * dir_a * norm + rowsum(inner))
+        alpha = now / (dir_a * dir_a * norm + colsum(inner))
         solved = solved + alpha * dir_p
         if step == ITERS - 1:
             break
         res_a = res_a - alpha * dir_a
         res_x = res_x - alpha * (dir_x + dir_p * scale)
         res_p = res_a * cross + times_gram(res_x)
-        fresh = res_a * res_a * norm + rowsum(res_x * (res_a * cross + res_p))
+        fresh = res_a * res_a * norm + colsum(res_x * (res_a * cross + res_p))
         beta = fresh / now
         dir_a = res_a + beta * dir_a
         dir_x = res_x + beta * dir_x
         dir_p = res_p + beta * dir_p
         now = fresh
-    columns[...] = solved.T
+    columns[...] = solved
     out_ref[...] = columns[pl.ds(low_ref[0] * share, share), :]
 
 
@@ -355,15 +362,15 @@
     nex = block.shape[0] - qshare - 1
     own = block[:nex]
     other = swap(block, flip | 1, 0)
-    early = swap(own, 0, 3)
+    early = swap(own, 0, 2)
     rest = (block + other)[nex:]
     after = jnp.concatenate([other[:nex], rest[:qshare] / rest[qshare, :qshare, None, :]], axis=0)
     whole = jnp.concatenate([own, after], axis=0)
-    far = swap(whole, 0, 2)
-    late = swap(lax.optimization_barrier((after, early))[0], 0, 3)
+    far = swap(whole, 0, 3)
+    late = swap(lax.optimization_barrier((after, early))[0], 0, 2)
     near = swap(whole, 0, 1)
     blocks = [whole, early, late, far, near]
-    hops = ((0, (0,)), (3, (1, 2)), (2, (3,)), (1, (4,)))
+    hops = ((0, (0,)), (2, (1, 2)), (3, (3,)), (1, (4,)))
     size = ntrain + nquery
     shape = (ntrain // 2 + nquery, 2 * ntrain) if folds(ntrain) else (size, size)
     gram = call(

time: 47 us -> 46.8 us (level)
  waiting for transfers between devices: 17.7 us -> 20.6 us
  starting transfers between devices: 17 us -> 14.2 us
    ppermute x12, waiting for transfers between devices: 17.7 us -> 20.6 us  [swap(): lax.ppermute(value, ('dp', 'tensor'), [(i, i ^ flip) for i in range(group...]
    ppermute x12, starting transfers between devices: 17 us -> 14.2 us  [swap(): lax.ppermute(value, ('dp', 'tensor'), [(i, i ^ flip) for i in range(group...]
  transfers between devices with their start and end apart: 12 -> 12, of which waited for: 6 -> 8; matrix products, arithmetic and copies ran while one was open for 0% -> 0% of each run, Pallas kernels for 14% -> 14%
where the time goes in v3:
time: 46.8 us; the launch traced here: 46.6 us
  waiting for transfers between devices  20.6 us (44%)
  starting transfers between devices  14.2 us (30%)
  Pallas kernels  11.5 us (25%)
    ppermute x12, waiting for transfers between devices, swap(): lax.ppermute(value, ('dp', 'tensor'), [(i, i ^ flip) for i in range(group...  20.6 us
    ppermute x12, starting transfers between devices, swap(): lax.ppermute(value, ('dp', 'tensor'), [(i, i ^ flip) for i in range(group...  14.2 us
    pallas_call x3, Pallas kernels, project(): call(functools.partial(project_kernel, mesh, parts, hops, tile), [jax.Sha...  9.32 us
    pallas_call x1, Pallas kernels, per_device(): call(functools.partial(solve_kernel, ntrain, rank * rank, share), jax.Sha...  1.29 us
  transfers between devices with their start and end apart: 12, of which 8 were waited for; matrix products, arithmetic and copies ran while one was open for 0% of the time, Pallas kernels for 14%

profile of v3, /device:TPU:0, one launch (start us, length us, event | category | flops | bytes accessed | tf_op | source)
XLA Modules:
  0.0 46.6 jit_solution(14490154462145171476)
XLA Ops:
  0.0 2.7 %project_3.1 = f32[320,128]{1,0:T(8,128)S(1)} custom-call(s32[1]{0:T(128)} %bitcast.1.at_ref, bf16[1024,3584]{1,0:T(8,128)(2,1)} %bitcast.16, bf16[1024,1024]{1,0:T(8,128)(2,1)} %bitcast.19, bf16[256,3584]{1,0:T(8,128)(2,1)} %bitcast.22, bf16[256,1024]{1,0:T(8,128)(2,1)} %bitcast.25, bf16[64,3584]{1,0:T(8,128)(2,1)} %bitcast.28, bf16[64,1024]{1,0:T(8,128)(2,1)} %bitcast.31), custom_call_target="tpu_custom_call" | custom-call | flops 188743680 | bytes 3538944 | tf_op jit(solution)/shard_map/project_3/pallas_call | solution.py:109
  2.7 5.1 %collective-permute-start = (f32[320,128]{1,0:T(8,128)S(1)}, f32[320,128]{1,0:T(8,128)S(1)}, u32[]{:S(2)}, u32[]{:S(2)}) collective-permute-start(f32[320,128]{1,0:T(8,128)S(1)} %project_3.1), channel_id=1, source_target_pairs={{0,3},{1,2},{2,1},{3,0},{4,7},{5,6},{6,5},{7,4},{8,11},{9,10},{10,... | collective-permute-start | bytes 491528 | tf_op jit(solution)/shard_map/ppermute | solution.py:35
  7.8 3.9 %project_2_1.1 = (f32[320,128]{1,0:T(8,128)S(1)}, f32[320,128]{1,0:T(8,128)S(1)}) custom-call(s32[1]{0:T(128)} %bitcast.1.at_ref, bf16[1024,3584]{1,0:T(8,128)(2,1)} %bitcast.17, bf16[1024,1024]{1,0:T(8,128)(2,1)} %bitcast.20, bf16[256,3584]{1,0:T(8,128)(2,1)} %bitcast.23, bf16[256,1024]{1,0:T(8,128)(2,1)} %bitcast.26, bf16[64,3584]{1,0:T(8,128)(2,1)} %bitcast.29, ...), custom_call_target="tpu_custom_call" | custom-call | flops 377487360 | bytes 6488064 | tf_op jit(solution)/shard_map/project_2_1/pallas_call | solution.py:109
  11.7 0.1 collective-permute-start.1
  11.8 0.6 %collective-permute-start.2 = (f32[320,128]{1,0:T(8,128)S(1)}, f32[320,128]{1,0:T(8,128)S(1)}, u32[]{:S(2)}, u32[]{:S(2)}) collective-permute-start(f32[320,128]{1,0:T(8,128)S(1)} %get-tuple-element.23), channel_id=1, source_target_pairs={{0,1},{1,0},{2,3},{3,2},{4,5},{5,4},{6,7},{7,6},{8,9},{9,8},{10,11... | collective-permute-start | bytes 491528 | tf_op jit(solution)/shard_map/ppermute | solution.py:35
  12.4 0.0 copy-start
  12.4 0.0 copy-start.1
  12.4 2.7 %project_0.1 = f32[320,128]{1,0:T(8,128)S(1)} custom-call(s32[1]{0:T(128)} %bitcast.1.at_ref, bf16[1024,3584]{1,0:T(8,128)(2,1)} %bitcast.18, bf16[1024,1024]{1,0:T(8,128)(2,1)} %bitcast.21, bf16[256,3584]{1,0:T(8,128)(2,1)} %bitcast.24, bf16[256,1024]{1,0:T(8,128)(2,1)} %bitcast.27, bf16[64,3584]{1,0:T(8,128)(2,1)} %bitcast.30, bf16[64,1024]{1,0:T(8,128)(2,1)} %bitcast.33), custom_call_target="tpu_custom_call" | custom-call | flops 188743680 | bytes 3538944 | tf_op jit(solution)/shard_map/project_0/pallas_call | solution.py:109
  15.1 0.0 collective-permute-done
  15.2 6.5 %collective-permute-done.1.refs_1_ = f32[320,128]{1,0:T(8,128)S(1)} collective-permute-done((f32[320,128]{1,0:T(8,128)S(1)}, f32[320,128]{1,0:T(8,128)S(1)}, u32[]{:S(2)}, u32[]{:S(2)}) %collective-permute-start.1) | collective-permute-done | bytes 163872 | tf_op jit(solution)/shard_map/ppermute | solution.py:35
  21.7 0.0 collective-permute-done.2.refs_2_
  21.7 0.0 copy-done
  21.7 0.0 copy-done.1
  21.7 0.4 outer.1
  22.1 0.1 collective-permute-start.3
  22.2 1.2 %collective-permute-done.3 = f32[2,7,8,128]{3,2,1,0:T(8,128)S(1)} collective-permute-done((f32[2,7,8,128]{3,2,1,0:T(8,128)S(1)}, f32[2,7,8,128]{3,2,1,0:T(8,128)S(1)}, u32[]{:S(2)}, u32[]{:S(2)}) %collective-permute-start.3) | collective-permute-done | bytes 57376 | tf_op jit(solution)/shard_map/ppermute | solution.py:35
  23.5 1.3 %collective-permute-start.4 = (f32[9,8,128]{2,1,0:T(8,128)S(1)}, f32[9,8,128]{2,1,0:T(8,128)S(1)}, u32[]{:S(2)}, u32[]{:S(2)}) collective-permute-start(f32[9,8,128]{2,1,0:T(8,128)S(1)} %get-tuple-element.32), channel_id=1, source_target_pairs={{0,12},{1,13},{2,14},{3,15},{4,8},{5,9},{6,10},{7,11},{8,4},{9,5},... | collective-permute-start | bytes 110600 | tf_op jit(solution)/shard_map/ppermute | solution.py:35
  24.8 2.2 %collective-permute-done.4 = f32[9,8,128]{2,1,0:T(8,128)S(1)} collective-permute-done((f32[9,8,128]{2,1,0:T(8,128)S(1)}, f32[9,8,128]{2,1,0:T(8,128)S(1)}, u32[]{:S(2)}, u32[]{:S(2)}) %collective-permute-start.4) | collective-permute-done | bytes 36896 | tf_op jit(solution)/shard_map/ppermute | solution.py:35
  27.0 1.3 %collective-permute-start.5 = (f32[13,8,128]{2,1,0:T(8,128)S(1)}, f32[13,8,128]{2,1,0:T(8,128)S(1)}, u32[]{:S(2)}, u32[]{:S(2)}) collective-permute-start(f32[13,8,128]{2,1,0:T(8,128)S(1)} %pad_maximum_fusion.2), channel_id=1, source_target_pairs={{0,20},{1,21},{2,22},{3,23},{4,16},{5,17},{6,18},{7,19},{8,28},{9,... | collective-permute-start | bytes 159752 | tf_op jit(solution)/shard_map/ppermute | solution.py:35
  28.4 0.0 collective-permute-start.6
  28.4 2.5 %collective-permute-done.5 = f32[13,8,128]{2,1,0:T(8,128)S(1)} collective-permute-done((f32[13,8,128]{2,1,0:T(8,128)S(1)}, f32[13,8,128]{2,1,0:T(8,128)S(1)}, u32[]{:S(2)}, u32[]{:S(2)}) %collective-permute-start.5) | collective-permute-done | bytes 53280 | tf_op jit(solution)/shard_map/ppermute | solution.py:35
  31.0 2.6 %collective-permute-start.8 = (f32[20,8,128]{2,1,0:T(8,128)S(1)}, f32[20,8,128]{2,1,0:T(8,128)S(1)}, u32[]{:S(2)}, u32[]{:S(2)}) collective-permute-start(f32[20,8,128]{2,1,0:T(8,128)S(1)} %pad_maximum_fusion.refs_0_), channel_id=1, source_target_pairs={{0,3},{1,2},{2,1},{3,0},{4,7},{5,6},{6,5},{7,4},{8,11},{9,10},{10,... | collective-permute-start | bytes 245768 | tf_op jit(solution)/shard_map/ppermute | solution.py:35
  33.5 0.0 collective-permute-start.9
  33.5 0.0 collective-permute-done.6.refs_1_
  33.5 2.0 %collective-permute-start.7 = (f32[12,8,128]{2,1,0:T(8,128)S(1)}, f32[12,8,128]{2,1,0:T(8,128)S(1)}, u32[]{:S(2)}, u32[]{:S(2)}) collective-permute-start(f32[12,8,128]{2,1,0:T(8,128)S(1)} %pad_maximum_fusion.3), channel_id=1, source_target_pairs={{0,2},{1,3},{2,0},{3,1},{4,6},{5,7},{6,4},{7,5},{8,10},{9,11},{10,... | collective-permute-start | bytes 147464 | tf_op jit(solution)/shard_map/ppermute | solution.py:35
  35.5 3.4 %collective-permute-done.7.refs_2_ = f32[12,8,128]{2,1,0:T(8,128)S(1)} collective-permute-done((f32[12,8,128]{2,1,0:T(8,128)S(1)}, f32[12,8,128]{2,1,0:T(8,128)S(1)}, u32[]{:S(2)}, u32[]{:S(2)}) %collective-permute-start.7) | collective-permute-done | bytes 49184 | tf_op jit(solution)/shard_map/ppermute | solution.py:35
  38.9 0.0 collective-permute-done.8.refs_3_
  38.9 1.2 %collective-permute-done.9.refs_4_ = f32[20,8,128]{2,1,0:T(8,128)S(1)} collective-permute-done((f32[20,8,128]{2,1,0:T(8,128)S(1)}, f32[20,8,128]{2,1,0:T(8,128)S(1)}, u32[]{:S(2)}, u32[]{:S(2)}) %collective-permute-start.9) | collective-permute-done | bytes 81952 | tf_op jit(solution)/shard_map/ppermute | solution.py:35
  40.1 0.5 %gram.1 = f32[48,128]{1,0:T(8,128)S(1)} custom-call(s32[1]{0:T(128)} %bitcast.1.at_ref, f32[20,8,128]{2,1,0:T(8,128)S(1)} %pad_maximum_fusion.refs_0_, f32[8,8,128]{2,1,0:T(8,128)S(1)} %collective-permute-done.6.refs_1_, f32[12,8,128]{2,1,0:T(8,128)S(1)} %collective-permute-done.7.refs_2_, f32[20,8,128]{2,1,0:T(8,128)S(1)} %collective-permute-done.8.refs_3_, ...), custom_call_target="tpu_custom_call" | custom-call | tf_op jit(solution)/shard_map/gram/pallas_call | solution.py:376
  40.6 1.1 %collective-permute-start.10 = (f32[48,128]{1,0:T(8,128)S(1)}, f32[48,128]{1,0:T(8,128)S(1)}, u32[]{:S(2)}, u32[]{:S(2)}) collective-permute-start(f32[48,128]{1,0:T(8,128)S(1)} %gram.1), channel_id=1, source_target_pairs={{0,12},{1,13},{2,14},{3,15},{4,8},{5,9},{6,10},{7,11},{8,4},{9,5},... | collective-permute-start | bytes 73736 | tf_op jit(solution)/shard_map/ppermute | solution.py:35
  41.7 2.5 %collective-permute-done.10 = f32[48,128]{1,0:T(8,128)S(1)} collective-permute-done((f32[48,128]{1,0:T(8,128)S(1)}, f32[48,128]{1,0:T(8,128)S(1)}, u32[]{:S(2)}, u32[]{:S(2)}) %collective-permute-start.10) | collective-permute-done | bytes 24608 | tf_op jit(solution)/shard_map/ppermute | solution.py:35
  44.1 0.1 collective-permute-start.11
  44.3 1.1 %collective-permute-done.11.two_ref = f32[48,128]{1,0:T(8,128)S(1)} collective-permute-done((f32[48,128]{1,0:T(8,128)S(1)}, f32[48,128]{1,0:T(8,128)S(1)}, u32[]{:S(2)}, u32[]{:S(2)}) %collective-permute-start.11) | collective-permute-done | bytes 24608 | tf_op jit(solution)/shard_map/ppermute | solution.py:35
  45.3 1.3 %solve.1 = f32[2,16]{1,0:T(2,128)} custom-call(s32[1]{0:T(128)} %bitcast.low_ref, f32[48,128]{1,0:T(8,128)S(1)} %add.27.one_ref, f32[48,128]{1,0:T(8,128)S(1)} %collective-permute-done.11.two_ref), custom_call_target="tpu_custom_call" | custom-call | tf_op jit(solution)/shard_map/solve/pallas_call | solution.py:384
  (16 shorter events, 0.1 us)
Async XLA Ops:
  2.7 12.4 %collective-permute-start = (f32[320,128]{1,0:T(8,128)S(1)}, f32[320,128]{1,0:T(8,128)S(1)}, u32[]{:S(2)}, u32[]{:S(2)}) collective-permute-start(f32[320,128]{1,0:T(8,128)S(1)} %project_3.1), channel_id=1, source_target_pairs={{0,3},{1,2},{2,1},{3,0},{4,7},{5,6},{6,5},{7,4},{8,11},{9,10},{10,... | collective-permute-start | bytes 491528 | tf_op jit(solution)/shard_map/ppermute | solution.py:35
  11.7 10.0 %collective-permute-start.1 = (f32[320,128]{1,0:T(8,128)S(1)}, f32[320,128]{1,0:T(8,128)S(1)}, u32[]{:S(2)}, u32[]{:S(2)}) collective-permute-start(f32[320,128]{1,0:T(8,128)S(1)} %get-tuple-element.22), channel_id=1, source_target_pairs={{0,2},{1,3},{2,0},{3,1},{4,6},{5,7},{6,4},{7,5},{8,10},{9,11},{10,... | collective-permute-start | bytes 491528 | tf_op jit(solution)/shard_map/ppermute | solution.py:35
  11.8 9.9 %collective-permute-start.2 = (f32[320,128]{1,0:T(8,128)S(1)}, f32[320,128]{1,0:T(8,128)S(1)}, u32[]{:S(2)}, u32[]{:S(2)}) collective-permute-start(f32[320,128]{1,0:T(8,128)S(1)} %get-tuple-element.23), channel_id=1, source_target_pairs={{0,1},{1,0},{2,3},{3,2},{4,5},{5,4},{6,7},{7,6},{8,9},{9,8},{10,11... | collective-permute-start | bytes 491528 | tf_op jit(solution)/shard_map/ppermute | solution.py:35
  12.4 9.3 %copy-start = (s32[16,16]{1,0:T(8,128)S(1)}, s32[16,16]{1,0:T(8,128)}, u32[]{:S(2)}) copy-start(s32[16,16]{1,0:T(8,128)} %qids_ref.1) | copy-start | bytes 3076
  12.4 9.3 %copy-start.1 = (s32[8,128]{1,0:T(8,128)S(1)}, s32[8,128]{1,0:T(8,128)}, u32[]{:S(2)}) copy-start(s32[8,128]{1,0:T(8,128)} %ids_ref.1) | copy-start | bytes 12292
  22.1 1.3 %collective-permute-start.3 = (f32[2,7,8,128]{3,2,1,0:T(8,128)S(1)}, f32[2,7,8,128]{3,2,1,0:T(8,128)S(1)}, u32[]{:S(2)}, u32[]{:S(2)}) collective-permute-start(f32[2,7,8,128]{3,2,1,0:T(8,128)S(1)} %get-tuple-element.25), channel_id=1, source_target_pairs={{0,4},{1,5},{2,6},{3,7},{4,0},{5,1},{6,2},{7,3},{8,12},{9,13},{10,... | collective-permute-start | bytes 172040 | tf_op jit(solution)/shard_map/ppermute | solution.py:35
  23.5 3.5 %collective-permute-start.4 = (f32[9,8,128]{2,1,0:T(8,128)S(1)}, f32[9,8,128]{2,1,0:T(8,128)S(1)}, u32[]{:S(2)}, u32[]{:S(2)}) collective-permute-start(f32[9,8,128]{2,1,0:T(8,128)S(1)} %get-tuple-element.32), channel_id=1, source_target_pairs={{0,12},{1,13},{2,14},{3,15},{4,8},{5,9},{6,10},{7,11},{8,4},{9,5},... | collective-permute-start | bytes 110600 | tf_op jit(solution)/shard_map/ppermute | solution.py:35
  27.0 3.9 %collective-permute-start.5 = (f32[13,8,128]{2,1,0:T(8,128)S(1)}, f32[13,8,128]{2,1,0:T(8,128)S(1)}, u32[]{:S(2)}, u32[]{:S(2)}) collective-permute-start(f32[13,8,128]{2,1,0:T(8,128)S(1)} %pad_maximum_fusion.2), channel_id=1, source_target_pairs={{0,20},{1,21},{2,22},{3,23},{4,16},{5,17},{6,18},{7,19},{8,28},{9,... | collective-permute-start | bytes 159752 | tf_op jit(solution)/shard_map/ppermute | solution.py:35
  28.4 5.1 %collective-permute-start.6 = (f32[8,8,128]{2,1,0:T(8,128)S(1)}, f32[8,8,128]{2,1,0:T(8,128)S(1)}, u32[]{:S(2)}, u32[]{:S(2)}) collective-permute-start(f32[8,8,128]{2,1,0:T(8,128)S(1)} %pad_maximum_fusion.4), channel_id=1, source_target_pairs={{0,2},{1,3},{2,0},{3,1},{4,6},{5,7},{6,4},{7,5},{8,10},{9,11},{10,... | collective-permute-start | bytes 98312 | tf_op jit(solution)/shard_map/ppermute | solution.py:35
  31.0 8.0 %collective-permute-start.8 = (f32[20,8,128]{2,1,0:T(8,128)S(1)}, f32[20,8,128]{2,1,0:T(8,128)S(1)}, u32[]{:S(2)}, u32[]{:S(2)}) collective-permute-start(f32[20,8,128]{2,1,0:T(8,128)S(1)} %pad_maximum_fusion.refs_0_), channel_id=1, source_target_pairs={{0,3},{1,2},{2,1},{3,0},{4,7},{5,6},{6,5},{7,4},{8,11},{9,10},{10,... | collective-permute-start | bytes 245768 | tf_op jit(solution)/shard_map/ppermute | solution.py:35
  33.5 6.6 %collective-permute-start.9 = (f32[20,8,128]{2,1,0:T(8,128)S(1)}, f32[20,8,128]{2,1,0:T(8,128)S(1)}, u32[]{:S(2)}, u32[]{:S(2)}) collective-permute-start(f32[20,8,128]{2,1,0:T(8,128)S(1)} %pad_maximum_fusion.refs_0_), channel_id=1, source_target_pairs={{0,1},{1,0},{2,3},{3,2},{4,5},{5,4},{6,7},{7,6},{8,9},{9,8},{10,11... | collective-permute-start | bytes 245768 | tf_op jit(solution)/shard_map/ppermute | solution.py:35
  33.5 5.4 %collective-permute-start.7 = (f32[12,8,128]{2,1,0:T(8,128)S(1)}, f32[12,8,128]{2,1,0:T(8,128)S(1)}, u32[]{:S(2)}, u32[]{:S(2)}) collective-permute-start(f32[12,8,128]{2,1,0:T(8,128)S(1)} %pad_maximum_fusion.3), channel_id=1, source_target_pairs={{0,2},{1,3},{2,0},{3,1},{4,6},{5,7},{6,4},{7,5},{8,10},{9,11},{10,... | collective-permute-start | bytes 147464 | tf_op jit(solution)/shard_map/ppermute | solution.py:35
  40.6 3.5 %collective-permute-start.10 = (f32[48,128]{1,0:T(8,128)S(1)}, f32[48,128]{1,0:T(8,128)S(1)}, u32[]{:S(2)}, u32[]{:S(2)}) collective-permute-start(f32[48,128]{1,0:T(8,128)S(1)} %gram.1), channel_id=1, source_target_pairs={{0,12},{1,13},{2,14},{3,15},{4,8},{5,9},{6,10},{7,11},{8,4},{9,5},... | collective-permute-start | bytes 73736 | tf_op jit(solution)/shard_map/ppermute | solution.py:35
  44.1 1.2 %collective-permute-start.11 = (f32[48,128]{1,0:T(8,128)S(1)}, f32[48,128]{1,0:T(8,128)S(1)}, u32[]{:S(2)}, u32[]{:S(2)}) collective-permute-start(f32[48,128]{1,0:T(8,128)S(1)} %add.27.one_ref), channel_id=1, source_target_pairs={{0,4},{1,5},{2,6},{3,7},{4,0},{5,1},{6,2},{7,3},{8,12},{9,13},{10,... | collective-permute-start | bytes 73736 | tf_op jit(solution)/shard_map/ppermute | solution.py:35

commit v4 on v3

--- a/solution.py
+++ b/solution.py
@@ -72,29 +72,46 @@
             chunks.append((side, start, size, copies))
 
     def multiply(*sums):
+        pair = len(sums) // 2
         count = 0
         for side, start, size, copies in chunks:
             _, _, buf, _, held = sides[side]
             for copy in copies:
                 copy.wait()
-            for col in range(start, start + size, tile):
-                unit, turn = count % len(sums), count // len(sums)
+            for col in range(start, start + size, tile * pair):
+                unit, turn = count % 2, count // 2
                 count += 1
-                weight = [held[:, col : col + tile]]
+                cols = [c for c in range(col, col + tile * pair, tile) if c < start + size]
+                weight = [held[:, c : c + tile] for c in cols]
                 if side:
-                    weight.insert(0, jnp.zeros((side * rank, tile), held.dtype))
-                weight.append(jnp.zeros((tile - (side + 1) * rank, tile), held.dtype))
+                    weight.insert(0, jnp.zeros((pair * side * rank, tile), held.dtype))
+                filled = sum(part.shape[0] for part in weight)
+                if filled < tile:
+                    weight.append(jnp.zeros((tile - filled, tile), held.dtype))
                 weight = jnp.concatenate(weight, axis=0)
                 pltpu.matmul_push_rhs(weight, turn % 2, unit, transpose=True)
-                pltpu.matmul_acc_lhs(sums[unit], buf[:, col : col + tile], load_staged_rhs=turn % 2)
-        total = pltpu.matmul_pop(sums[0])[:, : 2 * rank]
-        for unit in sums[1:]:
-            total = total + pltpu.matmul_pop(unit)[:, : 2 * rank]
+                for index, c in enumerate(cols):
+                    load = {} if index else {"load_staged_rhs": turn % 2}
+                    pltpu.matmul_acc_lhs(sums[unit * pair + index], buf[:, c : c + tile], **load)
+        totals = [
+            pltpu.matmul_pop(sums[index]) + pltpu.matmul_pop(sums[pair + index])
+            for index in range(pair)
+        ]
+        parts_of = []
+        for side in range(2):
+            value = None
+            for index, total in enumerate(totals):
+                at_col = (pair * side + index) * rank
+                piece = total[:, at_col : at_col + rank]
+                value = piece if value is None else value + piece
+            parts_of.append(value)
+        value = jnp.concatenate(parts_of, axis=1)
         for slot, ref in enumerate(out_refs):
-            ref[...] = total[slot * rows : (slot + 1) * rows]
+            ref[...] = value[slot * rows : (slot + 1) * rows]
 
     with jax.sharding.use_abstract_mesh(mesh.abstract_mesh):
-        sums = [pltpu.ACC(unit)((hid.shape[0], tile), F32) for unit in range(2)]
+        pair = 2 if 2 * hid.shape[0] <= 1024 else 1
+        sums = [pltpu.ACC(unit)((hid.shape[0], tile), F32) for unit in range(2) for _ in range(pair)]
         pl.run_scoped(multiply, *sums)
 
 

time: 46.8 us -> 47 us (level)
  Pallas kernels: 11.5 us -> 12 us
  transfers between devices with their start and end apart: 12 -> 12, of which waited for: 8 -> 8; matrix products, arithmetic and copies ran while one was open for 0% -> 0% of each run, Pallas kernels for 14% -> 15%
where the time goes in v4:
time: 47 us; the launch traced here: 46.8 us
  waiting for transfers between devices  20.4 us (43%)
  starting transfers between devices  14.2 us (30%)
  Pallas kernels  12 us (26%)
    ppermute x12, waiting for transfers between devices, swap(): lax.ppermute(value, ('dp', 'tensor'), [(i, i ^ flip) for i in range(group...  20.4 us
    ppermute x12, starting transfers between devices, swap(): lax.ppermute(value, ('dp', 'tensor'), [(i, i ^ flip) for i in range(group...  14.2 us
    pallas_call x3, Pallas kernels, project(): call(functools.partial(project_kernel, mesh, parts, hops, tile), [jax.Sha...  9.78 us
    pallas_call x1, Pallas kernels, per_device(): call(functools.partial(solve_kernel, ntrain, rank * rank, share), jax.Sha...  1.29 us
  transfers between devices with their start and end apart: 12, of which 8 were waited for; matrix products, arithmetic and copies ran while one was open for 0% of the time, Pallas kernels for 15%

profile of v4, /device:TPU:0, one launch (start us, length us, event | category | flops | bytes accessed | tf_op | source)
XLA Modules:
  0.0 46.8 jit_solution(3643469391808028102)
XLA Ops:
  0.0 2.9 %project_3.1 = f32[320,128]{1,0:T(8,128)S(1)} custom-call(s32[1]{0:T(128)} %bitcast.1.at_ref, bf16[1024,3584]{1,0:T(8,128)(2,1)} %bitcast.16, bf16[1024,1024]{1,0:T(8,128)(2,1)} %bitcast.19, bf16[256,3584]{1,0:T(8,128)(2,1)} %bitcast.22, bf16[256,1024]{1,0:T(8,128)(2,1)} %bitcast.25, bf16[64,3584]{1,0:T(8,128)(2,1)} %bitcast.28, bf16[64,1024]{1,0:T(8,128)(2,1)} %bitcast.31), custom_call_target="tpu_custom_call" | custom-call | flops 188743680 | bytes 3538944 | tf_op jit(solution)/shard_map/project_3/pallas_call | solution.py:126
  2.9 5.1 %collective-permute-start = (f32[320,128]{1,0:T(8,128)S(1)}, f32[320,128]{1,0:T(8,128)S(1)}, u32[]{:S(2)}, u32[]{:S(2)}) collective-permute-start(f32[320,128]{1,0:T(8,128)S(1)} %project_3.1), channel_id=1, source_target_pairs={{0,3},{1,2},{2,1},{3,0},{4,7},{5,6},{6,5},{7,4},{8,11},{9,10},{10,... | collective-permute-start | bytes 491528 | tf_op jit(solution)/shard_map/ppermute | solution.py:35
  8.0 3.9 %project_2_1.1 = (f32[320,128]{1,0:T(8,128)S(1)}, f32[320,128]{1,0:T(8,128)S(1)}) custom-call(s32[1]{0:T(128)} %bitcast.1.at_ref, bf16[1024,3584]{1,0:T(8,128)(2,1)} %bitcast.17, bf16[1024,1024]{1,0:T(8,128)(2,1)} %bitcast.20, bf16[256,3584]{1,0:T(8,128)(2,1)} %bitcast.23, bf16[256,1024]{1,0:T(8,128)(2,1)} %bitcast.26, bf16[64,3584]{1,0:T(8,128)(2,1)} %bitcast.29, ...), custom_call_target="tpu_custom_call" | custom-call | flops 377487360 | bytes 6488064 | tf_op jit(solution)/shard_map/project_2_1/pallas_call | solution.py:126
  12.0 0.1 collective-permute-start.1
  12.0 0.6 %collective-permute-start.2 = (f32[320,128]{1,0:T(8,128)S(1)}, f32[320,128]{1,0:T(8,128)S(1)}, u32[]{:S(2)}, u32[]{:S(2)}) collective-permute-start(f32[320,128]{1,0:T(8,128)S(1)} %get-tuple-element.23), channel_id=1, source_target_pairs={{0,1},{1,0},{2,3},{3,2},{4,5},{5,4},{6,7},{7,6},{8,9},{9,8},{10,11... | collective-permute-start | bytes 491528 | tf_op jit(solution)/shard_map/ppermute | solution.py:35
  12.6 0.0 copy-start
  12.6 0.0 copy-start.1
  12.6 2.9 %project_0.1 = f32[320,128]{1,0:T(8,128)S(1)} custom-call(s32[1]{0:T(128)} %bitcast.1.at_ref, bf16[1024,3584]{1,0:T(8,128)(2,1)} %bitcast.18, bf16[1024,1024]{1,0:T(8,128)(2,1)} %bitcast.21, bf16[256,3584]{1,0:T(8,128)(2,1)} %bitcast.24, bf16[256,1024]{1,0:T(8,128)(2,1)} %bitcast.27, bf16[64,3584]{1,0:T(8,128)(2,1)} %bitcast.30, bf16[64,1024]{1,0:T(8,128)(2,1)} %bitcast.33), custom_call_target="tpu_custom_call" | custom-call | flops 188743680 | bytes 3538944 | tf_op jit(solution)/shard_map/project_0/pallas_call | solution.py:126
  15.6 0.0 collective-permute-done
  15.6 6.3 %collective-permute-done.1.refs_1_ = f32[320,128]{1,0:T(8,128)S(1)} collective-permute-done((f32[320,128]{1,0:T(8,128)S(1)}, f32[320,128]{1,0:T(8,128)S(1)}, u32[]{:S(2)}, u32[]{:S(2)}) %collective-permute-start.1) | collective-permute-done | bytes 163872 | tf_op jit(solution)/shard_map/ppermute | solution.py:35
  21.9 0.0 collective-permute-done.2.refs_2_
  21.9 0.0 copy-done
  21.9 0.0 copy-done.1
  21.9 0.4 outer.1
  22.4 0.1 collective-permute-start.3
  22.5 1.2 %collective-permute-done.3 = f32[2,7,8,128]{3,2,1,0:T(8,128)S(1)} collective-permute-done((f32[2,7,8,128]{3,2,1,0:T(8,128)S(1)}, f32[2,7,8,128]{3,2,1,0:T(8,128)S(1)}, u32[]{:S(2)}, u32[]{:S(2)}) %collective-permute-start.3) | collective-permute-done | bytes 57376 | tf_op jit(solution)/shard_map/ppermute | solution.py:35
  23.7 1.3 %collective-permute-start.4 = (f32[9,8,128]{2,1,0:T(8,128)S(1)}, f32[9,8,128]{2,1,0:T(8,128)S(1)}, u32[]{:S(2)}, u32[]{:S(2)}) collective-permute-start(f32[9,8,128]{2,1,0:T(8,128)S(1)} %get-tuple-element.32), channel_id=1, source_target_pairs={{0,12},{1,13},{2,14},{3,15},{4,8},{5,9},{6,10},{7,11},{8,4},{9,5},... | collective-permute-start | bytes 110600 | tf_op jit(solution)/shard_map/ppermute | solution.py:35
  25.1 2.2 %collective-permute-done.4 = f32[9,8,128]{2,1,0:T(8,128)S(1)} collective-permute-done((f32[9,8,128]{2,1,0:T(8,128)S(1)}, f32[9,8,128]{2,1,0:T(8,128)S(1)}, u32[]{:S(2)}, u32[]{:S(2)}) %collective-permute-start.4) | collective-permute-done | bytes 36896 | tf_op jit(solution)/shard_map/ppermute | solution.py:35
  27.3 1.4 %collective-permute-start.5 = (f32[13,8,128]{2,1,0:T(8,128)S(1)}, f32[13,8,128]{2,1,0:T(8,128)S(1)}, u32[]{:S(2)}, u32[]{:S(2)}) collective-permute-start(f32[13,8,128]{2,1,0:T(8,128)S(1)} %pad_maximum_fusion.2), channel_id=1, source_target_pairs={{0,20},{1,21},{2,22},{3,23},{4,16},{5,17},{6,18},{7,19},{8,28},{9,... | collective-permute-start | bytes 159752 | tf_op jit(solution)/shard_map/ppermute | solution.py:35
  28.6 0.0 collective-permute-start.6
  28.6 2.5 %collective-permute-done.5 = f32[13,8,128]{2,1,0:T(8,128)S(1)} collective-permute-done((f32[13,8,128]{2,1,0:T(8,128)S(1)}, f32[13,8,128]{2,1,0:T(8,128)S(1)}, u32[]{:S(2)}, u32[]{:S(2)}) %collective-permute-start.5) | collective-permute-done | bytes 53280 | tf_op jit(solution)/shard_map/ppermute | solution.py:35
  31.2 2.5 %collective-permute-start.8 = (f32[20,8,128]{2,1,0:T(8,128)S(1)}, f32[20,8,128]{2,1,0:T(8,128)S(1)}, u32[]{:S(2)}, u32[]{:S(2)}) collective-permute-start(f32[20,8,128]{2,1,0:T(8,128)S(1)} %pad_maximum_fusion.refs_0_), channel_id=1, source_target_pairs={{0,3},{1,2},{2,1},{3,0},{4,7},{5,6},{6,5},{7,4},{8,11},{9,10},{10,... | collective-permute-start | bytes 245768 | tf_op jit(solution)/shard_map/ppermute | solution.py:35
  33.7 0.0 collective-permute-start.9
  33.7 0.0 collective-permute-done.6.refs_1_
  33.7 2.0 %collective-permute-start.7 = (f32[12,8,128]{2,1,0:T(8,128)S(1)}, f32[12,8,128]{2,1,0:T(8,128)S(1)}, u32[]{:S(2)}, u32[]{:S(2)}) collective-permute-start(f32[12,8,128]{2,1,0:T(8,128)S(1)} %pad_maximum_fusion.3), channel_id=1, source_target_pairs={{0,2},{1,3},{2,0},{3,1},{4,6},{5,7},{6,4},{7,5},{8,10},{9,11},{10,... | collective-permute-start | bytes 147464 | tf_op jit(solution)/shard_map/ppermute | solution.py:35
  35.7 3.4 %collective-permute-done.7.refs_2_ = f32[12,8,128]{2,1,0:T(8,128)S(1)} collective-permute-done((f32[12,8,128]{2,1,0:T(8,128)S(1)}, f32[12,8,128]{2,1,0:T(8,128)S(1)}, u32[]{:S(2)}, u32[]{:S(2)}) %collective-permute-start.7) | collective-permute-done | bytes 49184 | tf_op jit(solution)/shard_map/ppermute | solution.py:35
  39.1 0.0 collective-permute-done.8.refs_3_
  39.1 1.2 %collective-permute-done.9.refs_4_ = f32[20,8,128]{2,1,0:T(8,128)S(1)} collective-permute-done((f32[20,8,128]{2,1,0:T(8,128)S(1)}, f32[20,8,128]{2,1,0:T(8,128)S(1)}, u32[]{:S(2)}, u32[]{:S(2)}) %collective-permute-start.9) | collective-permute-done | bytes 81952 | tf_op jit(solution)/shard_map/ppermute | solution.py:35
  40.4 0.5 %gram.1 = f32[48,128]{1,0:T(8,128)S(1)} custom-call(s32[1]{0:T(128)} %bitcast.1.at_ref, f32[20,8,128]{2,1,0:T(8,128)S(1)} %pad_maximum_fusion.refs_0_, f32[8,8,128]{2,1,0:T(8,128)S(1)} %collective-permute-done.6.refs_1_, f32[12,8,128]{2,1,0:T(8,128)S(1)} %collective-permute-done.7.refs_2_, f32[20,8,128]{2,1,0:T(8,128)S(1)} %collective-permute-done.8.refs_3_, ...), custom_call_target="tpu_custom_call" | custom-call | tf_op jit(solution)/shard_map/gram/pallas_call | solution.py:393
  40.8 1.0 %collective-permute-start.10 = (f32[48,128]{1,0:T(8,128)S(1)}, f32[48,128]{1,0:T(8,128)S(1)}, u32[]{:S(2)}, u32[]{:S(2)}) collective-permute-start(f32[48,128]{1,0:T(8,128)S(1)} %gram.1), channel_id=1, source_target_pairs={{0,12},{1,13},{2,14},{3,15},{4,8},{5,9},{6,10},{7,11},{8,4},{9,5},... | collective-permute-start | bytes 73736 | tf_op jit(solution)/shard_map/ppermute | solution.py:35
  41.9 2.5 %collective-permute-done.10 = f32[48,128]{1,0:T(8,128)S(1)} collective-permute-done((f32[48,128]{1,0:T(8,128)S(1)}, f32[48,128]{1,0:T(8,128)S(1)}, u32[]{:S(2)}, u32[]{:S(2)}) %collective-permute-start.10) | collective-permute-done | bytes 24608 | tf_op jit(solution)/shard_map/ppermute | solution.py:35
  44.4 0.1 collective-permute-start.11
  44.5 1.1 %collective-permute-done.11.two_ref = f32[48,128]{1,0:T(8,128)S(1)} collective-permute-done((f32[48,128]{1,0:T(8,128)S(1)}, f32[48,128]{1,0:T(8,128)S(1)}, u32[]{:S(2)}, u32[]{:S(2)}) %collective-permute-start.11) | collective-permute-done | bytes 24608 | tf_op jit(solution)/shard_map/ppermute | solution.py:35
  45.6 1.3 %solve.1 = f32[2,16]{1,0:T(2,128)} custom-call(s32[1]{0:T(128)} %bitcast.low_ref, f32[48,128]{1,0:T(8,128)S(1)} %add.27.one_ref, f32[48,128]{1,0:T(8,128)S(1)} %collective-permute-done.11.two_ref), custom_call_target="tpu_custom_call" | custom-call | tf_op jit(solution)/shard_map/solve/pallas_call | solution.py:401
  (16 shorter events, 0.1 us)
Async XLA Ops:
  2.9 12.6 %collective-permute-start = (f32[320,128]{1,0:T(8,128)S(1)}, f32[320,128]{1,0:T(8,128)S(1)}, u32[]{:S(2)}, u32[]{:S(2)}) collective-permute-start(f32[320,128]{1,0:T(8,128)S(1)} %project_3.1), channel_id=1, source_target_pairs={{0,3},{1,2},{2,1},{3,0},{4,7},{5,6},{6,5},{7,4},{8,11},{9,10},{10,... | collective-permute-start | bytes 491528 | tf_op jit(solution)/shard_map/ppermute | solution.py:35
  12.0 10.0 %collective-permute-start.1 = (f32[320,128]{1,0:T(8,128)S(1)}, f32[320,128]{1,0:T(8,128)S(1)}, u32[]{:S(2)}, u32[]{:S(2)}) collective-permute-start(f32[320,128]{1,0:T(8,128)S(1)} %get-tuple-element.22), channel_id=1, source_target_pairs={{0,2},{1,3},{2,0},{3,1},{4,6},{5,7},{6,4},{7,5},{8,10},{9,11},{10,... | collective-permute-start | bytes 491528 | tf_op jit(solution)/shard_map/ppermute | solution.py:35
  12.0 9.9 %collective-permute-start.2 = (f32[320,128]{1,0:T(8,128)S(1)}, f32[320,128]{1,0:T(8,128)S(1)}, u32[]{:S(2)}, u32[]{:S(2)}) collective-permute-start(f32[320,128]{1,0:T(8,128)S(1)} %get-tuple-element.23), channel_id=1, source_target_pairs={{0,1},{1,0},{2,3},{3,2},{4,5},{5,4},{6,7},{7,6},{8,9},{9,8},{10,11... | collective-permute-start | bytes 491528 | tf_op jit(solution)/shard_map/ppermute | solution.py:35
  12.6 9.3 %copy-start = (s32[16,16]{1,0:T(8,128)S(1)}, s32[16,16]{1,0:T(8,128)}, u32[]{:S(2)}) copy-start(s32[16,16]{1,0:T(8,128)} %qids_ref.1) | copy-start | bytes 3076
  12.6 9.3 %copy-start.1 = (s32[8,128]{1,0:T(8,128)S(1)}, s32[8,128]{1,0:T(8,128)}, u32[]{:S(2)}) copy-start(s32[8,128]{1,0:T(8,128)} %ids_ref.1) | copy-start | bytes 12292
  22.4 1.3 %collective-permute-start.3 = (f32[2,7,8,128]{3,2,1,0:T(8,128)S(1)}, f32[2,7,8,128]{3,2,1,0:T(8,128)S(1)}, u32[]{:S(2)}, u32[]{:S(2)}) collective-permute-start(f32[2,7,8,128]{3,2,1,0:T(8,128)S(1)} %get-tuple-element.25), channel_id=1, source_target_pairs={{0,4},{1,5},{2,6},{3,7},{4,0},{5,1},{6,2},{7,3},{8,12},{9,13},{10,... | collective-permute-start | bytes 172040 | tf_op jit(solution)/shard_map/ppermute | solution.py:35
  23.7 3.5 %collective-permute-start.4 = (f32[9,8,128]{2,1,0:T(8,128)S(1)}, f32[9,8,128]{2,1,0:T(8,128)S(1)}, u32[]{:S(2)}, u32[]{:S(2)}) collective-permute-start(f32[9,8,128]{2,1,0:T(8,128)S(1)} %get-tuple-element.32), channel_id=1, source_target_pairs={{0,12},{1,13},{2,14},{3,15},{4,8},{5,9},{6,10},{7,11},{8,4},{9,5},... | collective-permute-start | bytes 110600 | tf_op jit(solution)/shard_map/ppermute | solution.py:35
  27.3 3.9 %collective-permute-start.5 = (f32[13,8,128]{2,1,0:T(8,128)S(1)}, f32[13,8,128]{2,1,0:T(8,128)S(1)}, u32[]{:S(2)}, u32[]{:S(2)}) collective-permute-start(f32[13,8,128]{2,1,0:T(8,128)S(1)} %pad_maximum_fusion.2), channel_id=1, source_target_pairs={{0,20},{1,21},{2,22},{3,23},{4,16},{5,17},{6,18},{7,19},{8,28},{9,... | collective-permute-start | bytes 159752 | tf_op jit(solution)/shard_map/ppermute | solution.py:35
  28.6 5.1 %collective-permute-start.6 = (f32[8,8,128]{2,1,0:T(8,128)S(1)}, f32[8,8,128]{2,1,0:T(8,128)S(1)}, u32[]{:S(2)}, u32[]{:S(2)}) collective-permute-start(f32[8,8,128]{2,1,0:T(8,128)S(1)} %pad_maximum_fusion.4), channel_id=1, source_target_pairs={{0,2},{1,3},{2,0},{3,1},{4,6},{5,7},{6,4},{7,5},{8,10},{9,11},{10,... | collective-permute-start | bytes 98312 | tf_op jit(solution)/shard_map/ppermute | solution.py:35
  31.2 7.9 %collective-permute-start.8 = (f32[20,8,128]{2,1,0:T(8,128)S(1)}, f32[20,8,128]{2,1,0:T(8,128)S(1)}, u32[]{:S(2)}, u32[]{:S(2)}) collective-permute-start(f32[20,8,128]{2,1,0:T(8,128)S(1)} %pad_maximum_fusion.refs_0_), channel_id=1, source_target_pairs={{0,3},{1,2},{2,1},{3,0},{4,7},{5,6},{6,5},{7,4},{8,11},{9,10},{10,... | collective-permute-start | bytes 245768 | tf_op jit(solution)/shard_map/ppermute | solution.py:35
  33.7 6.6 %collective-permute-start.9 = (f32[20,8,128]{2,1,0:T(8,128)S(1)}, f32[20,8,128]{2,1,0:T(8,128)S(1)}, u32[]{:S(2)}, u32[]{:S(2)}) collective-permute-start(f32[20,8,128]{2,1,0:T(8,128)S(1)} %pad_maximum_fusion.refs_0_), channel_id=1, source_target_pairs={{0,1},{1,0},{2,3},{3,2},{4,5},{5,4},{6,7},{7,6},{8,9},{9,8},{10,11... | collective-permute-start | bytes 245768 | tf_op jit(solution)/shard_map/ppermute | solution.py:35
  33.7 5.4 %collective-permute-start.7 = (f32[12,8,128]{2,1,0:T(8,128)S(1)}, f32[12,8,128]{2,1,0:T(8,128)S(1)}, u32[]{:S(2)}, u32[]{:S(2)}) collective-permute-start(f32[12,8,128]{2,1,0:T(8,128)S(1)} %pad_maximum_fusion.3), channel_id=1, source_target_pairs={{0,2},{1,3},{2,0},{3,1},{4,6},{5,7},{6,4},{7,5},{8,10},{9,11},{10,... | collective-permute-start | bytes 147464 | tf_op jit(solution)/shard_map/ppermute | solution.py:35
  40.8 3.5 %collective-permute-start.10 = (f32[48,128]{1,0:T(8,128)S(1)}, f32[48,128]{1,0:T(8,128)S(1)}, u32[]{:S(2)}, u32[]{:S(2)}) collective-permute-start(f32[48,128]{1,0:T(8,128)S(1)} %gram.1), channel_id=1, source_target_pairs={{0,12},{1,13},{2,14},{3,15},{4,8},{5,9},{6,10},{7,11},{8,4},{9,5},... | collective-permute-start | bytes 73736 | tf_op jit(solution)/shard_map/ppermute | solution.py:35
  44.4 1.2 %collective-permute-start.11 = (f32[48,128]{1,0:T(8,128)S(1)}, f32[48,128]{1,0:T(8,128)S(1)}, u32[]{:S(2)}, u32[]{:S(2)}) collective-permute-start(f32[48,128]{1,0:T(8,128)S(1)} %add.27.one_ref), channel_id=1, source_target_pairs={{0,4},{1,5},{2,6},{3,7},{4,0},{5,1},{6,2},{7,3},{8,12},{9,13},{10,... | collective-permute-start | bytes 73736 | tf_op jit(solution)/shard_map/ppermute | solution.py:35

commit v5 on v3

--- a/solution.py
+++ b/solution.py
@@ -362,15 +362,18 @@
     nex = block.shape[0] - qshare - 1
     own = block[:nex]
     other = swap(block, flip | 1, 0)
-    early = swap(own, 0, 2)
+    ahead = {hop: swap(own, 0, hop) for hop in (2, 1)}
     rest = (block + other)[nex:]
     after = jnp.concatenate([other[:nex], rest[:qshare] / rest[qshare, :qshare, None, :]], axis=0)
     whole = jnp.concatenate([own, after], axis=0)
+
     far = swap(whole, 0, 3)
-    late = swap(lax.optimization_barrier((after, early))[0], 0, 2)
-    near = swap(whole, 0, 1)
-    blocks = [whole, early, late, far, near]
-    hops = ((0, (0,)), (2, (1, 2)), (3, (3,)), (1, (4,)))
+    behind = {
+        2: swap(lax.optimization_barrier((after, ahead[2], ahead[1]))[0], 0, 2),
+        1: swap(after, 0, 1),
+    }
+    blocks = [whole, ahead[1], behind[1], far, ahead[2], behind[2]]
+    hops = ((0, (0,)), (1, (1, 2)), (3, (3,)), (2, (4, 5)))
     size = ntrain + nquery
     shape = (ntrain // 2 + nquery, 2 * ntrain) if folds(ntrain) else (size, size)
     gram = call(

time: 46.8 us -> 46.3 us (0.989)
  waiting for transfers between devices: 20.6 us -> 16.8 us
  starting transfers between devices: 14.2 us -> 17.6 us
    ppermute x12 -> x13, waiting for transfers between devices: 20.6 us -> 16.8 us  [swap(): lax.ppermute(value, ('dp', 'tensor'), [(i, i ^ flip) for i in range(group...]
    ppermute x12 -> x13, starting transfers between devices: 14.2 us -> 17.6 us  [swap(): lax.ppermute(value, ('dp', 'tensor'), [(i, i ^ flip) for i in range(group...]
  transfers between devices with their start and end apart: 12 -> 13, of which waited for: 8 -> 6; matrix products, arithmetic and copies ran while one was open for 0% -> 0% of each run, Pallas kernels for 14% -> 14%
where the time goes in v5:
time: 46.3 us; the launch traced here: 46.2 us
  starting transfers between devices  17.6 us (38%)
  waiting for transfers between devices  16.8 us (36%)
  Pallas kernels  11.5 us (25%)
    ppermute x13, starting transfers between devices, swap(): lax.ppermute(value, ('dp', 'tensor'), [(i, i ^ flip) for i in range(group...  17.6 us
    ppermute x13, waiting for transfers between devices, swap(): lax.ppermute(value, ('dp', 'tensor'), [(i, i ^ flip) for i in range(group...  16.8 us
    pallas_call x3, Pallas kernels, project(): call(functools.partial(project_kernel, mesh, parts, hops, tile), [jax.Sha...  9.32 us
    pallas_call x1, Pallas kernels, per_device(): call(functools.partial(solve_kernel, ntrain, rank * rank, share), jax.Sha...  1.29 us
  transfers between devices with their start and end apart: 13, of which 6 were waited for; matrix products, arithmetic and copies ran while one was open for 0% of the time, Pallas kernels for 14%

profile of v5, /device:TPU:0, one launch (start us, length us, event | category | flops | bytes accessed | tf_op | source)
XLA Modules:
  0.0 46.2 jit_solution(4187401724584330518)
XLA Ops:
  0.0 2.7 %project_3.1 = f32[320,128]{1,0:T(8,128)S(1)} custom-call(s32[1]{0:T(128)} %bitcast.1.at_ref, bf16[1024,3584]{1,0:T(8,128)(2,1)} %bitcast.16, bf16[1024,1024]{1,0:T(8,128)(2,1)} %bitcast.19, bf16[256,3584]{1,0:T(8,128)(2,1)} %bitcast.22, bf16[256,1024]{1,0:T(8,128)(2,1)} %bitcast.25, bf16[64,3584]{1,0:T(8,128)(2,1)} %bitcast.28, bf16[64,1024]{1,0:T(8,128)(2,1)} %bitcast.31), custom_call_target="tpu_custom_call" | custom-call | flops 188743680 | bytes 3538944 | tf_op jit(solution)/shard_map/project_3/pallas_call | solution.py:109
  2.7 5.1 %collective-permute-start = (f32[320,128]{1,0:T(8,128)S(1)}, f32[320,128]{1,0:T(8,128)S(1)}, u32[]{:S(2)}, u32[]{:S(2)}) collective-permute-start(f32[320,128]{1,0:T(8,128)S(1)} %project_3.1), channel_id=1, source_target_pairs={{0,3},{1,2},{2,1},{3,0},{4,7},{5,6},{6,5},{7,4},{8,11},{9,10},{10,... | collective-permute-start | bytes 491528 | tf_op jit(solution)/shard_map/ppermute | solution.py:35
  7.8 3.9 %project_2_1.1 = (f32[320,128]{1,0:T(8,128)S(1)}, f32[320,128]{1,0:T(8,128)S(1)}) custom-call(s32[1]{0:T(128)} %bitcast.1.at_ref, bf16[1024,3584]{1,0:T(8,128)(2,1)} %bitcast.17, bf16[1024,1024]{1,0:T(8,128)(2,1)} %bitcast.20, bf16[256,3584]{1,0:T(8,128)(2,1)} %bitcast.23, bf16[256,1024]{1,0:T(8,128)(2,1)} %bitcast.26, bf16[64,3584]{1,0:T(8,128)(2,1)} %bitcast.29, ...), custom_call_target="tpu_custom_call" | custom-call | flops 377487360 | bytes 6488064 | tf_op jit(solution)/shard_map/project_2_1/pallas_call | solution.py:109
  11.7 0.1 collective-permute-start.1
  11.8 0.6 %collective-permute-start.2 = (f32[320,128]{1,0:T(8,128)S(1)}, f32[320,128]{1,0:T(8,128)S(1)}, u32[]{:S(2)}, u32[]{:S(2)}) collective-permute-start(f32[320,128]{1,0:T(8,128)S(1)} %get-tuple-element.23), channel_id=1, source_target_pairs={{0,1},{1,0},{2,3},{3,2},{4,5},{5,4},{6,7},{7,6},{8,9},{9,8},{10,11... | collective-permute-start | bytes 491528 | tf_op jit(solution)/shard_map/ppermute | solution.py:35
  12.4 0.0 copy-start
  12.4 0.0 copy-start.1
  12.4 2.7 %project_0.1 = f32[320,128]{1,0:T(8,128)S(1)} custom-call(s32[1]{0:T(128)} %bitcast.1.at_ref, bf16[1024,3584]{1,0:T(8,128)(2,1)} %bitcast.18, bf16[1024,1024]{1,0:T(8,128)(2,1)} %bitcast.21, bf16[256,3584]{1,0:T(8,128)(2,1)} %bitcast.24, bf16[256,1024]{1,0:T(8,128)(2,1)} %bitcast.27, bf16[64,3584]{1,0:T(8,128)(2,1)} %bitcast.30, bf16[64,1024]{1,0:T(8,128)(2,1)} %bitcast.33), custom_call_target="tpu_custom_call" | custom-call | flops 188743680 | bytes 3538944 | tf_op jit(solution)/shard_map/project_0/pallas_call | solution.py:109
  15.1 0.0 collective-permute-done
  15.2 6.5 %collective-permute-done.1.refs_1_ = f32[320,128]{1,0:T(8,128)S(1)} collective-permute-done((f32[320,128]{1,0:T(8,128)S(1)}, f32[320,128]{1,0:T(8,128)S(1)}, u32[]{:S(2)}, u32[]{:S(2)}) %collective-permute-start.1) | collective-permute-done | bytes 163872 | tf_op jit(solution)/shard_map/ppermute | solution.py:35
  21.7 0.0 collective-permute-done.2.refs_2_
  21.7 0.0 copy-done
  21.7 0.0 copy-done.1
  21.7 0.4 outer.1
  22.1 0.1 collective-permute-start.3
  22.2 1.2 %collective-permute-done.3 = f32[2,7,8,128]{3,2,1,0:T(8,128)S(1)} collective-permute-done((f32[2,7,8,128]{3,2,1,0:T(8,128)S(1)}, f32[2,7,8,128]{3,2,1,0:T(8,128)S(1)}, u32[]{:S(2)}, u32[]{:S(2)}) %collective-permute-start.3) | collective-permute-done | bytes 57376 | tf_op jit(solution)/shard_map/ppermute | solution.py:35
  23.5 1.3 %collective-permute-start.4 = (f32[9,8,128]{2,1,0:T(8,128)S(1)}, f32[9,8,128]{2,1,0:T(8,128)S(1)}, u32[]{:S(2)}, u32[]{:S(2)}) collective-permute-start(f32[9,8,128]{2,1,0:T(8,128)S(1)} %get-tuple-element.32), channel_id=1, source_target_pairs={{0,12},{1,13},{2,14},{3,15},{4,8},{5,9},{6,10},{7,11},{8,4},{9,5},... | collective-permute-start | bytes 110600 | tf_op jit(solution)/shard_map/ppermute | solution.py:35
  24.8 2.2 %collective-permute-done.4 = f32[9,8,128]{2,1,0:T(8,128)S(1)} collective-permute-done((f32[9,8,128]{2,1,0:T(8,128)S(1)}, f32[9,8,128]{2,1,0:T(8,128)S(1)}, u32[]{:S(2)}, u32[]{:S(2)}) %collective-permute-start.4) | collective-permute-done | bytes 36896 | tf_op jit(solution)/shard_map/ppermute | solution.py:35
  27.0 1.3 %collective-permute-start.5 = (f32[13,8,128]{2,1,0:T(8,128)S(1)}, f32[13,8,128]{2,1,0:T(8,128)S(1)}, u32[]{:S(2)}, u32[]{:S(2)}) collective-permute-start(f32[13,8,128]{2,1,0:T(8,128)S(1)} %pad_maximum_fusion.2), channel_id=1, source_target_pairs={{0,20},{1,21},{2,22},{3,23},{4,16},{5,17},{6,18},{7,19},{8,28},{9,... | collective-permute-start | bytes 159752 | tf_op jit(solution)/shard_map/ppermute | solution.py:35
  28.4 0.0 collective-permute-start.6
  28.4 3.0 %collective-permute-start.9 = (f32[8,8,128]{2,1,0:T(8,128)S(1)}, f32[8,8,128]{2,1,0:T(8,128)S(1)}, u32[]{:S(2)}, u32[]{:S(2)}) collective-permute-start(f32[8,8,128]{2,1,0:T(8,128)S(1)} %pad_maximum_fusion.4), channel_id=1, source_target_pairs={{0,2},{1,3},{2,0},{3,1},{4,6},{5,7},{6,4},{7,5},{8,10},{9,11},{10,... | collective-permute-start | bytes 98312 | tf_op jit(solution)/shard_map/ppermute | solution.py:35
  31.4 0.0 collective-permute-done.5
  31.5 2.0 %collective-permute-start.8 = (f32[20,8,128]{2,1,0:T(8,128)S(1)}, f32[20,8,128]{2,1,0:T(8,128)S(1)}, u32[]{:S(2)}, u32[]{:S(2)}) collective-permute-start(f32[20,8,128]{2,1,0:T(8,128)S(1)} %pad_maximum_fusion.refs_0_), channel_id=1, source_target_pairs={{0,3},{1,2},{2,1},{3,0},{4,7},{5,6},{6,5},{7,4},{8,11},{9,10},{10,... | collective-permute-start | bytes 245768 | tf_op jit(solution)/shard_map/ppermute | solution.py:35
  33.5 0.0 collective-permute-start.7
  33.5 0.0 collective-permute-done.6.refs_1_
  33.5 0.0 collective-permute-done.9.refs_4_
  33.5 2.8 %collective-permute-start.10 = (f32[12,8,128]{2,1,0:T(8,128)S(1)}, f32[12,8,128]{2,1,0:T(8,128)S(1)}, u32[]{:S(2)}, u32[]{:S(2)}) collective-permute-start(f32[12,8,128]{2,1,0:T(8,128)S(1)} %pad_maximum_fusion.3), channel_id=1, source_target_pairs={{0,2},{1,3},{2,0},{3,1},{4,6},{5,7},{6,4},{7,5},{8,10},{9,11},{10,... | collective-permute-start | bytes 147464 | tf_op jit(solution)/shard_map/ppermute | solution.py:35
  36.4 3.4 %collective-permute-done.7.refs_2_ = f32[12,8,128]{2,1,0:T(8,128)S(1)} collective-permute-done((f32[12,8,128]{2,1,0:T(8,128)S(1)}, f32[12,8,128]{2,1,0:T(8,128)S(1)}, u32[]{:S(2)}, u32[]{:S(2)}) %collective-permute-start.7) | collective-permute-done | bytes 49184 | tf_op jit(solution)/shard_map/ppermute | solution.py:35
  39.7 0.0 collective-permute-done.10.refs_5_
  39.7 0.0 collective-permute-done.8.refs_3_
  39.7 0.5 %gram.1 = f32[48,128]{1,0:T(8,128)S(1)} custom-call(s32[1]{0:T(128)} %bitcast.1.at_ref, f32[20,8,128]{2,1,0:T(8,128)S(1)} %pad_maximum_fusion.refs_0_, f32[8,8,128]{2,1,0:T(8,128)S(1)} %collective-permute-done.6.refs_1_, f32[12,8,128]{2,1,0:T(8,128)S(1)} %collective-permute-done.7.refs_2_, f32[20,8,128]{2,1,0:T(8,128)S(1)} %collective-permute-done.8.refs_3_, ...), custom_call_target="tpu_custom_call" | custom-call | tf_op jit(solution)/shard_map/gram/pallas_call | solution.py:379
  40.2 1.1 %collective-permute-start.11 = (f32[48,128]{1,0:T(8,128)S(1)}, f32[48,128]{1,0:T(8,128)S(1)}, u32[]{:S(2)}, u32[]{:S(2)}) collective-permute-start(f32[48,128]{1,0:T(8,128)S(1)} %gram.1), channel_id=1, source_target_pairs={{0,12},{1,13},{2,14},{3,15},{4,8},{5,9},{6,10},{7,11},{8,4},{9,5},... | collective-permute-start | bytes 73736 | tf_op jit(solution)/shard_map/ppermute | solution.py:35
  41.3 2.5 %collective-permute-done.11 = f32[48,128]{1,0:T(8,128)S(1)} collective-permute-done((f32[48,128]{1,0:T(8,128)S(1)}, f32[48,128]{1,0:T(8,128)S(1)}, u32[]{:S(2)}, u32[]{:S(2)}) %collective-permute-start.11) | collective-permute-done | bytes 24608 | tf_op jit(solution)/shard_map/ppermute | solution.py:35
  43.7 0.1 collective-permute-start.12
  43.8 1.1 %collective-permute-done.12.two_ref = f32[48,128]{1,0:T(8,128)S(1)} collective-permute-done((f32[48,128]{1,0:T(8,128)S(1)}, f32[48,128]{1,0:T(8,128)S(1)}, u32[]{:S(2)}, u32[]{:S(2)}) %collective-permute-start.12) | collective-permute-done | bytes 24608 | tf_op jit(solution)/shard_map/ppermute | solution.py:35
  44.9 1.3 %solve.1 = f32[2,16]{1,0:T(2,128)} custom-call(s32[1]{0:T(128)} %bitcast.low_ref, f32[48,128]{1,0:T(8,128)S(1)} %add.27.one_ref, f32[48,128]{1,0:T(8,128)S(1)} %collective-permute-done.12.two_ref), custom_call_target="tpu_custom_call" | custom-call | tf_op jit(solution)/shard_map/solve/pallas_call | solution.py:387
  (16 shorter events, 0.1 us)
Async XLA Ops:
  2.7 12.4 %collective-permute-start = (f32[320,128]{1,0:T(8,128)S(1)}, f32[320,128]{1,0:T(8,128)S(1)}, u32[]{:S(2)}, u32[]{:S(2)}) collective-permute-start(f32[320,128]{1,0:T(8,128)S(1)} %project_3.1), channel_id=1, source_target_pairs={{0,3},{1,2},{2,1},{3,0},{4,7},{5,6},{6,5},{7,4},{8,11},{9,10},{10,... | collective-permute-start | bytes 491528 | tf_op jit(solution)/shard_map/ppermute | solution.py:35
  11.7 10.0 %collective-permute-start.1 = (f32[320,128]{1,0:T(8,128)S(1)}, f32[320,128]{1,0:T(8,128)S(1)}, u32[]{:S(2)}, u32[]{:S(2)}) collective-permute-start(f32[320,128]{1,0:T(8,128)S(1)} %get-tuple-element.22), channel_id=1, source_target_pairs={{0,2},{1,3},{2,0},{3,1},{4,6},{5,7},{6,4},{7,5},{8,10},{9,11},{10,... | collective-permute-start | bytes 491528 | tf_op jit(solution)/shard_map/ppermute | solution.py:35
  11.8 9.9 %collective-permute-start.2 = (f32[320,128]{1,0:T(8,128)S(1)}, f32[320,128]{1,0:T(8,128)S(1)}, u32[]{:S(2)}, u32[]{:S(2)}) collective-permute-start(f32[320,128]{1,0:T(8,128)S(1)} %get-tuple-element.23), channel_id=1, source_target_pairs={{0,1},{1,0},{2,3},{3,2},{4,5},{5,4},{6,7},{7,6},{8,9},{9,8},{10,11... | collective-permute-start | bytes 491528 | tf_op jit(solution)/shard_map/ppermute | solution.py:35
  12.4 9.3 %copy-start = (s32[16,16]{1,0:T(8,128)S(1)}, s32[16,16]{1,0:T(8,128)}, u32[]{:S(2)}) copy-start(s32[16,16]{1,0:T(8,128)} %qids_ref.1) | copy-start | bytes 3076
  12.4 9.3 %copy-start.1 = (s32[8,128]{1,0:T(8,128)S(1)}, s32[8,128]{1,0:T(8,128)}, u32[]{:S(2)}) copy-start(s32[8,128]{1,0:T(8,128)} %ids_ref.1) | copy-start | bytes 12292
  22.1 1.3 %collective-permute-start.3 = (f32[2,7,8,128]{3,2,1,0:T(8,128)S(1)}, f32[2,7,8,128]{3,2,1,0:T(8,128)S(1)}, u32[]{:S(2)}, u32[]{:S(2)}) collective-permute-start(f32[2,7,8,128]{3,2,1,0:T(8,128)S(1)} %get-tuple-element.25), channel_id=1, source_target_pairs={{0,4},{1,5},{2,6},{3,7},{4,0},{5,1},{6,2},{7,3},{8,12},{9,13},{10,... | collective-permute-start | bytes 172040 | tf_op jit(solution)/shard_map/ppermute | solution.py:35
  23.5 3.5 %collective-permute-start.4 = (f32[9,8,128]{2,1,0:T(8,128)S(1)}, f32[9,8,128]{2,1,0:T(8,128)S(1)}, u32[]{:S(2)}, u32[]{:S(2)}) collective-permute-start(f32[9,8,128]{2,1,0:T(8,128)S(1)} %get-tuple-element.32), channel_id=1, source_target_pairs={{0,12},{1,13},{2,14},{3,15},{4,8},{5,9},{6,10},{7,11},{8,4},{9,5},... | collective-permute-start | bytes 110600 | tf_op jit(solution)/shard_map/ppermute | solution.py:35
  27.0 4.4 %collective-permute-start.5 = (f32[13,8,128]{2,1,0:T(8,128)S(1)}, f32[13,8,128]{2,1,0:T(8,128)S(1)}, u32[]{:S(2)}, u32[]{:S(2)}) collective-permute-start(f32[13,8,128]{2,1,0:T(8,128)S(1)} %pad_maximum_fusion.2), channel_id=1, source_target_pairs={{0,20},{1,21},{2,22},{3,23},{4,16},{5,17},{6,18},{7,19},{8,28},{9,... | collective-permute-start | bytes 159752 | tf_op jit(solution)/shard_map/ppermute | solution.py:35
  28.4 5.1 %collective-permute-start.6 = (f32[8,8,128]{2,1,0:T(8,128)S(1)}, f32[8,8,128]{2,1,0:T(8,128)S(1)}, u32[]{:S(2)}, u32[]{:S(2)}) collective-permute-start(f32[8,8,128]{2,1,0:T(8,128)S(1)} %pad_maximum_fusion.4), channel_id=1, source_target_pairs={{0,1},{1,0},{2,3},{3,2},{4,5},{5,4},{6,7},{7,6},{8,9},{9,8},{10,11... | collective-permute-start | bytes 98312 | tf_op jit(solution)/shard_map/ppermute | solution.py:35
  28.4 5.1 %collective-permute-start.9 = (f32[8,8,128]{2,1,0:T(8,128)S(1)}, f32[8,8,128]{2,1,0:T(8,128)S(1)}, u32[]{:S(2)}, u32[]{:S(2)}) collective-permute-start(f32[8,8,128]{2,1,0:T(8,128)S(1)} %pad_maximum_fusion.4), channel_id=1, source_target_pairs={{0,2},{1,3},{2,0},{3,1},{4,6},{5,7},{6,4},{7,5},{8,10},{9,11},{10,... | collective-permute-start | bytes 98312 | tf_op jit(solution)/shard_map/ppermute | solution.py:35
  31.5 8.2 %collective-permute-start.8 = (f32[20,8,128]{2,1,0:T(8,128)S(1)}, f32[20,8,128]{2,1,0:T(8,128)S(1)}, u32[]{:S(2)}, u32[]{:S(2)}) collective-permute-start(f32[20,8,128]{2,1,0:T(8,128)S(1)} %pad_maximum_fusion.refs_0_), channel_id=1, source_target_pairs={{0,3},{1,2},{2,1},{3,0},{4,7},{5,6},{6,5},{7,4},{8,11},{9,10},{10,... | collective-permute-start | bytes 245768 | tf_op jit(solution)/shard_map/ppermute | solution.py:35
  33.5 6.2 %collective-permute-start.7 = (f32[12,8,128]{2,1,0:T(8,128)S(1)}, f32[12,8,128]{2,1,0:T(8,128)S(1)}, u32[]{:S(2)}, u32[]{:S(2)}) collective-permute-start(f32[12,8,128]{2,1,0:T(8,128)S(1)} %pad_maximum_fusion.3), channel_id=1, source_target_pairs={{0,1},{1,0},{2,3},{3,2},{4,5},{5,4},{6,7},{7,6},{8,9},{9,8},{10,11... | collective-permute-start | bytes 147464 | tf_op jit(solution)/shard_map/ppermute | solution.py:35
  33.5 6.2 %collective-permute-start.10 = (f32[12,8,128]{2,1,0:T(8,128)S(1)}, f32[12,8,128]{2,1,0:T(8,128)S(1)}, u32[]{:S(2)}, u32[]{:S(2)}) collective-permute-start(f32[12,8,128]{2,1,0:T(8,128)S(1)} %pad_maximum_fusion.3), channel_id=1, source_target_pairs={{0,2},{1,3},{2,0},{3,1},{4,6},{5,7},{6,4},{7,5},{8,10},{9,11},{10,... | collective-permute-start | bytes 147464 | tf_op jit(solution)/shard_map/ppermute | solution.py:35
  40.2 3.5 %collective-permute-start.11 = (f32[48,128]{1,0:T(8,128)S(1)}, f32[48,128]{1,0:T(8,128)S(1)}, u32[]{:S(2)}, u32[]{:S(2)}) collective-permute-start(f32[48,128]{1,0:T(8,128)S(1)} %gram.1), channel_id=1, source_target_pairs={{0,12},{1,13},{2,14},{3,15},{4,8},{5,9},{6,10},{7,11},{8,4},{9,5},... | collective-permute-start | bytes 73736 | tf_op jit(solution)/shard_map/ppermute | solution.py:35
  43.7 1.2 %collective-permute-start.12 = (f32[48,128]{1,0:T(8,128)S(1)}, f32[48,128]{1,0:T(8,128)S(1)}, u32[]{:S(2)}, u32[]{:S(2)}) collective-permute-start(f32[48,128]{1,0:T(8,128)S(1)} %add.27.one_ref), channel_id=1, source_target_pairs={{0,4},{1,5},{2,6},{3,7},{4,0},{5,1},{6,2},{7,3},{8,12},{9,13},{10,... | collective-permute-start | bytes 73736 | tf_op jit(solution)/shard_map/ppermute | solution.py:35

commit v6 on v5

--- a/solution.py
+++ b/solution.py
@@ -73,28 +73,29 @@
 
     def multiply(*sums):
         count = 0
+        half = hid.shape[0] // 2
         for side, start, size, copies in chunks:
             _, _, buf, _, held = sides[side]
             for copy in copies:
                 copy.wait()
             for col in range(start, start + size, tile):
-                unit, turn = count % len(sums), count // len(sums)
+                turn = count % 2
                 count += 1
                 weight = [held[:, col : col + tile]]
                 if side:
                     weight.insert(0, jnp.zeros((side * rank, tile), held.dtype))
                 weight.append(jnp.zeros((tile - (side + 1) * rank, tile), held.dtype))
                 weight = jnp.concatenate(weight, axis=0)
-                pltpu.matmul_push_rhs(weight, turn % 2, unit, transpose=True)
-                pltpu.matmul_acc_lhs(sums[unit], buf[:, col : col + tile], load_staged_rhs=turn % 2)
-        total = pltpu.matmul_pop(sums[0])[:, : 2 * rank]
-        for unit in sums[1:]:
-            total = total + pltpu.matmul_pop(unit)[:, : 2 * rank]
+                for unit, acc in enumerate(sums):
+                    pltpu.matmul_push_rhs(weight, turn, unit, transpose=True)
+                    tokens = buf[unit * half : (unit + 1) * half, col : col + tile]
+                    pltpu.matmul_acc_lhs(acc, tokens, load_staged_rhs=turn)
+        total = jnp.concatenate([pltpu.matmul_pop(acc)[:, : 2 * rank] for acc in sums], axis=0)
         for slot, ref in enumerate(out_refs):
             ref[...] = total[slot * rows : (slot + 1) * rows]
 
     with jax.sharding.use_abstract_mesh(mesh.abstract_mesh):
-        sums = [pltpu.ACC(unit)((hid.shape[0], tile), F32) for unit in range(2)]
+        sums = [pltpu.ACC(unit)((hid.shape[0] // 2, tile), F32) for unit in range(2)]
         pl.run_scoped(multiply, *sums)
 
 
@@ -190,32 +191,35 @@
         send_ref[flip] = scratch[mine ^ 2 ^ flip]
 
 
-def gram_kernel(qshare, hops, at_ref, *refs):
-    piece_refs, (out_ref, scratch) = refs[:-2], refs[-2:]
-    at = at_ref[0]
-    _, half, lanes = piece_refs[0].shape
-    nquery = scratch.shape[0]
-    examples = []
-    for hop, pieces in hops:
-        for piece in pieces[:-1]:
-            examples.append((piece_refs[piece], piece_refs[piece].shape[0]))
-        last = piece_refs[pieces[-1]]
-        nex = last.shape[0] - qshare
-        examples.append((last, nex))
-        scratch[pl.ds((at ^ hop) * qshare, qshare)] = last[nex:]
-    ntrain = sum(nex for _, nex in examples)
-    both = jnp.concatenate(
+def as_rows(values):
+    half = values[0].shape[1]
+    return jnp.concatenate(
         [
-            jnp.concatenate(
-                [ref[:nex, row, :] for ref, nex in examples] + [scratch[:, row, :]], axis=0
-            )
-            for row in range(half)
+            jnp.concatenate([value[:, row, :] for value in values], axis=0) for row in range(half)
         ],
         axis=1,
     )
+
+
+def rows_kernel(qshare, whole_ref, *refs):
+    own = whole_ref.at[: whole_ref.shape[0] - qshare]
+    refs[-1][...] = as_rows([own, *refs[:-1]])
+
+
+def gram_kernel(qshare, hops, at_ref, first_ref, *refs):
+    piece_refs, (out_ref, scratch) = refs[:-2], refs[-2:]
+    nquery = scratch.shape[0]
+    examples = []
+    for hop, ref in zip(hops, piece_refs):
+        nex = ref.shape[0] - qshare
+        if hop:
+            examples.append(ref.at[:nex])
+        scratch[pl.ds((at_ref[0] ^ hop) * qshare, qshare)] = ref[nex:]
+    both = jnp.concatenate([first_ref[...], as_rows([*examples, scratch])], axis=0)
+    ntrain = both.shape[0] - nquery
     size = ntrain + nquery
     high, low = halves(both)
-    gap = jnp.zeros((-size % 128, half * lanes), high.dtype)
+    gap = jnp.zeros((-size % 128, both.shape[1]), high.dtype)
     left = jnp.concatenate([high, low], axis=0)
     right = jnp.concatenate([high, gap, low], axis=0)
     total = lax.dot_general(left, right, NT, preferred_element_type=F32)
@@ -372,17 +376,22 @@
         2: swap(lax.optimization_barrier((after, ahead[2], ahead[1]))[0], 0, 2),
         1: swap(after, 0, 1),
     }
-    blocks = [whole, ahead[1], behind[1], far, ahead[2], behind[2]]
-    hops = ((0, (0,)), (1, (1, 2)), (3, (3,)), (2, (4, 5)))
+    first = call(
+        functools.partial(rows_kernel, qshare),
+        jax.ShapeDtypeStruct((4 * nex, half * 2 * rank), F32),
+        "rows",
+    )(whole, ahead[1], ahead[2])
+    blocks = [whole, behind[1], far, behind[2]]
+    hops = (0, 1, 3, 2)
     size = ntrain + nquery
     shape = (ntrain // 2 + nquery, 2 * ntrain) if folds(ntrain) else (size, size)
     gram = call(
         functools.partial(gram_kernel, qshare, hops),
         jax.ShapeDtypeStruct(shape, F32),
         "gram",
-        in_specs=[SMEM_SPEC] + [VMEM_SPEC] * len(blocks),
+        in_specs=[SMEM_SPEC] + [VMEM_SPEC] * (1 + len(blocks)),
         scratch_shapes=[pltpu.VMEM((nquery, half, 2 * rank), F32)],
-    )(at, *blocks)
+    )(at, first, *blocks)
     gram = gram + swap(gram, 3, 0)
     return call(
         functools.partial(solve_kernel, ntrain, rank * rank, share),

time: 46.3 us -> 46.7 us (level)
  Pallas kernels: 11.5 us -> 12.1 us
    pallas_call x3, Pallas kernels: 9.32 us -> 9.9 us  [project(): call(functools.partial(project_kernel, mesh, parts, hops, tile), [jax.Sha...]
  transfers between devices with their start and end apart: 13 -> 13, of which waited for: 6 -> 6; matrix products, arithmetic and copies ran while one was open for 0% -> 0% of each run, Pallas kernels for 14% -> 15%
where the time goes in v6:
time: 46.7 us; the launch traced here: 46.5 us
  starting transfers between devices  17.5 us (37%)
  waiting for transfers between devices  16.6 us (36%)
  Pallas kernels  12.1 us (26%)
    ppermute x13, starting transfers between devices, swap(): lax.ppermute(value, ('dp', 'tensor'), [(i, i ^ flip) for i in range(group...  17.5 us
    ppermute x13, waiting for transfers between devices, swap(): lax.ppermute(value, ('dp', 'tensor'), [(i, i ^ flip) for i in range(group...  16.6 us
    pallas_call x3, Pallas kernels, project(): call(functools.partial(project_kernel, mesh, parts, hops, tile), [jax.Sha...  9.9 us
    pallas_call x1, Pallas kernels, per_device(): call(functools.partial(solve_kernel, ntrain, rank * rank, share), jax.Sha...  1.29 us
  transfers between devices with their start and end apart: 13, of which 6 were waited for; matrix products, arithmetic and copies ran while one was open for 0% of the time, Pallas kernels for 15%

profile of v6, /device:TPU:0, one launch (start us, length us, event | category | flops | bytes accessed | tf_op | source)
XLA Modules:
  0.0 46.5 jit_solution(10382316419001043296)
XLA Ops:
  0.0 3.1 %project_3.1 = f32[320,128]{1,0:T(8,128)S(1)} custom-call(s32[1]{0:T(128)} %bitcast.1.at_ref, bf16[1024,3584]{1,0:T(8,128)(2,1)} %bitcast.16, bf16[1024,1024]{1,0:T(8,128)(2,1)} %bitcast.19, bf16[256,3584]{1,0:T(8,128)(2,1)} %bitcast.22, bf16[256,1024]{1,0:T(8,128)(2,1)} %bitcast.25, bf16[64,3584]{1,0:T(8,128)(2,1)} %bitcast.28, bf16[64,1024]{1,0:T(8,128)(2,1)} %bitcast.31), custom_call_target="tpu_custom_call" | custom-call | flops 188743680 | bytes 3538944 | tf_op jit(solution)/shard_map/project_3/pallas_call | solution.py:110
  3.1 5.1 %collective-permute-start = (f32[320,128]{1,0:T(8,128)S(1)}, f32[320,128]{1,0:T(8,128)S(1)}, u32[]{:S(2)}, u32[]{:S(2)}) collective-permute-start(f32[320,128]{1,0:T(8,128)S(1)} %project_3.1), channel_id=1, source_target_pairs={{0,3},{1,2},{2,1},{3,0},{4,7},{5,6},{6,5},{7,4},{8,11},{9,10},{10,... | collective-permute-start | bytes 491528 | tf_op jit(solution)/shard_map/ppermute | solution.py:35
  8.2 3.8 %project_2_1.1 = (f32[320,128]{1,0:T(8,128)S(1)}, f32[320,128]{1,0:T(8,128)S(1)}) custom-call(s32[1]{0:T(128)} %bitcast.1.at_ref, bf16[1024,3584]{1,0:T(8,128)(2,1)} %bitcast.17, bf16[1024,1024]{1,0:T(8,128)(2,1)} %bitcast.20, bf16[256,3584]{1,0:T(8,128)(2,1)} %bitcast.23, bf16[256,1024]{1,0:T(8,128)(2,1)} %bitcast.26, bf16[64,3584]{1,0:T(8,128)(2,1)} %bitcast.29, ...), custom_call_target="tpu_custom_call" | custom-call | flops 377487360 | bytes 6488064 | tf_op jit(solution)/shard_map/project_2_1/pallas_call | solution.py:110
  12.0 0.1 collective-permute-start.1
  12.0 0.6 %collective-permute-start.2 = (f32[320,128]{1,0:T(8,128)S(1)}, f32[320,128]{1,0:T(8,128)S(1)}, u32[]{:S(2)}, u32[]{:S(2)}) collective-permute-start(f32[320,128]{1,0:T(8,128)S(1)} %get-tuple-element.23), channel_id=1, source_target_pairs={{0,1},{1,0},{2,3},{3,2},{4,5},{5,4},{6,7},{7,6},{8,9},{9,8},{10,11... | collective-permute-start | bytes 491528 | tf_op jit(solution)/shard_map/ppermute | solution.py:35
  12.6 0.0 copy-start
  12.6 0.0 copy-start.1
  12.6 3.1 %project_0.1 = f32[320,128]{1,0:T(8,128)S(1)} custom-call(s32[1]{0:T(128)} %bitcast.1.at_ref, bf16[1024,3584]{1,0:T(8,128)(2,1)} %bitcast.18, bf16[1024,1024]{1,0:T(8,128)(2,1)} %bitcast.21, bf16[256,3584]{1,0:T(8,128)(2,1)} %bitcast.24, bf16[256,1024]{1,0:T(8,128)(2,1)} %bitcast.27, bf16[64,3584]{1,0:T(8,128)(2,1)} %bitcast.30, bf16[64,1024]{1,0:T(8,128)(2,1)} %bitcast.33), custom_call_target="tpu_custom_call" | custom-call | flops 188743680 | bytes 3538944 | tf_op jit(solution)/shard_map/project_0/pallas_call | solution.py:110
  15.7 0.0 collective-permute-done
  15.7 6.3 %collective-permute-done.1.refs_1_ = f32[320,128]{1,0:T(8,128)S(1)} collective-permute-done((f32[320,128]{1,0:T(8,128)S(1)}, f32[320,128]{1,0:T(8,128)S(1)}, u32[]{:S(2)}, u32[]{:S(2)}) %collective-permute-start.1) | collective-permute-done | bytes 163872 | tf_op jit(solution)/shard_map/ppermute | solution.py:35
  22.1 0.0 collective-permute-done.2.refs_2_
  22.1 0.0 copy-done
  22.1 0.0 copy-done.1
  22.1 0.4 outer.1
  22.5 0.1 collective-permute-start.3
  22.6 1.2 %collective-permute-done.3 = f32[2,7,8,128]{3,2,1,0:T(8,128)S(1)} collective-permute-done((f32[2,7,8,128]{3,2,1,0:T(8,128)S(1)}, f32[2,7,8,128]{3,2,1,0:T(8,128)S(1)}, u32[]{:S(2)}, u32[]{:S(2)}) %collective-permute-start.3) | collective-permute-done | bytes 57376 | tf_op jit(solution)/shard_map/ppermute | solution.py:35
  23.9 1.3 %collective-permute-start.4 = (f32[9,8,128]{2,1,0:T(8,128)S(1)}, f32[9,8,128]{2,1,0:T(8,128)S(1)}, u32[]{:S(2)}, u32[]{:S(2)}) collective-permute-start(f32[9,8,128]{2,1,0:T(8,128)S(1)} %get-tuple-element.32), channel_id=1, source_target_pairs={{0,12},{1,13},{2,14},{3,15},{4,8},{5,9},{6,10},{7,11},{8,4},{9,5},... | collective-permute-start | bytes 110600 | tf_op jit(solution)/shard_map/ppermute | solution.py:35
  25.2 2.2 %collective-permute-done.4 = f32[9,8,128]{2,1,0:T(8,128)S(1)} collective-permute-done((f32[9,8,128]{2,1,0:T(8,128)S(1)}, f32[9,8,128]{2,1,0:T(8,128)S(1)}, u32[]{:S(2)}, u32[]{:S(2)}) %collective-permute-start.4) | collective-permute-done | bytes 36896 | tf_op jit(solution)/shard_map/ppermute | solution.py:35
  27.4 1.3 %collective-permute-start.5 = (f32[13,8,128]{2,1,0:T(8,128)S(1)}, f32[13,8,128]{2,1,0:T(8,128)S(1)}, u32[]{:S(2)}, u32[]{:S(2)}) collective-permute-start(f32[13,8,128]{2,1,0:T(8,128)S(1)} %pad_maximum_fusion.2), channel_id=1, source_target_pairs={{0,20},{1,21},{2,22},{3,23},{4,16},{5,17},{6,18},{7,19},{8,28},{9,... | collective-permute-start | bytes 159752 | tf_op jit(solution)/shard_map/ppermute | solution.py:35
  28.8 0.0 collective-permute-start.6
  28.8 3.0 %collective-permute-start.7 = (f32[8,8,128]{2,1,0:T(8,128)S(1)}, f32[8,8,128]{2,1,0:T(8,128)S(1)}, u32[]{:S(2)}, u32[]{:S(2)}) collective-permute-start(f32[8,8,128]{2,1,0:T(8,128)S(1)} %pad_maximum_fusion.4), channel_id=1, source_target_pairs={{0,2},{1,3},{2,0},{3,1},{4,6},{5,7},{6,4},{7,5},{8,10},{9,11},{10,... | collective-permute-start | bytes 98312 | tf_op jit(solution)/shard_map/ppermute | solution.py:35
  31.8 0.0 collective-permute-done.5
  31.9 2.0 %collective-permute-start.9 = (f32[20,8,128]{2,1,0:T(8,128)S(1)}, f32[20,8,128]{2,1,0:T(8,128)S(1)}, u32[]{:S(2)}, u32[]{:S(2)}) collective-permute-start(f32[20,8,128]{2,1,0:T(8,128)S(1)} %pad_maximum_fusion.whole_ref.refs_0_), channel_id=1, source_target_pairs={{0,3},{1,2},{2,1},{3,0},{4,7},{5,6},{6,5},{7,4},{8,11},{9,10},{10,... | collective-permute-start | bytes 245768 | tf_op jit(solution)/shard_map/ppermute | solution.py:35
  33.9 0.0 collective-permute-start.8
  33.9 0.0 collective-permute-done.6.refs_0_
  33.9 0.0 collective-permute-done.7.refs_1_
  33.9 2.8 %collective-permute-start.10 = (f32[12,8,128]{2,1,0:T(8,128)S(1)}, f32[12,8,128]{2,1,0:T(8,128)S(1)}, u32[]{:S(2)}, u32[]{:S(2)}) collective-permute-start(f32[12,8,128]{2,1,0:T(8,128)S(1)} %pad_maximum_fusion.3), channel_id=1, source_target_pairs={{0,2},{1,3},{2,0},{3,1},{4,6},{5,7},{6,4},{7,5},{8,10},{9,11},{10,... | collective-permute-start | bytes 147464 | tf_op jit(solution)/shard_map/ppermute | solution.py:35
  36.7 0.1 rows.1.first_ref
  36.8 3.3 %collective-permute-done.8.refs_1_ = f32[12,8,128]{2,1,0:T(8,128)S(1)} collective-permute-done((f32[12,8,128]{2,1,0:T(8,128)S(1)}, f32[12,8,128]{2,1,0:T(8,128)S(1)}, u32[]{:S(2)}, u32[]{:S(2)}) %collective-permute-start.8) | collective-permute-done | bytes 49184 | tf_op jit(solution)/shard_map/ppermute | solution.py:35
  40.1 0.0 collective-permute-done.10.refs_3_
  40.1 0.0 collective-permute-done.9.refs_2_
  40.1 0.4 gram.1
  40.5 1.0 %collective-permute-start.11 = (f32[48,128]{1,0:T(8,128)S(1)}, f32[48,128]{1,0:T(8,128)S(1)}, u32[]{:S(2)}, u32[]{:S(2)}) collective-permute-start(f32[48,128]{1,0:T(8,128)S(1)} %gram.1), channel_id=1, source_target_pairs={{0,12},{1,13},{2,14},{3,15},{4,8},{5,9},{6,10},{7,11},{8,4},{9,5},... | collective-permute-start | bytes 73736 | tf_op jit(solution)/shard_map/ppermute | solution.py:35
  41.6 2.5 %collective-permute-done.11 = f32[48,128]{1,0:T(8,128)S(1)} collective-permute-done((f32[48,128]{1,0:T(8,128)S(1)}, f32[48,128]{1,0:T(8,128)S(1)}, u32[]{:S(2)}, u32[]{:S(2)}) %collective-permute-start.11) | collective-permute-done | bytes 24608 | tf_op jit(solution)/shard_map/ppermute | solution.py:35
  44.0 0.1 collective-permute-start.12
  44.2 1.1 %collective-permute-done.12.two_ref = f32[48,128]{1,0:T(8,128)S(1)} collective-permute-done((f32[48,128]{1,0:T(8,128)S(1)}, f32[48,128]{1,0:T(8,128)S(1)}, u32[]{:S(2)}, u32[]{:S(2)}) %collective-permute-start.12) | collective-permute-done | bytes 24608 | tf_op jit(solution)/shard_map/ppermute | solution.py:35
  45.2 1.3 %solve.1 = f32[2,16]{1,0:T(2,128)} custom-call(s32[1]{0:T(128)} %bitcast.low_ref, f32[48,128]{1,0:T(8,128)S(1)} %add.27.one_ref, f32[48,128]{1,0:T(8,128)S(1)} %collective-permute-done.12.two_ref), custom_call_target="tpu_custom_call" | custom-call | tf_op jit(solution)/shard_map/solve/pallas_call | solution.py:396
  (16 shorter events, 0.1 us)
Async XLA Ops:
  3.1 12.6 %collective-permute-start = (f32[320,128]{1,0:T(8,128)S(1)}, f32[320,128]{1,0:T(8,128)S(1)}, u32[]{:S(2)}, u32[]{:S(2)}) collective-permute-start(f32[320,128]{1,0:T(8,128)S(1)} %project_3.1), channel_id=1, source_target_pairs={{0,3},{1,2},{2,1},{3,0},{4,7},{5,6},{6,5},{7,4},{8,11},{9,10},{10,... | collective-permute-start | bytes 491528 | tf_op jit(solution)/shard_map/ppermute | solution.py:35
  12.0 10.1 %collective-permute-start.1 = (f32[320,128]{1,0:T(8,128)S(1)}, f32[320,128]{1,0:T(8,128)S(1)}, u32[]{:S(2)}, u32[]{:S(2)}) collective-permute-start(f32[320,128]{1,0:T(8,128)S(1)} %get-tuple-element.22), channel_id=1, source_target_pairs={{0,2},{1,3},{2,0},{3,1},{4,6},{5,7},{6,4},{7,5},{8,10},{9,11},{10,... | collective-permute-start | bytes 491528 | tf_op jit(solution)/shard_map/ppermute | solution.py:35
  12.0 10.0 %collective-permute-start.2 = (f32[320,128]{1,0:T(8,128)S(1)}, f32[320,128]{1,0:T(8,128)S(1)}, u32[]{:S(2)}, u32[]{:S(2)}) collective-permute-start(f32[320,128]{1,0:T(8,128)S(1)} %get-tuple-element.23), channel_id=1, source_target_pairs={{0,1},{1,0},{2,3},{3,2},{4,5},{5,4},{6,7},{7,6},{8,9},{9,8},{10,11... | collective-permute-start | bytes 491528 | tf_op jit(solution)/shard_map/ppermute | solution.py:35
  12.6 9.5 %copy-start = (s32[16,16]{1,0:T(8,128)S(1)}, s32[16,16]{1,0:T(8,128)}, u32[]{:S(2)}) copy-start(s32[16,16]{1,0:T(8,128)} %qids_ref.1) | copy-start | bytes 3076
  12.6 9.5 %copy-start.1 = (s32[8,128]{1,0:T(8,128)S(1)}, s32[8,128]{1,0:T(8,128)}, u32[]{:S(2)}) copy-start(s32[8,128]{1,0:T(8,128)} %ids_ref.1) | copy-start | bytes 12292
  22.5 1.3 %collective-permute-start.3 = (f32[2,7,8,128]{3,2,1,0:T(8,128)S(1)}, f32[2,7,8,128]{3,2,1,0:T(8,128)S(1)}, u32[]{:S(2)}, u32[]{:S(2)}) collective-permute-start(f32[2,7,8,128]{3,2,1,0:T(8,128)S(1)} %get-tuple-element.25), channel_id=1, source_target_pairs={{0,4},{1,5},{2,6},{3,7},{4,0},{5,1},{6,2},{7,3},{8,12},{9,13},{10,... | collective-permute-start | bytes 172040 | tf_op jit(solution)/shard_map/ppermute | solution.py:35
  23.9 3.5 %collective-permute-start.4 = (f32[9,8,128]{2,1,0:T(8,128)S(1)}, f32[9,8,128]{2,1,0:T(8,128)S(1)}, u32[]{:S(2)}, u32[]{:S(2)}) collective-permute-start(f32[9,8,128]{2,1,0:T(8,128)S(1)} %get-tuple-element.32), channel_id=1, source_target_pairs={{0,12},{1,13},{2,14},{3,15},{4,8},{5,9},{6,10},{7,11},{8,4},{9,5},... | collective-permute-start | bytes 110600 | tf_op jit(solution)/shard_map/ppermute | solution.py:35
  27.4 4.4 %collective-permute-start.5 = (f32[13,8,128]{2,1,0:T(8,128)S(1)}, f32[13,8,128]{2,1,0:T(8,128)S(1)}, u32[]{:S(2)}, u32[]{:S(2)}) collective-permute-start(f32[13,8,128]{2,1,0:T(8,128)S(1)} %pad_maximum_fusion.2), channel_id=1, source_target_pairs={{0,20},{1,21},{2,22},{3,23},{4,16},{5,17},{6,18},{7,19},{8,28},{9,... | collective-permute-start | bytes 159752 | tf_op jit(solution)/shard_map/ppermute | solution.py:35
  28.8 5.1 %collective-permute-start.6 = (f32[8,8,128]{2,1,0:T(8,128)S(1)}, f32[8,8,128]{2,1,0:T(8,128)S(1)}, u32[]{:S(2)}, u32[]{:S(2)}) collective-permute-start(f32[8,8,128]{2,1,0:T(8,128)S(1)} %pad_maximum_fusion.4), channel_id=1, source_target_pairs={{0,1},{1,0},{2,3},{3,2},{4,5},{5,4},{6,7},{7,6},{8,9},{9,8},{10,11... | collective-permute-start | bytes 98312 | tf_op jit(solution)/shard_map/ppermute | solution.py:35
  28.8 5.1 %collective-permute-start.7 = (f32[8,8,128]{2,1,0:T(8,128)S(1)}, f32[8,8,128]{2,1,0:T(8,128)S(1)}, u32[]{:S(2)}, u32[]{:S(2)}) collective-permute-start(f32[8,8,128]{2,1,0:T(8,128)S(1)} %pad_maximum_fusion.4), channel_id=1, source_target_pairs={{0,2},{1,3},{2,0},{3,1},{4,6},{5,7},{6,4},{7,5},{8,10},{9,11},{10,... | collective-permute-start | bytes 98312 | tf_op jit(solution)/shard_map/ppermute | solution.py:35
  31.9 8.2 %collective-permute-start.9 = (f32[20,8,128]{2,1,0:T(8,128)S(1)}, f32[20,8,128]{2,1,0:T(8,128)S(1)}, u32[]{:S(2)}, u32[]{:S(2)}) collective-permute-start(f32[20,8,128]{2,1,0:T(8,128)S(1)} %pad_maximum_fusion.whole_ref.refs_0_), channel_id=1, source_target_pairs={{0,3},{1,2},{2,1},{3,0},{4,7},{5,6},{6,5},{7,4},{8,11},{9,10},{10,... | collective-permute-start | bytes 245768 | tf_op jit(solution)/shard_map/ppermute | solution.py:35
  33.9 6.2 %collective-permute-start.8 = (f32[12,8,128]{2,1,0:T(8,128)S(1)}, f32[12,8,128]{2,1,0:T(8,128)S(1)}, u32[]{:S(2)}, u32[]{:S(2)}) collective-permute-start(f32[12,8,128]{2,1,0:T(8,128)S(1)} %pad_maximum_fusion.3), channel_id=1, source_target_pairs={{0,1},{1,0},{2,3},{3,2},{4,5},{5,4},{6,7},{7,6},{8,9},{9,8},{10,11... | collective-permute-start | bytes 147464 | tf_op jit(solution)/shard_map/ppermute | solution.py:35
  33.9 6.2 %collective-permute-start.10 = (f32[12,8,128]{2,1,0:T(8,128)S(1)}, f32[12,8,128]{2,1,0:T(8,128)S(1)}, u32[]{:S(2)}, u32[]{:S(2)}) collective-permute-start(f32[12,8,128]{2,1,0:T(8,128)S(1)} %pad_maximum_fusion.3), channel_id=1, source_target_pairs={{0,2},{1,3},{2,0},{3,1},{4,6},{5,7},{6,4},{7,5},{8,10},{9,11},{10,... | collective-permute-start | bytes 147464 | tf_op jit(solution)/shard_map/ppermute | solution.py:35
  40.5 3.5 %collective-permute-start.11 = (f32[48,128]{1,0:T(8,128)S(1)}, f32[48,128]{1,0:T(8,128)S(1)}, u32[]{:S(2)}, u32[]{:S(2)}) collective-permute-start(f32[48,128]{1,0:T(8,128)S(1)} %gram.1), channel_id=1, source_target_pairs={{0,12},{1,13},{2,14},{3,15},{4,8},{5,9},{6,10},{7,11},{8,4},{9,5},... | collective-permute-start | bytes 73736 | tf_op jit(solution)/shard_map/ppermute | solution.py:35
  44.0 1.2 %collective-permute-start.12 = (f32[48,128]{1,0:T(8,128)S(1)}, f32[48,128]{1,0:T(8,128)S(1)}, u32[]{:S(2)}, u32[]{:S(2)}) collective-permute-start(f32[48,128]{1,0:T(8,128)S(1)} %add.27.one_ref), channel_id=1, source_target_pairs={{0,4},{1,5},{2,6},{3,7},{4,0},{5,1},{6,2},{7,3},{8,12},{9,13},{10,... | collective-permute-start | bytes 73736 | tf_op jit(solution)/shard_map/ppermute | solution.py:35

commit v7 on v6

--- a/solution.py
+++ b/solution.py
@@ -67,35 +67,45 @@
             copies = []
             for src, dst in pairs:
                 copies.append(pltpu.make_async_copy(src, dst, sems.at[started]))
-                copies[-1].start()
                 started += 1
             chunks.append((side, start, size, copies))
+    for *_, copies in chunks[:-1]:
+        for copy in copies:
+            copy.start()
+
+    by_rows = len(hops) > 1
+    held_rows = hid.shape[0] // 2 if by_rows else hid.shape[0]
 
     def multiply(*sums):
         count = 0
-        half = hid.shape[0] // 2
-        for side, start, size, copies in chunks:
+        for index, (side, start, size, copies) in enumerate(chunks):
             _, _, buf, _, held = sides[side]
             for copy in copies:
                 copy.wait()
+            if index == 0:
+                for copy in chunks[-1][-1]:
+                    copy.start()
             for col in range(start, start + size, tile):
-                turn = count % 2
-                count += 1
                 weight = [held[:, col : col + tile]]
                 if side:
                     weight.insert(0, jnp.zeros((side * rank, tile), held.dtype))
                 weight.append(jnp.zeros((tile - (side + 1) * rank, tile), held.dtype))
                 weight = jnp.concatenate(weight, axis=0)
-                for unit, acc in enumerate(sums):
+                units = range(len(sums)) if by_rows else (count % len(sums),)
+                turn = (count if by_rows else count // len(sums)) % 2
+                count += 1
+                for unit in units:
+                    first = unit * held_rows if by_rows else 0
                     pltpu.matmul_push_rhs(weight, turn, unit, transpose=True)
-                    tokens = buf[unit * half : (unit + 1) * half, col : col + tile]
-                    pltpu.matmul_acc_lhs(acc, tokens, load_staged_rhs=turn)
-        total = jnp.concatenate([pltpu.matmul_pop(acc)[:, : 2 * rank] for acc in sums], axis=0)
+                    tokens = buf[first : first + held_rows, col : col + tile]
+                    pltpu.matmul_acc_lhs(sums[unit], tokens, load_staged_rhs=turn)
+        total = [pltpu.matmul_pop(acc)[:, : 2 * rank] for acc in sums]
+        total = jnp.concatenate(total, axis=0) if by_rows else sum(total)
         for slot, ref in enumerate(out_refs):
             ref[...] = total[slot * rows : (slot + 1) * rows]
 
     with jax.sharding.use_abstract_mesh(mesh.abstract_mesh):
-        sums = [pltpu.ACC(unit)((hid.shape[0] // 2, tile), F32) for unit in range(2)]
+        sums = [pltpu.ACC(unit)((held_rows, tile), F32) for unit in range(2)]
         pl.run_scoped(multiply, *sums)
 
 

time: 46.7 us -> 46.6 us (level)
  no operation moved by 1% of the time
where the time goes in v7:
time: 46.6 us; the launch traced here: 46.4 us
  starting transfers between devices  17.5 us (38%)
  waiting for transfers between devices  16.7 us (36%)
  Pallas kernels  11.9 us (26%)
    ppermute x13, starting transfers between devices, swap(): lax.ppermute(value, ('dp', 'tensor'), [(i, i ^ flip) for i in range(group...  17.5 us
    ppermute x13, waiting for transfers between devices, swap(): lax.ppermute(value, ('dp', 'tensor'), [(i, i ^ flip) for i in range(group...  16.7 us
    pallas_call x3, Pallas kernels, project(): call(functools.partial(project_kernel, mesh, parts, hops, tile), [jax.Sha...  9.65 us
    pallas_call x1, Pallas kernels, per_device(): call(functools.partial(solve_kernel, ntrain, rank * rank, share), jax.Sha...  1.29 us
  transfers between devices with their start and end apart: 13, of which 6 were waited for; matrix products, arithmetic and copies ran while one was open for 0% of the time, Pallas kernels for 15%

profile of v7, /device:TPU:0, one launch (start us, length us, event | category | flops | bytes accessed | tf_op | source)
XLA Modules:
  0.0 46.4 jit_solution(7103724711656248190)
XLA Ops:
  0.0 2.9 %project_3.1 = f32[320,128]{1,0:T(8,128)S(1)} custom-call(s32[1]{0:T(128)} %bitcast.1.at_ref, bf16[1024,3584]{1,0:T(8,128)(2,1)} %bitcast.16, bf16[1024,1024]{1,0:T(8,128)(2,1)} %bitcast.19, bf16[256,3584]{1,0:T(8,128)(2,1)} %bitcast.22, bf16[256,1024]{1,0:T(8,128)(2,1)} %bitcast.25, bf16[64,3584]{1,0:T(8,128)(2,1)} %bitcast.28, bf16[64,1024]{1,0:T(8,128)(2,1)} %bitcast.31), custom_call_target="tpu_custom_call" | custom-call | flops 188743680 | bytes 3538944 | tf_op jit(solution)/shard_map/project_3/pallas_call | solution.py:120
  2.9 5.1 %collective-permute-start = (f32[320,128]{1,0:T(8,128)S(1)}, f32[320,128]{1,0:T(8,128)S(1)}, u32[]{:S(2)}, u32[]{:S(2)}) collective-permute-start(f32[320,128]{1,0:T(8,128)S(1)} %project_3.1), channel_id=1, source_target_pairs={{0,3},{1,2},{2,1},{3,0},{4,7},{5,6},{6,5},{7,4},{8,11},{9,10},{10,... | collective-permute-start | bytes 491528 | tf_op jit(solution)/shard_map/ppermute | solution.py:35
  8.0 3.8 %project_2_1.1 = (f32[320,128]{1,0:T(8,128)S(1)}, f32[320,128]{1,0:T(8,128)S(1)}) custom-call(s32[1]{0:T(128)} %bitcast.1.at_ref, bf16[1024,3584]{1,0:T(8,128)(2,1)} %bitcast.17, bf16[1024,1024]{1,0:T(8,128)(2,1)} %bitcast.20, bf16[256,3584]{1,0:T(8,128)(2,1)} %bitcast.23, bf16[256,1024]{1,0:T(8,128)(2,1)} %bitcast.26, bf16[64,3584]{1,0:T(8,128)(2,1)} %bitcast.29, ...), custom_call_target="tpu_custom_call" | custom-call | flops 377487360 | bytes 6488064 | tf_op jit(solution)/shard_map/project_2_1/pallas_call | solution.py:120
  11.9 0.1 collective-permute-start.1
  12.0 0.6 %collective-permute-start.2 = (f32[320,128]{1,0:T(8,128)S(1)}, f32[320,128]{1,0:T(8,128)S(1)}, u32[]{:S(2)}, u32[]{:S(2)}) collective-permute-start(f32[320,128]{1,0:T(8,128)S(1)} %get-tuple-element.23), channel_id=1, source_target_pairs={{0,1},{1,0},{2,3},{3,2},{4,5},{5,4},{6,7},{7,6},{8,9},{9,8},{10,11... | collective-permute-start | bytes 491528 | tf_op jit(solution)/shard_map/ppermute | solution.py:35
  12.5 0.0 copy-start
  12.5 0.0 copy-start.1
  12.5 2.9 %project_0.1 = f32[320,128]{1,0:T(8,128)S(1)} custom-call(s32[1]{0:T(128)} %bitcast.1.at_ref, bf16[1024,3584]{1,0:T(8,128)(2,1)} %bitcast.18, bf16[1024,1024]{1,0:T(8,128)(2,1)} %bitcast.21, bf16[256,3584]{1,0:T(8,128)(2,1)} %bitcast.24, bf16[256,1024]{1,0:T(8,128)(2,1)} %bitcast.27, bf16[64,3584]{1,0:T(8,128)(2,1)} %bitcast.30, bf16[64,1024]{1,0:T(8,128)(2,1)} %bitcast.33), custom_call_target="tpu_custom_call" | custom-call | flops 188743680 | bytes 3538944 | tf_op jit(solution)/shard_map/project_0/pallas_call | solution.py:120
  15.5 0.0 collective-permute-done
  15.5 6.4 %collective-permute-done.1.refs_1_ = f32[320,128]{1,0:T(8,128)S(1)} collective-permute-done((f32[320,128]{1,0:T(8,128)S(1)}, f32[320,128]{1,0:T(8,128)S(1)}, u32[]{:S(2)}, u32[]{:S(2)}) %collective-permute-start.1) | collective-permute-done | bytes 163872 | tf_op jit(solution)/shard_map/ppermute | solution.py:35
  21.9 0.0 collective-permute-done.2.refs_2_
  21.9 0.0 copy-done
  21.9 0.0 copy-done.1
  21.9 0.4 outer.1
  22.4 0.1 collective-permute-start.3
  22.4 1.2 %collective-permute-done.3 = f32[2,7,8,128]{3,2,1,0:T(8,128)S(1)} collective-permute-done((f32[2,7,8,128]{3,2,1,0:T(8,128)S(1)}, f32[2,7,8,128]{3,2,1,0:T(8,128)S(1)}, u32[]{:S(2)}, u32[]{:S(2)}) %collective-permute-start.3) | collective-permute-done | bytes 57376 | tf_op jit(solution)/shard_map/ppermute | solution.py:35
  23.7 1.3 %collective-permute-start.4 = (f32[9,8,128]{2,1,0:T(8,128)S(1)}, f32[9,8,128]{2,1,0:T(8,128)S(1)}, u32[]{:S(2)}, u32[]{:S(2)}) collective-permute-start(f32[9,8,128]{2,1,0:T(8,128)S(1)} %get-tuple-element.32), channel_id=1, source_target_pairs={{0,12},{1,13},{2,14},{3,15},{4,8},{5,9},{6,10},{7,11},{8,4},{9,5},... | collective-permute-start | bytes 110600 | tf_op jit(solution)/shard_map/ppermute | solution.py:35
  25.0 2.2 %collective-permute-done.4 = f32[9,8,128]{2,1,0:T(8,128)S(1)} collective-permute-done((f32[9,8,128]{2,1,0:T(8,128)S(1)}, f32[9,8,128]{2,1,0:T(8,128)S(1)}, u32[]{:S(2)}, u32[]{:S(2)}) %collective-permute-start.4) | collective-permute-done | bytes 36896 | tf_op jit(solution)/shard_map/ppermute | solution.py:35
  27.2 1.4 %collective-permute-start.5 = (f32[13,8,128]{2,1,0:T(8,128)S(1)}, f32[13,8,128]{2,1,0:T(8,128)S(1)}, u32[]{:S(2)}, u32[]{:S(2)}) collective-permute-start(f32[13,8,128]{2,1,0:T(8,128)S(1)} %pad_maximum_fusion.2), channel_id=1, source_target_pairs={{0,20},{1,21},{2,22},{3,23},{4,16},{5,17},{6,18},{7,19},{8,28},{9,... | collective-permute-start | bytes 159752 | tf_op jit(solution)/shard_map/ppermute | solution.py:35
  28.6 0.0 collective-permute-start.6
  28.6 3.0 %collective-permute-start.7 = (f32[8,8,128]{2,1,0:T(8,128)S(1)}, f32[8,8,128]{2,1,0:T(8,128)S(1)}, u32[]{:S(2)}, u32[]{:S(2)}) collective-permute-start(f32[8,8,128]{2,1,0:T(8,128)S(1)} %pad_maximum_fusion.4), channel_id=1, source_target_pairs={{0,2},{1,3},{2,0},{3,1},{4,6},{5,7},{6,4},{7,5},{8,10},{9,11},{10,... | collective-permute-start | bytes 98312 | tf_op jit(solution)/shard_map/ppermute | solution.py:35
  31.6 0.0 collective-permute-done.5
  31.7 2.0 %collective-permute-start.9 = (f32[20,8,128]{2,1,0:T(8,128)S(1)}, f32[20,8,128]{2,1,0:T(8,128)S(1)}, u32[]{:S(2)}, u32[]{:S(2)}) collective-permute-start(f32[20,8,128]{2,1,0:T(8,128)S(1)} %pad_maximum_fusion.whole_ref.refs_0_), channel_id=1, source_target_pairs={{0,3},{1,2},{2,1},{3,0},{4,7},{5,6},{6,5},{7,4},{8,11},{9,10},{10,... | collective-permute-start | bytes 245768 | tf_op jit(solution)/shard_map/ppermute | solution.py:35
  33.7 0.0 collective-permute-start.8
  33.7 0.0 collective-permute-done.6.refs_0_
  33.7 0.0 collective-permute-done.7.refs_1_
  33.7 2.8 %collective-permute-start.10 = (f32[12,8,128]{2,1,0:T(8,128)S(1)}, f32[12,8,128]{2,1,0:T(8,128)S(1)}, u32[]{:S(2)}, u32[]{:S(2)}) collective-permute-start(f32[12,8,128]{2,1,0:T(8,128)S(1)} %pad_maximum_fusion.3), channel_id=1, source_target_pairs={{0,2},{1,3},{2,0},{3,1},{4,6},{5,7},{6,4},{7,5},{8,10},{9,11},{10,... | collective-permute-start | bytes 147464 | tf_op jit(solution)/shard_map/ppermute | solution.py:35
  36.6 0.1 rows.1.first_ref
  36.6 3.3 %collective-permute-done.8.refs_1_ = f32[12,8,128]{2,1,0:T(8,128)S(1)} collective-permute-done((f32[12,8,128]{2,1,0:T(8,128)S(1)}, f32[12,8,128]{2,1,0:T(8,128)S(1)}, u32[]{:S(2)}, u32[]{:S(2)}) %collective-permute-start.8) | collective-permute-done | bytes 49184 | tf_op jit(solution)/shard_map/ppermute | solution.py:35
  39.9 0.0 collective-permute-done.10.refs_3_
  39.9 0.0 collective-permute-done.9.refs_2_
  39.9 0.4 gram.1
  40.4 1.0 %collective-permute-start.11 = (f32[48,128]{1,0:T(8,128)S(1)}, f32[48,128]{1,0:T(8,128)S(1)}, u32[]{:S(2)}, u32[]{:S(2)}) collective-permute-start(f32[48,128]{1,0:T(8,128)S(1)} %gram.1), channel_id=1, source_target_pairs={{0,12},{1,13},{2,14},{3,15},{4,8},{5,9},{6,10},{7,11},{8,4},{9,5},... | collective-permute-start | bytes 73736 | tf_op jit(solution)/shard_map/ppermute | solution.py:35
  41.4 2.5 %collective-permute-done.11 = f32[48,128]{1,0:T(8,128)S(1)} collective-permute-done((f32[48,128]{1,0:T(8,128)S(1)}, f32[48,128]{1,0:T(8,128)S(1)}, u32[]{:S(2)}, u32[]{:S(2)}) %collective-permute-start.11) | collective-permute-done | bytes 24608 | tf_op jit(solution)/shard_map/ppermute | solution.py:35
  43.9 0.1 collective-permute-start.12
  44.0 1.1 %collective-permute-done.12.two_ref = f32[48,128]{1,0:T(8,128)S(1)} collective-permute-done((f32[48,128]{1,0:T(8,128)S(1)}, f32[48,128]{1,0:T(8,128)S(1)}, u32[]{:S(2)}, u32[]{:S(2)}) %collective-permute-start.12) | collective-permute-done | bytes 24608 | tf_op jit(solution)/shard_map/ppermute | solution.py:35
  45.1 1.3 %solve.1 = f32[2,16]{1,0:T(2,128)} custom-call(s32[1]{0:T(128)} %bitcast.low_ref, f32[48,128]{1,0:T(8,128)S(1)} %add.27.one_ref, f32[48,128]{1,0:T(8,128)S(1)} %collective-permute-done.12.two_ref), custom_call_target="tpu_custom_call" | custom-call | tf_op jit(solution)/shard_map/solve/pallas_call | solution.py:406
  (16 shorter events, 0.1 us)
Async XLA Ops:
  2.9 12.6 %collective-permute-start = (f32[320,128]{1,0:T(8,128)S(1)}, f32[320,128]{1,0:T(8,128)S(1)}, u32[]{:S(2)}, u32[]{:S(2)}) collective-permute-start(f32[320,128]{1,0:T(8,128)S(1)} %project_3.1), channel_id=1, source_target_pairs={{0,3},{1,2},{2,1},{3,0},{4,7},{5,6},{6,5},{7,4},{8,11},{9,10},{10,... | collective-permute-start | bytes 491528 | tf_op jit(solution)/shard_map/ppermute | solution.py:35
  11.9 10.0 %collective-permute-start.1 = (f32[320,128]{1,0:T(8,128)S(1)}, f32[320,128]{1,0:T(8,128)S(1)}, u32[]{:S(2)}, u32[]{:S(2)}) collective-permute-start(f32[320,128]{1,0:T(8,128)S(1)} %get-tuple-element.22), channel_id=1, source_target_pairs={{0,2},{1,3},{2,0},{3,1},{4,6},{5,7},{6,4},{7,5},{8,10},{9,11},{10,... | collective-permute-start | bytes 491528 | tf_op jit(solution)/shard_map/ppermute | solution.py:35
  12.0 10.0 %collective-permute-start.2 = (f32[320,128]{1,0:T(8,128)S(1)}, f32[320,128]{1,0:T(8,128)S(1)}, u32[]{:S(2)}, u32[]{:S(2)}) collective-permute-start(f32[320,128]{1,0:T(8,128)S(1)} %get-tuple-element.23), channel_id=1, source_target_pairs={{0,1},{1,0},{2,3},{3,2},{4,5},{5,4},{6,7},{7,6},{8,9},{9,8},{10,11... | collective-permute-start | bytes 491528 | tf_op jit(solution)/shard_map/ppermute | solution.py:35
  12.5 9.4 %copy-start = (s32[16,16]{1,0:T(8,128)S(1)}, s32[16,16]{1,0:T(8,128)}, u32[]{:S(2)}) copy-start(s32[16,16]{1,0:T(8,128)} %qids_ref.1) | copy-start | bytes 3076
  12.5 9.4 %copy-start.1 = (s32[8,128]{1,0:T(8,128)S(1)}, s32[8,128]{1,0:T(8,128)}, u32[]{:S(2)}) copy-start(s32[8,128]{1,0:T(8,128)} %ids_ref.1) | copy-start | bytes 12292
  22.4 1.3 %collective-permute-start.3 = (f32[2,7,8,128]{3,2,1,0:T(8,128)S(1)}, f32[2,7,8,128]{3,2,1,0:T(8,128)S(1)}, u32[]{:S(2)}, u32[]{:S(2)}) collective-permute-start(f32[2,7,8,128]{3,2,1,0:T(8,128)S(1)} %get-tuple-element.25), channel_id=1, source_target_pairs={{0,4},{1,5},{2,6},{3,7},{4,0},{5,1},{6,2},{7,3},{8,12},{9,13},{10,... | collective-permute-start | bytes 172040 | tf_op jit(solution)/shard_map/ppermute | solution.py:35
  23.7 3.5 %collective-permute-start.4 = (f32[9,8,128]{2,1,0:T(8,128)S(1)}, f32[9,8,128]{2,1,0:T(8,128)S(1)}, u32[]{:S(2)}, u32[]{:S(2)}) collective-permute-start(f32[9,8,128]{2,1,0:T(8,128)S(1)} %get-tuple-element.32), channel_id=1, source_target_pairs={{0,12},{1,13},{2,14},{3,15},{4,8},{5,9},{6,10},{7,11},{8,4},{9,5},... | collective-permute-start | bytes 110600 | tf_op jit(solution)/shard_map/ppermute | solution.py:35
  27.2 4.4 %collective-permute-start.5 = (f32[13,8,128]{2,1,0:T(8,128)S(1)}, f32[13,8,128]{2,1,0:T(8,128)S(1)}, u32[]{:S(2)}, u32[]{:S(2)}) collective-permute-start(f32[13,8,128]{2,1,0:T(8,128)S(1)} %pad_maximum_fusion.2), channel_id=1, source_target_pairs={{0,20},{1,21},{2,22},{3,23},{4,16},{5,17},{6,18},{7,19},{8,28},{9,... | collective-permute-start | bytes 159752 | tf_op jit(solution)/shard_map/ppermute | solution.py:35
  28.6 5.1 %collective-permute-start.6 = (f32[8,8,128]{2,1,0:T(8,128)S(1)}, f32[8,8,128]{2,1,0:T(8,128)S(1)}, u32[]{:S(2)}, u32[]{:S(2)}) collective-permute-start(f32[8,8,128]{2,1,0:T(8,128)S(1)} %pad_maximum_fusion.4), channel_id=1, source_target_pairs={{0,1},{1,0},{2,3},{3,2},{4,5},{5,4},{6,7},{7,6},{8,9},{9,8},{10,11... | collective-permute-start | bytes 98312 | tf_op jit(solution)/shard_map/ppermute | solution.py:35
  28.6 5.1 %collective-permute-start.7 = (f32[8,8,128]{2,1,0:T(8,128)S(1)}, f32[8,8,128]{2,1,0:T(8,128)S(1)}, u32[]{:S(2)}, u32[]{:S(2)}) collective-permute-start(f32[8,8,128]{2,1,0:T(8,128)S(1)} %pad_maximum_fusion.4), channel_id=1, source_target_pairs={{0,2},{1,3},{2,0},{3,1},{4,6},{5,7},{6,4},{7,5},{8,10},{9,11},{10,... | collective-permute-start | bytes 98312 | tf_op jit(solution)/shard_map/ppermute | solution.py:35
  31.7 8.2 %collective-permute-start.9 = (f32[20,8,128]{2,1,0:T(8,128)S(1)}, f32[20,8,128]{2,1,0:T(8,128)S(1)}, u32[]{:S(2)}, u32[]{:S(2)}) collective-permute-start(f32[20,8,128]{2,1,0:T(8,128)S(1)} %pad_maximum_fusion.whole_ref.refs_0_), channel_id=1, source_target_pairs={{0,3},{1,2},{2,1},{3,0},{4,7},{5,6},{6,5},{7,4},{8,11},{9,10},{10,... | collective-permute-start | bytes 245768 | tf_op jit(solution)/shard_map/ppermute | solution.py:35
  33.7 6.2 %collective-permute-start.8 = (f32[12,8,128]{2,1,0:T(8,128)S(1)}, f32[12,8,128]{2,1,0:T(8,128)S(1)}, u32[]{:S(2)}, u32[]{:S(2)}) collective-permute-start(f32[12,8,128]{2,1,0:T(8,128)S(1)} %pad_maximum_fusion.3), channel_id=1, source_target_pairs={{0,1},{1,0},{2,3},{3,2},{4,5},{5,4},{6,7},{7,6},{8,9},{9,8},{10,11... | collective-permute-start | bytes 147464 | tf_op jit(solution)/shard_map/ppermute | solution.py:35
  33.7 6.2 %collective-permute-start.10 = (f32[12,8,128]{2,1,0:T(8,128)S(1)}, f32[12,8,128]{2,1,0:T(8,128)S(1)}, u32[]{:S(2)}, u32[]{:S(2)}) collective-permute-start(f32[12,8,128]{2,1,0:T(8,128)S(1)} %pad_maximum_fusion.3), channel_id=1, source_target_pairs={{0,2},{1,3},{2,0},{3,1},{4,6},{5,7},{6,4},{7,5},{8,10},{9,11},{10,... | collective-permute-start | bytes 147464 | tf_op jit(solution)/shard_map/ppermute | solution.py:35
  40.4 3.5 %collective-permute-start.11 = (f32[48,128]{1,0:T(8,128)S(1)}, f32[48,128]{1,0:T(8,128)S(1)}, u32[]{:S(2)}, u32[]{:S(2)}) collective-permute-start(f32[48,128]{1,0:T(8,128)S(1)} %gram.1), channel_id=1, source_target_pairs={{0,12},{1,13},{2,14},{3,15},{4,8},{5,9},{6,10},{7,11},{8,4},{9,5},... | collective-permute-start | bytes 73736 | tf_op jit(solution)/shard_map/ppermute | solution.py:35
  43.9 1.2 %collective-permute-start.12 = (f32[48,128]{1,0:T(8,128)S(1)}, f32[48,128]{1,0:T(8,128)S(1)}, u32[]{:S(2)}, u32[]{:S(2)}) collective-permute-start(f32[48,128]{1,0:T(8,128)S(1)} %add.27.one_ref), channel_id=1, source_target_pairs={{0,4},{1,5},{2,6},{3,7},{4,0},{5,1},{6,2},{7,3},{8,12},{9,13},{10,... | collective-permute-start | bytes 73736 | tf_op jit(solution)/shard_map/ppermute | solution.py:35

commit v8 on v7

--- a/solution.py
+++ b/solution.py
@@ -67,24 +67,19 @@
             copies = []
             for src, dst in pairs:
                 copies.append(pltpu.make_async_copy(src, dst, sems.at[started]))
+                copies[-1].start()
                 started += 1
             chunks.append((side, start, size, copies))
-    for *_, copies in chunks[:-1]:
-        for copy in copies:
-            copy.start()
 
     by_rows = len(hops) > 1
     held_rows = hid.shape[0] // 2 if by_rows else hid.shape[0]
 
     def multiply(*sums):
         count = 0
-        for index, (side, start, size, copies) in enumerate(chunks):
+        for side, start, size, copies in chunks:
             _, _, buf, _, held = sides[side]
             for copy in copies:
                 copy.wait()
-            if index == 0:
-                for copy in chunks[-1][-1]:
-                    copy.start()
             for col in range(start, start + size, tile):
                 weight = [held[:, col : col + tile]]
                 if side:

time: 46.6 us -> 46.3 us (level)
  Pallas kernels: 11.9 us -> 11.4 us
    pallas_call x3, Pallas kernels: 9.65 us -> 9.17 us  [project(): call(functools.partial(project_kernel, mesh, parts, hops, tile), [jax.Sha...]
  transfers between devices with their start and end apart: 13 -> 13, of which waited for: 6 -> 6; matrix products, arithmetic and copies ran while one was open for 0% -> 0% of each run, Pallas kernels for 15% -> 14%
where the time goes in v8:
time: 46.3 us; the launch traced here: 46.2 us
  starting transfers between devices  17.6 us (38%)
  waiting for transfers between devices  16.9 us (37%)
  Pallas kernels  11.4 us (25%)
    ppermute x13, starting transfers between devices, swap(): lax.ppermute(value, ('dp', 'tensor'), [(i, i ^ flip) for i in range(group...  17.6 us
    ppermute x13, waiting for transfers between devices, swap(): lax.ppermute(value, ('dp', 'tensor'), [(i, i ^ flip) for i in range(group...  16.9 us
    pallas_call x3, Pallas kernels, project(): call(functools.partial(project_kernel, mesh, parts, hops, tile), [jax.Sha...  9.17 us
    pallas_call x1, Pallas kernels, per_device(): call(functools.partial(solve_kernel, ntrain, rank * rank, share), jax.Sha...  1.29 us
  transfers between devices with their start and end apart: 13, of which 6 were waited for; matrix products, arithmetic and copies ran while one was open for 0% of the time, Pallas kernels for 14%

profile of v8, /device:TPU:0, one launch (start us, length us, event | category | flops | bytes accessed | tf_op | source)
XLA Modules:
  0.0 46.2 jit_solution(17152934912713138280)
XLA Ops:
  0.0 2.7 %project_3.1 = f32[320,128]{1,0:T(8,128)S(1)} custom-call(s32[1]{0:T(128)} %bitcast.1.at_ref, bf16[1024,3584]{1,0:T(8,128)(2,1)} %bitcast.16, bf16[1024,1024]{1,0:T(8,128)(2,1)} %bitcast.19, bf16[256,3584]{1,0:T(8,128)(2,1)} %bitcast.22, bf16[256,1024]{1,0:T(8,128)(2,1)} %bitcast.25, bf16[64,3584]{1,0:T(8,128)(2,1)} %bitcast.28, bf16[64,1024]{1,0:T(8,128)(2,1)} %bitcast.31), custom_call_target="tpu_custom_call" | custom-call | flops 188743680 | bytes 3538944 | tf_op jit(solution)/shard_map/project_3/pallas_call | solution.py:115
  2.7 5.1 %collective-permute-start = (f32[320,128]{1,0:T(8,128)S(1)}, f32[320,128]{1,0:T(8,128)S(1)}, u32[]{:S(2)}, u32[]{:S(2)}) collective-permute-start(f32[320,128]{1,0:T(8,128)S(1)} %project_3.1), channel_id=1, source_target_pairs={{0,3},{1,2},{2,1},{3,0},{4,7},{5,6},{6,5},{7,4},{8,11},{9,10},{10,... | collective-permute-start | bytes 491528 | tf_op jit(solution)/shard_map/ppermute | solution.py:35
  7.8 3.8 %project_2_1.1 = (f32[320,128]{1,0:T(8,128)S(1)}, f32[320,128]{1,0:T(8,128)S(1)}) custom-call(s32[1]{0:T(128)} %bitcast.1.at_ref, bf16[1024,3584]{1,0:T(8,128)(2,1)} %bitcast.17, bf16[1024,1024]{1,0:T(8,128)(2,1)} %bitcast.20, bf16[256,3584]{1,0:T(8,128)(2,1)} %bitcast.23, bf16[256,1024]{1,0:T(8,128)(2,1)} %bitcast.26, bf16[64,3584]{1,0:T(8,128)(2,1)} %bitcast.29, ...), custom_call_target="tpu_custom_call" | custom-call | flops 377487360 | bytes 6488064 | tf_op jit(solution)/shard_map/project_2_1/pallas_call | solution.py:115
  11.6 0.1 collective-permute-start.1
  11.7 0.6 %collective-permute-start.2 = (f32[320,128]{1,0:T(8,128)S(1)}, f32[320,128]{1,0:T(8,128)S(1)}, u32[]{:S(2)}, u32[]{:S(2)}) collective-permute-start(f32[320,128]{1,0:T(8,128)S(1)} %get-tuple-element.23), channel_id=1, source_target_pairs={{0,1},{1,0},{2,3},{3,2},{4,5},{5,4},{6,7},{7,6},{8,9},{9,8},{10,11... | collective-permute-start | bytes 491528 | tf_op jit(solution)/shard_map/ppermute | solution.py:35
  12.2 0.0 copy-start
  12.2 0.0 copy-start.1
  12.2 2.7 %project_0.1 = f32[320,128]{1,0:T(8,128)S(1)} custom-call(s32[1]{0:T(128)} %bitcast.1.at_ref, bf16[1024,3584]{1,0:T(8,128)(2,1)} %bitcast.18, bf16[1024,1024]{1,0:T(8,128)(2,1)} %bitcast.21, bf16[256,3584]{1,0:T(8,128)(2,1)} %bitcast.24, bf16[256,1024]{1,0:T(8,128)(2,1)} %bitcast.27, bf16[64,3584]{1,0:T(8,128)(2,1)} %bitcast.30, bf16[64,1024]{1,0:T(8,128)(2,1)} %bitcast.33), custom_call_target="tpu_custom_call" | custom-call | flops 188743680 | bytes 3538944 | tf_op jit(solution)/shard_map/project_0/pallas_call | solution.py:115
  15.0 0.0 collective-permute-done
  15.0 6.7 %collective-permute-done.1.refs_1_ = f32[320,128]{1,0:T(8,128)S(1)} collective-permute-done((f32[320,128]{1,0:T(8,128)S(1)}, f32[320,128]{1,0:T(8,128)S(1)}, u32[]{:S(2)}, u32[]{:S(2)}) %collective-permute-start.1) | collective-permute-done | bytes 163872 | tf_op jit(solution)/shard_map/ppermute | solution.py:35
  21.7 0.0 collective-permute-done.2.refs_2_
  21.7 0.0 copy-done
  21.7 0.0 copy-done.1
  21.7 0.4 outer.1
  22.1 0.1 collective-permute-start.3
  22.2 1.2 %collective-permute-done.3 = f32[2,7,8,128]{3,2,1,0:T(8,128)S(1)} collective-permute-done((f32[2,7,8,128]{3,2,1,0:T(8,128)S(1)}, f32[2,7,8,128]{3,2,1,0:T(8,128)S(1)}, u32[]{:S(2)}, u32[]{:S(2)}) %collective-permute-start.3) | collective-permute-done | bytes 57376 | tf_op jit(solution)/shard_map/ppermute | solution.py:35
  23.5 1.3 %collective-permute-start.4 = (f32[9,8,128]{2,1,0:T(8,128)S(1)}, f32[9,8,128]{2,1,0:T(8,128)S(1)}, u32[]{:S(2)}, u32[]{:S(2)}) collective-permute-start(f32[9,8,128]{2,1,0:T(8,128)S(1)} %get-tuple-element.32), channel_id=1, source_target_pairs={{0,12},{1,13},{2,14},{3,15},{4,8},{5,9},{6,10},{7,11},{8,4},{9,5},... | collective-permute-start | bytes 110600 | tf_op jit(solution)/shard_map/ppermute | solution.py:35
  24.8 2.2 %collective-permute-done.4 = f32[9,8,128]{2,1,0:T(8,128)S(1)} collective-permute-done((f32[9,8,128]{2,1,0:T(8,128)S(1)}, f32[9,8,128]{2,1,0:T(8,128)S(1)}, u32[]{:S(2)}, u32[]{:S(2)}) %collective-permute-start.4) | collective-permute-done | bytes 36896 | tf_op jit(solution)/shard_map/ppermute | solution.py:35
  27.0 1.3 %collective-permute-start.5 = (f32[13,8,128]{2,1,0:T(8,128)S(1)}, f32[13,8,128]{2,1,0:T(8,128)S(1)}, u32[]{:S(2)}, u32[]{:S(2)}) collective-permute-start(f32[13,8,128]{2,1,0:T(8,128)S(1)} %pad_maximum_fusion.2), channel_id=1, source_target_pairs={{0,20},{1,21},{2,22},{3,23},{4,16},{5,17},{6,18},{7,19},{8,28},{9,... | collective-permute-start | bytes 159752 | tf_op jit(solution)/shard_map/ppermute | solution.py:35
  28.4 0.0 collective-permute-start.6
  28.4 3.0 %collective-permute-start.7 = (f32[8,8,128]{2,1,0:T(8,128)S(1)}, f32[8,8,128]{2,1,0:T(8,128)S(1)}, u32[]{:S(2)}, u32[]{:S(2)}) collective-permute-start(f32[8,8,128]{2,1,0:T(8,128)S(1)} %pad_maximum_fusion.4), channel_id=1, source_target_pairs={{0,2},{1,3},{2,0},{3,1},{4,6},{5,7},{6,4},{7,5},{8,10},{9,11},{10,... | collective-permute-start | bytes 98312 | tf_op jit(solution)/shard_map/ppermute | solution.py:35
  31.4 0.0 collective-permute-done.5
  31.5 2.0 %collective-permute-start.9 = (f32[20,8,128]{2,1,0:T(8,128)S(1)}, f32[20,8,128]{2,1,0:T(8,128)S(1)}, u32[]{:S(2)}, u32[]{:S(2)}) collective-permute-start(f32[20,8,128]{2,1,0:T(8,128)S(1)} %pad_maximum_fusion.whole_ref.refs_0_), channel_id=1, source_target_pairs={{0,3},{1,2},{2,1},{3,0},{4,7},{5,6},{6,5},{7,4},{8,11},{9,10},{10,... | collective-permute-start | bytes 245768 | tf_op jit(solution)/shard_map/ppermute | solution.py:35
  33.5 0.0 collective-permute-start.8
  33.5 0.0 collective-permute-done.6.refs_0_
  33.5 0.0 collective-permute-done.7.refs_1_
  33.5 2.8 %collective-permute-start.10 = (f32[12,8,128]{2,1,0:T(8,128)S(1)}, f32[12,8,128]{2,1,0:T(8,128)S(1)}, u32[]{:S(2)}, u32[]{:S(2)}) collective-permute-start(f32[12,8,128]{2,1,0:T(8,128)S(1)} %pad_maximum_fusion.3), channel_id=1, source_target_pairs={{0,2},{1,3},{2,0},{3,1},{4,6},{5,7},{6,4},{7,5},{8,10},{9,11},{10,... | collective-permute-start | bytes 147464 | tf_op jit(solution)/shard_map/ppermute | solution.py:35
  36.4 0.1 rows.1.first_ref
  36.4 3.3 %collective-permute-done.8.refs_1_ = f32[12,8,128]{2,1,0:T(8,128)S(1)} collective-permute-done((f32[12,8,128]{2,1,0:T(8,128)S(1)}, f32[12,8,128]{2,1,0:T(8,128)S(1)}, u32[]{:S(2)}, u32[]{:S(2)}) %collective-permute-start.8) | collective-permute-done | bytes 49184 | tf_op jit(solution)/shard_map/ppermute | solution.py:35
  39.7 0.0 collective-permute-done.10.refs_3_
  39.7 0.0 collective-permute-done.9.refs_2_
  39.7 0.4 gram.1
  40.1 1.1 %collective-permute-start.11 = (f32[48,128]{1,0:T(8,128)S(1)}, f32[48,128]{1,0:T(8,128)S(1)}, u32[]{:S(2)}, u32[]{:S(2)}) collective-permute-start(f32[48,128]{1,0:T(8,128)S(1)} %gram.1), channel_id=1, source_target_pairs={{0,12},{1,13},{2,14},{3,15},{4,8},{5,9},{6,10},{7,11},{8,4},{9,5},... | collective-permute-start | bytes 73736 | tf_op jit(solution)/shard_map/ppermute | solution.py:35
  41.2 2.5 %collective-permute-done.11 = f32[48,128]{1,0:T(8,128)S(1)} collective-permute-done((f32[48,128]{1,0:T(8,128)S(1)}, f32[48,128]{1,0:T(8,128)S(1)}, u32[]{:S(2)}, u32[]{:S(2)}) %collective-permute-start.11) | collective-permute-done | bytes 24608 | tf_op jit(solution)/shard_map/ppermute | solution.py:35
  43.7 0.1 collective-permute-start.12
  43.8 1.1 %collective-permute-done.12.two_ref = f32[48,128]{1,0:T(8,128)S(1)} collective-permute-done((f32[48,128]{1,0:T(8,128)S(1)}, f32[48,128]{1,0:T(8,128)S(1)}, u32[]{:S(2)}, u32[]{:S(2)}) %collective-permute-start.12) | collective-permute-done | bytes 24608 | tf_op jit(solution)/shard_map/ppermute | solution.py:35
  44.9 1.3 %solve.1 = f32[2,16]{1,0:T(2,128)} custom-call(s32[1]{0:T(128)} %bitcast.low_ref, f32[48,128]{1,0:T(8,128)S(1)} %add.27.one_ref, f32[48,128]{1,0:T(8,128)S(1)} %collective-permute-done.12.two_ref), custom_call_target="tpu_custom_call" | custom-call | tf_op jit(solution)/shard_map/solve/pallas_call | solution.py:401
  (16 shorter events, 0.1 us)
Async XLA Ops:
  2.7 12.3 %collective-permute-start = (f32[320,128]{1,0:T(8,128)S(1)}, f32[320,128]{1,0:T(8,128)S(1)}, u32[]{:S(2)}, u32[]{:S(2)}) collective-permute-start(f32[320,128]{1,0:T(8,128)S(1)} %project_3.1), channel_id=1, source_target_pairs={{0,3},{1,2},{2,1},{3,0},{4,7},{5,6},{6,5},{7,4},{8,11},{9,10},{10,... | collective-permute-start | bytes 491528 | tf_op jit(solution)/shard_map/ppermute | solution.py:35
  11.6 10.1 %collective-permute-start.1 = (f32[320,128]{1,0:T(8,128)S(1)}, f32[320,128]{1,0:T(8,128)S(1)}, u32[]{:S(2)}, u32[]{:S(2)}) collective-permute-start(f32[320,128]{1,0:T(8,128)S(1)} %get-tuple-element.22), channel_id=1, source_target_pairs={{0,2},{1,3},{2,0},{3,1},{4,6},{5,7},{6,4},{7,5},{8,10},{9,11},{10,... | collective-permute-start | bytes 491528 | tf_op jit(solution)/shard_map/ppermute | solution.py:35
  11.7 10.0 %collective-permute-start.2 = (f32[320,128]{1,0:T(8,128)S(1)}, f32[320,128]{1,0:T(8,128)S(1)}, u32[]{:S(2)}, u32[]{:S(2)}) collective-permute-start(f32[320,128]{1,0:T(8,128)S(1)} %get-tuple-element.23), channel_id=1, source_target_pairs={{0,1},{1,0},{2,3},{3,2},{4,5},{5,4},{6,7},{7,6},{8,9},{9,8},{10,11... | collective-permute-start | bytes 491528 | tf_op jit(solution)/shard_map/ppermute | solution.py:35
  12.2 9.5 %copy-start = (s32[16,16]{1,0:T(8,128)S(1)}, s32[16,16]{1,0:T(8,128)}, u32[]{:S(2)}) copy-start(s32[16,16]{1,0:T(8,128)} %qids_ref.1) | copy-start | bytes 3076
  12.2 9.5 %copy-start.1 = (s32[8,128]{1,0:T(8,128)S(1)}, s32[8,128]{1,0:T(8,128)}, u32[]{:S(2)}) copy-start(s32[8,128]{1,0:T(8,128)} %ids_ref.1) | copy-start | bytes 12292
  22.1 1.3 %collective-permute-start.3 = (f32[2,7,8,128]{3,2,1,0:T(8,128)S(1)}, f32[2,7,8,128]{3,2,1,0:T(8,128)S(1)}, u32[]{:S(2)}, u32[]{:S(2)}) collective-permute-start(f32[2,7,8,128]{3,2,1,0:T(8,128)S(1)} %get-tuple-element.25), channel_id=1, source_target_pairs={{0,4},{1,5},{2,6},{3,7},{4,0},{5,1},{6,2},{7,3},{8,12},{9,13},{10,... | collective-permute-start | bytes 172040 | tf_op jit(solution)/shard_map/ppermute | solution.py:35
  23.5 3.5 %collective-permute-start.4 = (f32[9,8,128]{2,1,0:T(8,128)S(1)}, f32[9,8,128]{2,1,0:T(8,128)S(1)}, u32[]{:S(2)}, u32[]{:S(2)}) collective-permute-start(f32[9,8,128]{2,1,0:T(8,128)S(1)} %get-tuple-element.32), channel_id=1, source_target_pairs={{0,12},{1,13},{2,14},{3,15},{4,8},{5,9},{6,10},{7,11},{8,4},{9,5},... | collective-permute-start | bytes 110600 | tf_op jit(solution)/shard_map/ppermute | solution.py:35
  27.0 4.4 %collective-permute-start.5 = (f32[13,8,128]{2,1,0:T(8,128)S(1)}, f32[13,8,128]{2,1,0:T(8,128)S(1)}, u32[]{:S(2)}, u32[]{:S(2)}) collective-permute-start(f32[13,8,128]{2,1,0:T(8,128)S(1)} %pad_maximum_fusion.2), channel_id=1, source_target_pairs={{0,20},{1,21},{2,22},{3,23},{4,16},{5,17},{6,18},{7,19},{8,28},{9,... | collective-permute-start | bytes 159752 | tf_op jit(solution)/shard_map/ppermute | solution.py:35
  28.4 5.1 %collective-permute-start.6 = (f32[8,8,128]{2,1,0:T(8,128)S(1)}, f32[8,8,128]{2,1,0:T(8,128)S(1)}, u32[]{:S(2)}, u32[]{:S(2)}) collective-permute-start(f32[8,8,128]{2,1,0:T(8,128)S(1)} %pad_maximum_fusion.4), channel_id=1, source_target_pairs={{0,1},{1,0},{2,3},{3,2},{4,5},{5,4},{6,7},{7,6},{8,9},{9,8},{10,11... | collective-permute-start | bytes 98312 | tf_op jit(solution)/shard_map/ppermute | solution.py:35
  28.4 5.1 %collective-permute-start.7 = (f32[8,8,128]{2,1,0:T(8,128)S(1)}, f32[8,8,128]{2,1,0:T(8,128)S(1)}, u32[]{:S(2)}, u32[]{:S(2)}) collective-permute-start(f32[8,8,128]{2,1,0:T(8,128)S(1)} %pad_maximum_fusion.4), channel_id=1, source_target_pairs={{0,2},{1,3},{2,0},{3,1},{4,6},{5,7},{6,4},{7,5},{8,10},{9,11},{10,... | collective-permute-start | bytes 98312 | tf_op jit(solution)/shard_map/ppermute | solution.py:35
  31.5 8.2 %collective-permute-start.9 = (f32[20,8,128]{2,1,0:T(8,128)S(1)}, f32[20,8,128]{2,1,0:T(8,128)S(1)}, u32[]{:S(2)}, u32[]{:S(2)}) collective-permute-start(f32[20,8,128]{2,1,0:T(8,128)S(1)} %pad_maximum_fusion.whole_ref.refs_0_), channel_id=1, source_target_pairs={{0,3},{1,2},{2,1},{3,0},{4,7},{5,6},{6,5},{7,4},{8,11},{9,10},{10,... | collective-permute-start | bytes 245768 | tf_op jit(solution)/shard_map/ppermute | solution.py:35
  33.5 6.2 %collective-permute-start.8 = (f32[12,8,128]{2,1,0:T(8,128)S(1)}, f32[12,8,128]{2,1,0:T(8,128)S(1)}, u32[]{:S(2)}, u32[]{:S(2)}) collective-permute-start(f32[12,8,128]{2,1,0:T(8,128)S(1)} %pad_maximum_fusion.3), channel_id=1, source_target_pairs={{0,1},{1,0},{2,3},{3,2},{4,5},{5,4},{6,7},{7,6},{8,9},{9,8},{10,11... | collective-permute-start | bytes 147464 | tf_op jit(solution)/shard_map/ppermute | solution.py:35
  33.5 6.2 %collective-permute-start.10 = (f32[12,8,128]{2,1,0:T(8,128)S(1)}, f32[12,8,128]{2,1,0:T(8,128)S(1)}, u32[]{:S(2)}, u32[]{:S(2)}) collective-permute-start(f32[12,8,128]{2,1,0:T(8,128)S(1)} %pad_maximum_fusion.3), channel_id=1, source_target_pairs={{0,2},{1,3},{2,0},{3,1},{4,6},{5,7},{6,4},{7,5},{8,10},{9,11},{10,... | collective-permute-start | bytes 147464 | tf_op jit(solution)/shard_map/ppermute | solution.py:35
  40.1 3.5 %collective-permute-start.11 = (f32[48,128]{1,0:T(8,128)S(1)}, f32[48,128]{1,0:T(8,128)S(1)}, u32[]{:S(2)}, u32[]{:S(2)}) collective-permute-start(f32[48,128]{1,0:T(8,128)S(1)} %gram.1), channel_id=1, source_target_pairs={{0,12},{1,13},{2,14},{3,15},{4,8},{5,9},{6,10},{7,11},{8,4},{9,5},... | collective-permute-start | bytes 73736 | tf_op jit(solution)/shard_map/ppermute | solution.py:35
  43.7 1.2 %collective-permute-start.12 = (f32[48,128]{1,0:T(8,128)S(1)}, f32[48,128]{1,0:T(8,128)S(1)}, u32[]{:S(2)}, u32[]{:S(2)}) collective-permute-start(f32[48,128]{1,0:T(8,128)S(1)} %add.27.one_ref), channel_id=1, source_target_pairs={{0,4},{1,5},{2,6},{3,7},{4,0},{5,1},{6,2},{7,3},{8,12},{9,13},{10,... | collective-permute-start | bytes 73736 | tf_op jit(solution)/shard_map/ppermute | solution.py:35

commit v9 on v8

--- a/solution.py
+++ b/solution.py
@@ -75,25 +75,47 @@
     held_rows = hid.shape[0] // 2 if by_rows else hid.shape[0]
 
     def multiply(*sums):
-        count = 0
-        for side, start, size, copies in chunks:
+        used = [0] * len(sums)
+        for side in (1, 0):
             _, _, buf, _, held = sides[side]
-            for copy in copies:
-                copy.wait()
-            for col in range(start, start + size, tile):
+            mine = [chunk for chunk in chunks if chunk[0] == side]
+            tiles = range(0, buf.shape[1], tile)
+            turns = [
+                list(tiles) if by_rows else list(tiles)[unit :: len(sums)]
+                for unit in range(len(sums))
+            ]
+
+            def push(unit, place):
+                if place >= len(turns[unit]):
+                    return
+                col = turns[unit][place]
                 weight = [held[:, col : col + tile]]
                 if side:
                     weight.insert(0, jnp.zeros((side * rank, tile), held.dtype))
                 weight.append(jnp.zeros((tile - (side + 1) * rank, tile), held.dtype))
                 weight = jnp.concatenate(weight, axis=0)
-                units = range(len(sums)) if by_rows else (count % len(sums),)
-                turn = (count if by_rows else count // len(sums)) % 2
-                count += 1
-                for unit in units:
-                    first = unit * held_rows if by_rows else 0
-                    pltpu.matmul_push_rhs(weight, turn, unit, transpose=True)
-                    tokens = buf[first : first + held_rows, col : col + tile]
-                    pltpu.matmul_acc_lhs(sums[unit], tokens, load_staged_rhs=turn)
+                pltpu.matmul_push_rhs(weight, (used[unit] + place) % 2, unit, transpose=True)
+
+            mine[0][3][0].wait()
+            for place in range(2):
+                for unit in range(len(sums)):
+                    push(unit, place)
+            for _, start, size, copies in mine:
+                for copy in copies[0 if start else 1 :]:
+                    copy.wait()
+                for col in range(start, start + size, tile):
+                    for unit, acc in enumerate(sums):
+                        if col not in turns[unit]:
+                            continue
+                        place = turns[unit].index(col)
+                        first = unit * held_rows if by_rows else 0
+                        tokens = buf[first : first + held_rows, col : col + tile]
+                        pltpu.matmul_acc_lhs(
+                            acc, tokens, load_staged_rhs=(used[unit] + place) % 2
+                        )
+                        push(unit, place + 2)
+            for unit in range(len(sums)):
+                used[unit] += len(turns[unit])
         total = [pltpu.matmul_pop(acc)[:, : 2 * rank] for acc in sums]
         total = jnp.concatenate(total, axis=0) if by_rows else sum(total)
         for slot, ref in enumerate(out_refs):

time: 46.3 us -> 46.1 us (level)
  Pallas kernels: 11.4 us -> 10.8 us
    pallas_call x3, Pallas kernels: 9.17 us -> 8.61 us  [project(): call(functools.partial(project_kernel, mesh, parts, hops, tile), [jax.Sha...]
  transfers between devices with their start and end apart: 13 -> 13, of which waited for: 6 -> 6; matrix products, arithmetic and copies ran while one was open for 0% -> 0% of each run, Pallas kernels for 14% -> 13%
where the time goes in v9:
time: 46.1 us; the launch traced here: 46 us
  starting transfers between devices  17.5 us (38%)
  waiting for transfers between devices  17.3 us (38%)
  Pallas kernels  10.8 us (23%)
    ppermute x13, starting transfers between devices, swap(): lax.ppermute(value, ('dp', 'tensor'), [(i, i ^ flip) for i in range(group...  17.5 us
    ppermute x13, waiting for transfers between devices, swap(): lax.ppermute(value, ('dp', 'tensor'), [(i, i ^ flip) for i in range(group...  17.3 us
    pallas_call x3, Pallas kernels, project(): call(functools.partial(project_kernel, mesh, parts, hops, tile), [jax.Sha...  8.61 us
    pallas_call x1, Pallas kernels, per_device(): call(functools.partial(solve_kernel, ntrain, rank * rank, share), jax.Sha...  1.29 us
  transfers between devices with their start and end apart: 13, of which 6 were waited for; matrix products, arithmetic and copies ran while one was open for 0% of the time, Pallas kernels for 13%

profile of v9, /device:TPU:0, one launch (start us, length us, event | category | flops | bytes accessed | tf_op | source)
XLA Modules:
  0.0 46.0 jit_solution(15345380231345292535)
XLA Ops:
  0.0 2.5 %project_3.1 = f32[320,128]{1,0:T(8,128)S(1)} custom-call(s32[1]{0:T(128)} %bitcast.1.at_ref, bf16[1024,3584]{1,0:T(8,128)(2,1)} %bitcast.16, bf16[1024,1024]{1,0:T(8,128)(2,1)} %bitcast.19, bf16[256,3584]{1,0:T(8,128)(2,1)} %bitcast.22, bf16[256,1024]{1,0:T(8,128)(2,1)} %bitcast.25, bf16[64,3584]{1,0:T(8,128)(2,1)} %bitcast.28, bf16[64,1024]{1,0:T(8,128)(2,1)} %bitcast.31), custom_call_target="tpu_custom_call" | custom-call | flops 188743680 | bytes 3538944 | tf_op jit(solution)/shard_map/project_3/pallas_call | solution.py:137
  2.5 5.1 %collective-permute-start = (f32[320,128]{1,0:T(8,128)S(1)}, f32[320,128]{1,0:T(8,128)S(1)}, u32[]{:S(2)}, u32[]{:S(2)}) collective-permute-start(f32[320,128]{1,0:T(8,128)S(1)} %project_3.1), channel_id=1, source_target_pairs={{0,3},{1,2},{2,1},{3,0},{4,7},{5,6},{6,5},{7,4},{8,11},{9,10},{10,... | collective-permute-start | bytes 491528 | tf_op jit(solution)/shard_map/ppermute | solution.py:35
  7.6 3.6 %project_2_1.1 = (f32[320,128]{1,0:T(8,128)S(1)}, f32[320,128]{1,0:T(8,128)S(1)}) custom-call(s32[1]{0:T(128)} %bitcast.1.at_ref, bf16[1024,3584]{1,0:T(8,128)(2,1)} %bitcast.17, bf16[1024,1024]{1,0:T(8,128)(2,1)} %bitcast.20, bf16[256,3584]{1,0:T(8,128)(2,1)} %bitcast.23, bf16[256,1024]{1,0:T(8,128)(2,1)} %bitcast.26, bf16[64,3584]{1,0:T(8,128)(2,1)} %bitcast.29, ...), custom_call_target="tpu_custom_call" | custom-call | flops 377487360 | bytes 6488064 | tf_op jit(solution)/shard_map/project_2_1/pallas_call | solution.py:137
  11.2 0.1 collective-permute-start.1
  11.3 0.6 %collective-permute-start.2 = (f32[320,128]{1,0:T(8,128)S(1)}, f32[320,128]{1,0:T(8,128)S(1)}, u32[]{:S(2)}, u32[]{:S(2)}) collective-permute-start(f32[320,128]{1,0:T(8,128)S(1)} %get-tuple-element.23), channel_id=1, source_target_pairs={{0,1},{1,0},{2,3},{3,2},{4,5},{5,4},{6,7},{7,6},{8,9},{9,8},{10,11... | collective-permute-start | bytes 491528 | tf_op jit(solution)/shard_map/ppermute | solution.py:35
  11.9 0.0 copy-start
  11.9 0.0 copy-start.1
  11.9 2.5 %project_0.1 = f32[320,128]{1,0:T(8,128)S(1)} custom-call(s32[1]{0:T(128)} %bitcast.1.at_ref, bf16[1024,3584]{1,0:T(8,128)(2,1)} %bitcast.18, bf16[1024,1024]{1,0:T(8,128)(2,1)} %bitcast.21, bf16[256,3584]{1,0:T(8,128)(2,1)} %bitcast.24, bf16[256,1024]{1,0:T(8,128)(2,1)} %bitcast.27, bf16[64,3584]{1,0:T(8,128)(2,1)} %bitcast.30, bf16[64,1024]{1,0:T(8,128)(2,1)} %bitcast.33), custom_call_target="tpu_custom_call" | custom-call | flops 188743680 | bytes 3538944 | tf_op jit(solution)/shard_map/project_0/pallas_call | solution.py:137
  14.4 0.0 collective-permute-done
  14.5 7.1 %collective-permute-done.1.refs_1_ = f32[320,128]{1,0:T(8,128)S(1)} collective-permute-done((f32[320,128]{1,0:T(8,128)S(1)}, f32[320,128]{1,0:T(8,128)S(1)}, u32[]{:S(2)}, u32[]{:S(2)}) %collective-permute-start.1) | collective-permute-done | bytes 163872 | tf_op jit(solution)/shard_map/ppermute | solution.py:35
  21.5 0.0 collective-permute-done.2.refs_2_
  21.5 0.0 copy-done
  21.5 0.0 copy-done.1
  21.5 0.4 outer.1
  22.0 0.1 collective-permute-start.3
  22.0 1.2 %collective-permute-done.3 = f32[2,7,8,128]{3,2,1,0:T(8,128)S(1)} collective-permute-done((f32[2,7,8,128]{3,2,1,0:T(8,128)S(1)}, f32[2,7,8,128]{3,2,1,0:T(8,128)S(1)}, u32[]{:S(2)}, u32[]{:S(2)}) %collective-permute-start.3) | collective-permute-done | bytes 57376 | tf_op jit(solution)/shard_map/ppermute | solution.py:35
  23.3 1.3 %collective-permute-start.4 = (f32[9,8,128]{2,1,0:T(8,128)S(1)}, f32[9,8,128]{2,1,0:T(8,128)S(1)}, u32[]{:S(2)}, u32[]{:S(2)}) collective-permute-start(f32[9,8,128]{2,1,0:T(8,128)S(1)} %get-tuple-element.32), channel_id=1, source_target_pairs={{0,12},{1,13},{2,14},{3,15},{4,8},{5,9},{6,10},{7,11},{8,4},{9,5},... | collective-permute-start | bytes 110600 | tf_op jit(solution)/shard_map/ppermute | solution.py:35
  24.6 2.2 %collective-permute-done.4 = f32[9,8,128]{2,1,0:T(8,128)S(1)} collective-permute-done((f32[9,8,128]{2,1,0:T(8,128)S(1)}, f32[9,8,128]{2,1,0:T(8,128)S(1)}, u32[]{:S(2)}, u32[]{:S(2)}) %collective-permute-start.4) | collective-permute-done | bytes 36896 | tf_op jit(solution)/shard_map/ppermute | solution.py:35
  26.9 1.4 %collective-permute-start.5 = (f32[13,8,128]{2,1,0:T(8,128)S(1)}, f32[13,8,128]{2,1,0:T(8,128)S(1)}, u32[]{:S(2)}, u32[]{:S(2)}) collective-permute-start(f32[13,8,128]{2,1,0:T(8,128)S(1)} %pad_maximum_fusion.2), channel_id=1, source_target_pairs={{0,20},{1,21},{2,22},{3,23},{4,16},{5,17},{6,18},{7,19},{8,28},{9,... | collective-permute-start | bytes 159752 | tf_op jit(solution)/shard_map/ppermute | solution.py:35
  28.2 0.0 collective-permute-start.6
  28.2 3.0 %collective-permute-start.7 = (f32[8,8,128]{2,1,0:T(8,128)S(1)}, f32[8,8,128]{2,1,0:T(8,128)S(1)}, u32[]{:S(2)}, u32[]{:S(2)}) collective-permute-start(f32[8,8,128]{2,1,0:T(8,128)S(1)} %pad_maximum_fusion.4), channel_id=1, source_target_pairs={{0,2},{1,3},{2,0},{3,1},{4,6},{5,7},{6,4},{7,5},{8,10},{9,11},{10,... | collective-permute-start | bytes 98312 | tf_op jit(solution)/shard_map/ppermute | solution.py:35
  31.2 0.0 collective-permute-done.5
  31.3 2.0 %collective-permute-start.9 = (f32[20,8,128]{2,1,0:T(8,128)S(1)}, f32[20,8,128]{2,1,0:T(8,128)S(1)}, u32[]{:S(2)}, u32[]{:S(2)}) collective-permute-start(f32[20,8,128]{2,1,0:T(8,128)S(1)} %pad_maximum_fusion.whole_ref.refs_0_), channel_id=1, source_target_pairs={{0,3},{1,2},{2,1},{3,0},{4,7},{5,6},{6,5},{7,4},{8,11},{9,10},{10,... | collective-permute-start | bytes 245768 | tf_op jit(solution)/shard_map/ppermute | solution.py:35
  33.3 0.0 collective-permute-start.8
  33.3 0.0 collective-permute-done.6.refs_0_
  33.3 0.0 collective-permute-done.7.refs_1_
  33.3 2.8 %collective-permute-start.10 = (f32[12,8,128]{2,1,0:T(8,128)S(1)}, f32[12,8,128]{2,1,0:T(8,128)S(1)}, u32[]{:S(2)}, u32[]{:S(2)}) collective-permute-start(f32[12,8,128]{2,1,0:T(8,128)S(1)} %pad_maximum_fusion.3), channel_id=1, source_target_pairs={{0,2},{1,3},{2,0},{3,1},{4,6},{5,7},{6,4},{7,5},{8,10},{9,11},{10,... | collective-permute-start | bytes 147464 | tf_op jit(solution)/shard_map/ppermute | solution.py:35
  36.2 0.1 rows.1.first_ref
  36.2 3.3 %collective-permute-done.8.refs_1_ = f32[12,8,128]{2,1,0:T(8,128)S(1)} collective-permute-done((f32[12,8,128]{2,1,0:T(8,128)S(1)}, f32[12,8,128]{2,1,0:T(8,128)S(1)}, u32[]{:S(2)}, u32[]{:S(2)}) %collective-permute-start.8) | collective-permute-done | bytes 49184 | tf_op jit(solution)/shard_map/ppermute | solution.py:35
  39.5 0.0 collective-permute-done.10.refs_3_
  39.5 0.0 collective-permute-done.9.refs_2_
  39.5 0.4 gram.1
  40.0 1.0 %collective-permute-start.11 = (f32[48,128]{1,0:T(8,128)S(1)}, f32[48,128]{1,0:T(8,128)S(1)}, u32[]{:S(2)}, u32[]{:S(2)}) collective-permute-start(f32[48,128]{1,0:T(8,128)S(1)} %gram.1), channel_id=1, source_target_pairs={{0,12},{1,13},{2,14},{3,15},{4,8},{5,9},{6,10},{7,11},{8,4},{9,5},... | collective-permute-start | bytes 73736 | tf_op jit(solution)/shard_map/ppermute | solution.py:35
  41.0 2.5 %collective-permute-done.11 = f32[48,128]{1,0:T(8,128)S(1)} collective-permute-done((f32[48,128]{1,0:T(8,128)S(1)}, f32[48,128]{1,0:T(8,128)S(1)}, u32[]{:S(2)}, u32[]{:S(2)}) %collective-permute-start.11) | collective-permute-done | bytes 24608 | tf_op jit(solution)/shard_map/ppermute | solution.py:35
  43.5 0.1 collective-permute-start.12
  43.6 1.1 %collective-permute-done.12.two_ref = f32[48,128]{1,0:T(8,128)S(1)} collective-permute-done((f32[48,128]{1,0:T(8,128)S(1)}, f32[48,128]{1,0:T(8,128)S(1)}, u32[]{:S(2)}, u32[]{:S(2)}) %collective-permute-start.12) | collective-permute-done | bytes 24608 | tf_op jit(solution)/shard_map/ppermute | solution.py:35
  44.7 1.3 %solve.1 = f32[2,16]{1,0:T(2,128)} custom-call(s32[1]{0:T(128)} %bitcast.low_ref, f32[48,128]{1,0:T(8,128)S(1)} %add.27.one_ref, f32[48,128]{1,0:T(8,128)S(1)} %collective-permute-done.12.two_ref), custom_call_target="tpu_custom_call" | custom-call | tf_op jit(solution)/shard_map/solve/pallas_call | solution.py:423
  (16 shorter events, 0.1 us)
Async XLA Ops:
  2.5 11.9 %collective-permute-start = (f32[320,128]{1,0:T(8,128)S(1)}, f32[320,128]{1,0:T(8,128)S(1)}, u32[]{:S(2)}, u32[]{:S(2)}) collective-permute-start(f32[320,128]{1,0:T(8,128)S(1)} %project_3.1), channel_id=1, source_target_pairs={{0,3},{1,2},{2,1},{3,0},{4,7},{5,6},{6,5},{7,4},{8,11},{9,10},{10,... | collective-permute-start | bytes 491528 | tf_op jit(solution)/shard_map/ppermute | solution.py:35
  11.2 10.3 %collective-permute-start.1 = (f32[320,128]{1,0:T(8,128)S(1)}, f32[320,128]{1,0:T(8,128)S(1)}, u32[]{:S(2)}, u32[]{:S(2)}) collective-permute-start(f32[320,128]{1,0:T(8,128)S(1)} %get-tuple-element.22), channel_id=1, source_target_pairs={{0,2},{1,3},{2,0},{3,1},{4,6},{5,7},{6,4},{7,5},{8,10},{9,11},{10,... | collective-permute-start | bytes 491528 | tf_op jit(solution)/shard_map/ppermute | solution.py:35
  11.3 10.2 %collective-permute-start.2 = (f32[320,128]{1,0:T(8,128)S(1)}, f32[320,128]{1,0:T(8,128)S(1)}, u32[]{:S(2)}, u32[]{:S(2)}) collective-permute-start(f32[320,128]{1,0:T(8,128)S(1)} %get-tuple-element.23), channel_id=1, source_target_pairs={{0,1},{1,0},{2,3},{3,2},{4,5},{5,4},{6,7},{7,6},{8,9},{9,8},{10,11... | collective-permute-start | bytes 491528 | tf_op jit(solution)/shard_map/ppermute | solution.py:35
  11.9 9.6 %copy-start = (s32[16,16]{1,0:T(8,128)S(1)}, s32[16,16]{1,0:T(8,128)}, u32[]{:S(2)}) copy-start(s32[16,16]{1,0:T(8,128)} %qids_ref.1) | copy-start | bytes 3076
  11.9 9.6 %copy-start.1 = (s32[8,128]{1,0:T(8,128)S(1)}, s32[8,128]{1,0:T(8,128)}, u32[]{:S(2)}) copy-start(s32[8,128]{1,0:T(8,128)} %ids_ref.1) | copy-start | bytes 12292
  22.0 1.3 %collective-permute-start.3 = (f32[2,7,8,128]{3,2,1,0:T(8,128)S(1)}, f32[2,7,8,128]{3,2,1,0:T(8,128)S(1)}, u32[]{:S(2)}, u32[]{:S(2)}) collective-permute-start(f32[2,7,8,128]{3,2,1,0:T(8,128)S(1)} %get-tuple-element.25), channel_id=1, source_target_pairs={{0,4},{1,5},{2,6},{3,7},{4,0},{5,1},{6,2},{7,3},{8,12},{9,13},{10,... | collective-permute-start | bytes 172040 | tf_op jit(solution)/shard_map/ppermute | solution.py:35
  23.3 3.5 %collective-permute-start.4 = (f32[9,8,128]{2,1,0:T(8,128)S(1)}, f32[9,8,128]{2,1,0:T(8,128)S(1)}, u32[]{:S(2)}, u32[]{:S(2)}) collective-permute-start(f32[9,8,128]{2,1,0:T(8,128)S(1)} %get-tuple-element.32), channel_id=1, source_target_pairs={{0,12},{1,13},{2,14},{3,15},{4,8},{5,9},{6,10},{7,11},{8,4},{9,5},... | collective-permute-start | bytes 110600 | tf_op jit(solution)/shard_map/ppermute | solution.py:35
  26.9 4.4 %collective-permute-start.5 = (f32[13,8,128]{2,1,0:T(8,128)S(1)}, f32[13,8,128]{2,1,0:T(8,128)S(1)}, u32[]{:S(2)}, u32[]{:S(2)}) collective-permute-start(f32[13,8,128]{2,1,0:T(8,128)S(1)} %pad_maximum_fusion.2), channel_id=1, source_target_pairs={{0,20},{1,21},{2,22},{3,23},{4,16},{5,17},{6,18},{7,19},{8,28},{9,... | collective-permute-start | bytes 159752 | tf_op jit(solution)/shard_map/ppermute | solution.py:35
  28.2 5.1 %collective-permute-start.6 = (f32[8,8,128]{2,1,0:T(8,128)S(1)}, f32[8,8,128]{2,1,0:T(8,128)S(1)}, u32[]{:S(2)}, u32[]{:S(2)}) collective-permute-start(f32[8,8,128]{2,1,0:T(8,128)S(1)} %pad_maximum_fusion.4), channel_id=1, source_target_pairs={{0,1},{1,0},{2,3},{3,2},{4,5},{5,4},{6,7},{7,6},{8,9},{9,8},{10,11... | collective-permute-start | bytes 98312 | tf_op jit(solution)/shard_map/ppermute | solution.py:35
  28.2 5.1 %collective-permute-start.7 = (f32[8,8,128]{2,1,0:T(8,128)S(1)}, f32[8,8,128]{2,1,0:T(8,128)S(1)}, u32[]{:S(2)}, u32[]{:S(2)}) collective-permute-start(f32[8,8,128]{2,1,0:T(8,128)S(1)} %pad_maximum_fusion.4), channel_id=1, source_target_pairs={{0,2},{1,3},{2,0},{3,1},{4,6},{5,7},{6,4},{7,5},{8,10},{9,11},{10,... | collective-permute-start | bytes 98312 | tf_op jit(solution)/shard_map/ppermute | solution.py:35
  31.3 8.2 %collective-permute-start.9 = (f32[20,8,128]{2,1,0:T(8,128)S(1)}, f32[20,8,128]{2,1,0:T(8,128)S(1)}, u32[]{:S(2)}, u32[]{:S(2)}) collective-permute-start(f32[20,8,128]{2,1,0:T(8,128)S(1)} %pad_maximum_fusion.whole_ref.refs_0_), channel_id=1, source_target_pairs={{0,3},{1,2},{2,1},{3,0},{4,7},{5,6},{6,5},{7,4},{8,11},{9,10},{10,... | collective-permute-start | bytes 245768 | tf_op jit(solution)/shard_map/ppermute | solution.py:35
  33.3 6.2 %collective-permute-start.8 = (f32[12,8,128]{2,1,0:T(8,128)S(1)}, f32[12,8,128]{2,1,0:T(8,128)S(1)}, u32[]{:S(2)}, u32[]{:S(2)}) collective-permute-start(f32[12,8,128]{2,1,0:T(8,128)S(1)} %pad_maximum_fusion.3), channel_id=1, source_target_pairs={{0,1},{1,0},{2,3},{3,2},{4,5},{5,4},{6,7},{7,6},{8,9},{9,8},{10,11... | collective-permute-start | bytes 147464 | tf_op jit(solution)/shard_map/ppermute | solution.py:35
  33.3 6.2 %collective-permute-start.10 = (f32[12,8,128]{2,1,0:T(8,128)S(1)}, f32[12,8,128]{2,1,0:T(8,128)S(1)}, u32[]{:S(2)}, u32[]{:S(2)}) collective-permute-start(f32[12,8,128]{2,1,0:T(8,128)S(1)} %pad_maximum_fusion.3), channel_id=1, source_target_pairs={{0,2},{1,3},{2,0},{3,1},{4,6},{5,7},{6,4},{7,5},{8,10},{9,11},{10,... | collective-permute-start | bytes 147464 | tf_op jit(solution)/shard_map/ppermute | solution.py:35
  40.0 3.5 %collective-permute-start.11 = (f32[48,128]{1,0:T(8,128)S(1)}, f32[48,128]{1,0:T(8,128)S(1)}, u32[]{:S(2)}, u32[]{:S(2)}) collective-permute-start(f32[48,128]{1,0:T(8,128)S(1)} %gram.1), channel_id=1, source_target_pairs={{0,12},{1,13},{2,14},{3,15},{4,8},{5,9},{6,10},{7,11},{8,4},{9,5},... | collective-permute-start | bytes 73736 | tf_op jit(solution)/shard_map/ppermute | solution.py:35
  43.5 1.2 %collective-permute-start.12 = (f32[48,128]{1,0:T(8,128)S(1)}, f32[48,128]{1,0:T(8,128)S(1)}, u32[]{:S(2)}, u32[]{:S(2)}) collective-permute-start(f32[48,128]{1,0:T(8,128)S(1)} %add.27.one_ref), channel_id=1, source_target_pairs={{0,4},{1,5},{2,6},{3,7},{4,0},{5,1},{6,2},{7,3},{8,12},{9,13},{10,... | collective-permute-start | bytes 73736 | tf_op jit(solution)/shard_map/ppermute | solution.py:35

commit v10 on v9

--- a/solution.py
+++ b/solution.py
@@ -49,11 +49,7 @@
     for side in (1, 0):
         train, query, buf, weight, held = sides[side]
         wide = buf.shape[1]
-        first = wide if side else 4 * tile
-        second = (wide - first + tile) // (2 * tile) * tile
-        for start, size in ((0, first), (first, second), (first + second, wide - first - second)):
-            if not size:
-                continue
+        for start, size in ((0, wide),):
             cols = pl.ds(start, size)
             pairs = [] if start else [(weight, held)]
             for slot, hop in enumerate(hops):

time: 46.1 us -> 46.4 us (level)
  Pallas kernels: 10.8 us -> 12.1 us
  waiting for transfers between devices: 17.3 us -> 16.4 us
    pallas_call x3, Pallas kernels: 8.61 us -> 9.84 us  [project(): call(functools.partial(project_kernel, mesh, parts, hops, tile), [jax.Sha...]
    ppermute x13, waiting for transfers between devices: 17.3 us -> 16.4 us  [swap(): lax.ppermute(value, ('dp', 'tensor'), [(i, i ^ flip) for i in range(group...]
  transfers between devices with their start and end apart: 13 -> 13, of which waited for: 6 -> 6; matrix products, arithmetic and copies ran while one was open for 0% -> 0% of each run, Pallas kernels for 13% -> 15%
where the time goes in v10:
time: 46.4 us; the launch traced here: 46.2 us
  starting transfers between devices  17.5 us (38%)
  waiting for transfers between devices  16.4 us (35%)
  Pallas kernels  12.1 us (26%)
    ppermute x13, starting transfers between devices, swap(): lax.ppermute(value, ('dp', 'tensor'), [(i, i ^ flip) for i in range(group...  17.5 us
    ppermute x13, waiting for transfers between devices, swap(): lax.ppermute(value, ('dp', 'tensor'), [(i, i ^ flip) for i in range(group...  16.4 us
    pallas_call x3, Pallas kernels, project(): call(functools.partial(project_kernel, mesh, parts, hops, tile), [jax.Sha...  9.84 us
    pallas_call x1, Pallas kernels, per_device(): call(functools.partial(solve_kernel, ntrain, rank * rank, share), jax.Sha...  1.29 us
  transfers between devices with their start and end apart: 13, of which 6 were waited for; matrix products, arithmetic and copies ran while one was open for 0% of the time, Pallas kernels for 15%

profile of v10, /device:TPU:0, one launch (start us, length us, event | category | flops | bytes accessed | tf_op | source)
XLA Modules:
  0.0 46.2 jit_solution(4968373696789165415)
XLA Ops:
  0.0 2.8 %project_3.1 = f32[320,128]{1,0:T(8,128)S(1)} custom-call(s32[1]{0:T(128)} %bitcast.1.at_ref, bf16[1024,3584]{1,0:T(8,128)(2,1)} %bitcast.16, bf16[1024,1024]{1,0:T(8,128)(2,1)} %bitcast.19, bf16[256,3584]{1,0:T(8,128)(2,1)} %bitcast.22, bf16[256,1024]{1,0:T(8,128)(2,1)} %bitcast.25, bf16[64,3584]{1,0:T(8,128)(2,1)} %bitcast.28, bf16[64,1024]{1,0:T(8,128)(2,1)} %bitcast.31), custom_call_target="tpu_custom_call" | custom-call | flops 188743680 | bytes 3538944 | tf_op jit(solution)/shard_map/project_3/pallas_call | solution.py:133
  2.8 5.1 %collective-permute-start = (f32[320,128]{1,0:T(8,128)S(1)}, f32[320,128]{1,0:T(8,128)S(1)}, u32[]{:S(2)}, u32[]{:S(2)}) collective-permute-start(f32[320,128]{1,0:T(8,128)S(1)} %project_3.1), channel_id=1, source_target_pairs={{0,3},{1,2},{2,1},{3,0},{4,7},{5,6},{6,5},{7,4},{8,11},{9,10},{10,... | collective-permute-start | bytes 491528 | tf_op jit(solution)/shard_map/ppermute | solution.py:35
  7.9 4.3 %project_2_1.1 = (f32[320,128]{1,0:T(8,128)S(1)}, f32[320,128]{1,0:T(8,128)S(1)}) custom-call(s32[1]{0:T(128)} %bitcast.1.at_ref, bf16[1024,3584]{1,0:T(8,128)(2,1)} %bitcast.17, bf16[1024,1024]{1,0:T(8,128)(2,1)} %bitcast.20, bf16[256,3584]{1,0:T(8,128)(2,1)} %bitcast.23, bf16[256,1024]{1,0:T(8,128)(2,1)} %bitcast.26, bf16[64,3584]{1,0:T(8,128)(2,1)} %bitcast.29, ...), custom_call_target="tpu_custom_call" | custom-call | flops 377487360 | bytes 6488064 | tf_op jit(solution)/shard_map/project_2_1/pallas_call | solution.py:133
  12.2 0.1 collective-permute-start.1
  12.3 0.6 %collective-permute-start.2 = (f32[320,128]{1,0:T(8,128)S(1)}, f32[320,128]{1,0:T(8,128)S(1)}, u32[]{:S(2)}, u32[]{:S(2)}) collective-permute-start(f32[320,128]{1,0:T(8,128)S(1)} %get-tuple-element.23), channel_id=1, source_target_pairs={{0,1},{1,0},{2,3},{3,2},{4,5},{5,4},{6,7},{7,6},{8,9},{9,8},{10,11... | collective-permute-start | bytes 491528 | tf_op jit(solution)/shard_map/ppermute | solution.py:35
  12.8 0.0 copy-start
  12.8 0.0 copy-start.1
  12.8 2.8 %project_0.1 = f32[320,128]{1,0:T(8,128)S(1)} custom-call(s32[1]{0:T(128)} %bitcast.1.at_ref, bf16[1024,3584]{1,0:T(8,128)(2,1)} %bitcast.18, bf16[1024,1024]{1,0:T(8,128)(2,1)} %bitcast.21, bf16[256,3584]{1,0:T(8,128)(2,1)} %bitcast.24, bf16[256,1024]{1,0:T(8,128)(2,1)} %bitcast.27, bf16[64,3584]{1,0:T(8,128)(2,1)} %bitcast.30, bf16[64,1024]{1,0:T(8,128)(2,1)} %bitcast.33), custom_call_target="tpu_custom_call" | custom-call | flops 188743680 | bytes 3538944 | tf_op jit(solution)/shard_map/project_0/pallas_call | solution.py:133
  15.6 0.0 collective-permute-done
  15.7 6.1 %collective-permute-done.1.refs_1_ = f32[320,128]{1,0:T(8,128)S(1)} collective-permute-done((f32[320,128]{1,0:T(8,128)S(1)}, f32[320,128]{1,0:T(8,128)S(1)}, u32[]{:S(2)}, u32[]{:S(2)}) %collective-permute-start.1) | collective-permute-done | bytes 163872 | tf_op jit(solution)/shard_map/ppermute | solution.py:35
  21.8 0.0 collective-permute-done.2.refs_2_
  21.8 0.0 copy-done
  21.8 0.0 copy-done.1
  21.8 0.4 outer.1
  22.2 0.1 collective-permute-start.3
  22.3 1.2 %collective-permute-done.3 = f32[2,7,8,128]{3,2,1,0:T(8,128)S(1)} collective-permute-done((f32[2,7,8,128]{3,2,1,0:T(8,128)S(1)}, f32[2,7,8,128]{3,2,1,0:T(8,128)S(1)}, u32[]{:S(2)}, u32[]{:S(2)}) %collective-permute-start.3) | collective-permute-done | bytes 57376 | tf_op jit(solution)/shard_map/ppermute | solution.py:35
  23.6 1.3 %collective-permute-start.4 = (f32[9,8,128]{2,1,0:T(8,128)S(1)}, f32[9,8,128]{2,1,0:T(8,128)S(1)}, u32[]{:S(2)}, u32[]{:S(2)}) collective-permute-start(f32[9,8,128]{2,1,0:T(8,128)S(1)} %get-tuple-element.32), channel_id=1, source_target_pairs={{0,12},{1,13},{2,14},{3,15},{4,8},{5,9},{6,10},{7,11},{8,4},{9,5},... | collective-permute-start | bytes 110600 | tf_op jit(solution)/shard_map/ppermute | solution.py:35
  24.9 2.2 %collective-permute-done.4 = f32[9,8,128]{2,1,0:T(8,128)S(1)} collective-permute-done((f32[9,8,128]{2,1,0:T(8,128)S(1)}, f32[9,8,128]{2,1,0:T(8,128)S(1)}, u32[]{:S(2)}, u32[]{:S(2)}) %collective-permute-start.4) | collective-permute-done | bytes 36896 | tf_op jit(solution)/shard_map/ppermute | solution.py:35
  27.1 1.3 %collective-permute-start.5 = (f32[13,8,128]{2,1,0:T(8,128)S(1)}, f32[13,8,128]{2,1,0:T(8,128)S(1)}, u32[]{:S(2)}, u32[]{:S(2)}) collective-permute-start(f32[13,8,128]{2,1,0:T(8,128)S(1)} %pad_maximum_fusion.2), channel_id=1, source_target_pairs={{0,20},{1,21},{2,22},{3,23},{4,16},{5,17},{6,18},{7,19},{8,28},{9,... | collective-permute-start | bytes 159752 | tf_op jit(solution)/shard_map/ppermute | solution.py:35
  28.5 0.0 collective-permute-start.6
  28.5 3.0 %collective-permute-start.7 = (f32[8,8,128]{2,1,0:T(8,128)S(1)}, f32[8,8,128]{2,1,0:T(8,128)S(1)}, u32[]{:S(2)}, u32[]{:S(2)}) collective-permute-start(f32[8,8,128]{2,1,0:T(8,128)S(1)} %pad_maximum_fusion.4), channel_id=1, source_target_pairs={{0,2},{1,3},{2,0},{3,1},{4,6},{5,7},{6,4},{7,5},{8,10},{9,11},{10,... | collective-permute-start | bytes 98312 | tf_op jit(solution)/shard_map/ppermute | solution.py:35
  31.5 0.0 collective-permute-done.5
  31.6 2.0 %collective-permute-start.9 = (f32[20,8,128]{2,1,0:T(8,128)S(1)}, f32[20,8,128]{2,1,0:T(8,128)S(1)}, u32[]{:S(2)}, u32[]{:S(2)}) collective-permute-start(f32[20,8,128]{2,1,0:T(8,128)S(1)} %pad_maximum_fusion.whole_ref.refs_0_), channel_id=1, source_target_pairs={{0,3},{1,2},{2,1},{3,0},{4,7},{5,6},{6,5},{7,4},{8,11},{9,10},{10,... | collective-permute-start | bytes 245768 | tf_op jit(solution)/shard_map/ppermute | solution.py:35
  33.6 0.0 collective-permute-start.8
  33.6 0.0 collective-permute-done.6.refs_0_
  33.6 0.0 collective-permute-done.7.refs_1_
  33.6 2.8 %collective-permute-start.10 = (f32[12,8,128]{2,1,0:T(8,128)S(1)}, f32[12,8,128]{2,1,0:T(8,128)S(1)}, u32[]{:S(2)}, u32[]{:S(2)}) collective-permute-start(f32[12,8,128]{2,1,0:T(8,128)S(1)} %pad_maximum_fusion.3), channel_id=1, source_target_pairs={{0,2},{1,3},{2,0},{3,1},{4,6},{5,7},{6,4},{7,5},{8,10},{9,11},{10,... | collective-permute-start | bytes 147464 | tf_op jit(solution)/shard_map/ppermute | solution.py:35
  36.4 0.1 rows.1.first_ref
  36.5 3.3 %collective-permute-done.8.refs_1_ = f32[12,8,128]{2,1,0:T(8,128)S(1)} collective-permute-done((f32[12,8,128]{2,1,0:T(8,128)S(1)}, f32[12,8,128]{2,1,0:T(8,128)S(1)}, u32[]{:S(2)}, u32[]{:S(2)}) %collective-permute-start.8) | collective-permute-done | bytes 49184 | tf_op jit(solution)/shard_map/ppermute | solution.py:35
  39.8 0.0 collective-permute-done.10.refs_3_
  39.8 0.0 collective-permute-done.9.refs_2_
  39.8 0.4 gram.1
  40.2 1.0 %collective-permute-start.11 = (f32[48,128]{1,0:T(8,128)S(1)}, f32[48,128]{1,0:T(8,128)S(1)}, u32[]{:S(2)}, u32[]{:S(2)}) collective-permute-start(f32[48,128]{1,0:T(8,128)S(1)} %gram.1), channel_id=1, source_target_pairs={{0,12},{1,13},{2,14},{3,15},{4,8},{5,9},{6,10},{7,11},{8,4},{9,5},... | collective-permute-start | bytes 73736 | tf_op jit(solution)/shard_map/ppermute | solution.py:35
  41.3 2.5 %collective-permute-done.11 = f32[48,128]{1,0:T(8,128)S(1)} collective-permute-done((f32[48,128]{1,0:T(8,128)S(1)}, f32[48,128]{1,0:T(8,128)S(1)}, u32[]{:S(2)}, u32[]{:S(2)}) %collective-permute-start.11) | collective-permute-done | bytes 24608 | tf_op jit(solution)/shard_map/ppermute | solution.py:35
  43.8 0.1 collective-permute-start.12
  43.9 1.1 %collective-permute-done.12.two_ref = f32[48,128]{1,0:T(8,128)S(1)} collective-permute-done((f32[48,128]{1,0:T(8,128)S(1)}, f32[48,128]{1,0:T(8,128)S(1)}, u32[]{:S(2)}, u32[]{:S(2)}) %collective-permute-start.12) | collective-permute-done | bytes 24608 | tf_op jit(solution)/shard_map/ppermute | solution.py:35
  45.0 1.3 %solve.1 = f32[2,16]{1,0:T(2,128)} custom-call(s32[1]{0:T(128)} %bitcast.low_ref, f32[48,128]{1,0:T(8,128)S(1)} %add.27.one_ref, f32[48,128]{1,0:T(8,128)S(1)} %collective-permute-done.12.two_ref), custom_call_target="tpu_custom_call" | custom-call | tf_op jit(solution)/shard_map/solve/pallas_call | solution.py:419
  (16 shorter events, 0.1 us)
Async XLA Ops:
  2.8 12.9 %collective-permute-start = (f32[320,128]{1,0:T(8,128)S(1)}, f32[320,128]{1,0:T(8,128)S(1)}, u32[]{:S(2)}, u32[]{:S(2)}) collective-permute-start(f32[320,128]{1,0:T(8,128)S(1)} %project_3.1), channel_id=1, source_target_pairs={{0,3},{1,2},{2,1},{3,0},{4,7},{5,6},{6,5},{7,4},{8,11},{9,10},{10,... | collective-permute-start | bytes 491528 | tf_op jit(solution)/shard_map/ppermute | solution.py:35
  12.2 9.6 %collective-permute-start.1 = (f32[320,128]{1,0:T(8,128)S(1)}, f32[320,128]{1,0:T(8,128)S(1)}, u32[]{:S(2)}, u32[]{:S(2)}) collective-permute-start(f32[320,128]{1,0:T(8,128)S(1)} %get-tuple-element.22), channel_id=1, source_target_pairs={{0,2},{1,3},{2,0},{3,1},{4,6},{5,7},{6,4},{7,5},{8,10},{9,11},{10,... | collective-permute-start | bytes 491528 | tf_op jit(solution)/shard_map/ppermute | solution.py:35
  12.3 9.5 %collective-permute-start.2 = (f32[320,128]{1,0:T(8,128)S(1)}, f32[320,128]{1,0:T(8,128)S(1)}, u32[]{:S(2)}, u32[]{:S(2)}) collective-permute-start(f32[320,128]{1,0:T(8,128)S(1)} %get-tuple-element.23), channel_id=1, source_target_pairs={{0,1},{1,0},{2,3},{3,2},{4,5},{5,4},{6,7},{7,6},{8,9},{9,8},{10,11... | collective-permute-start | bytes 491528 | tf_op jit(solution)/shard_map/ppermute | solution.py:35
  12.8 8.9 %copy-start = (s32[16,16]{1,0:T(8,128)S(1)}, s32[16,16]{1,0:T(8,128)}, u32[]{:S(2)}) copy-start(s32[16,16]{1,0:T(8,128)} %qids_ref.1) | copy-start | bytes 3076
  12.8 8.9 %copy-start.1 = (s32[8,128]{1,0:T(8,128)S(1)}, s32[8,128]{1,0:T(8,128)}, u32[]{:S(2)}) copy-start(s32[8,128]{1,0:T(8,128)} %ids_ref.1) | copy-start | bytes 12292
  22.2 1.3 %collective-permute-start.3 = (f32[2,7,8,128]{3,2,1,0:T(8,128)S(1)}, f32[2,7,8,128]{3,2,1,0:T(8,128)S(1)}, u32[]{:S(2)}, u32[]{:S(2)}) collective-permute-start(f32[2,7,8,128]{3,2,1,0:T(8,128)S(1)} %get-tuple-element.25), channel_id=1, source_target_pairs={{0,4},{1,5},{2,6},{3,7},{4,0},{5,1},{6,2},{7,3},{8,12},{9,13},{10,... | collective-permute-start | bytes 172040 | tf_op jit(solution)/shard_map/ppermute | solution.py:35
  23.6 3.5 %collective-permute-start.4 = (f32[9,8,128]{2,1,0:T(8,128)S(1)}, f32[9,8,128]{2,1,0:T(8,128)S(1)}, u32[]{:S(2)}, u32[]{:S(2)}) collective-permute-start(f32[9,8,128]{2,1,0:T(8,128)S(1)} %get-tuple-element.32), channel_id=1, source_target_pairs={{0,12},{1,13},{2,14},{3,15},{4,8},{5,9},{6,10},{7,11},{8,4},{9,5},... | collective-permute-start | bytes 110600 | tf_op jit(solution)/shard_map/ppermute | solution.py:35
  27.1 4.4 %collective-permute-start.5 = (f32[13,8,128]{2,1,0:T(8,128)S(1)}, f32[13,8,128]{2,1,0:T(8,128)S(1)}, u32[]{:S(2)}, u32[]{:S(2)}) collective-permute-start(f32[13,8,128]{2,1,0:T(8,128)S(1)} %pad_maximum_fusion.2), channel_id=1, source_target_pairs={{0,20},{1,21},{2,22},{3,23},{4,16},{5,17},{6,18},{7,19},{8,28},{9,... | collective-permute-start | bytes 159752 | tf_op jit(solution)/shard_map/ppermute | solution.py:35
  28.5 5.1 %collective-permute-start.6 = (f32[8,8,128]{2,1,0:T(8,128)S(1)}, f32[8,8,128]{2,1,0:T(8,128)S(1)}, u32[]{:S(2)}, u32[]{:S(2)}) collective-permute-start(f32[8,8,128]{2,1,0:T(8,128)S(1)} %pad_maximum_fusion.4), channel_id=1, source_target_pairs={{0,1},{1,0},{2,3},{3,2},{4,5},{5,4},{6,7},{7,6},{8,9},{9,8},{10,11... | collective-permute-start | bytes 98312 | tf_op jit(solution)/shard_map/ppermute | solution.py:35
  28.5 5.1 %collective-permute-start.7 = (f32[8,8,128]{2,1,0:T(8,128)S(1)}, f32[8,8,128]{2,1,0:T(8,128)S(1)}, u32[]{:S(2)}, u32[]{:S(2)}) collective-permute-start(f32[8,8,128]{2,1,0:T(8,128)S(1)} %pad_maximum_fusion.4), channel_id=1, source_target_pairs={{0,2},{1,3},{2,0},{3,1},{4,6},{5,7},{6,4},{7,5},{8,10},{9,11},{10,... | collective-permute-start | bytes 98312 | tf_op jit(solution)/shard_map/ppermute | solution.py:35
  31.6 8.2 %collective-permute-start.9 = (f32[20,8,128]{2,1,0:T(8,128)S(1)}, f32[20,8,128]{2,1,0:T(8,128)S(1)}, u32[]{:S(2)}, u32[]{:S(2)}) collective-permute-start(f32[20,8,128]{2,1,0:T(8,128)S(1)} %pad_maximum_fusion.whole_ref.refs_0_), channel_id=1, source_target_pairs={{0,3},{1,2},{2,1},{3,0},{4,7},{5,6},{6,5},{7,4},{8,11},{9,10},{10,... | collective-permute-start | bytes 245768 | tf_op jit(solution)/shard_map/ppermute | solution.py:35
  33.6 6.2 %collective-permute-start.8 = (f32[12,8,128]{2,1,0:T(8,128)S(1)}, f32[12,8,128]{2,1,0:T(8,128)S(1)}, u32[]{:S(2)}, u32[]{:S(2)}) collective-permute-start(f32[12,8,128]{2,1,0:T(8,128)S(1)} %pad_maximum_fusion.3), channel_id=1, source_target_pairs={{0,1},{1,0},{2,3},{3,2},{4,5},{5,4},{6,7},{7,6},{8,9},{9,8},{10,11... | collective-permute-start | bytes 147464 | tf_op jit(solution)/shard_map/ppermute | solution.py:35
  33.6 6.2 %collective-permute-start.10 = (f32[12,8,128]{2,1,0:T(8,128)S(1)}, f32[12,8,128]{2,1,0:T(8,128)S(1)}, u32[]{:S(2)}, u32[]{:S(2)}) collective-permute-start(f32[12,8,128]{2,1,0:T(8,128)S(1)} %pad_maximum_fusion.3), channel_id=1, source_target_pairs={{0,2},{1,3},{2,0},{3,1},{4,6},{5,7},{6,4},{7,5},{8,10},{9,11},{10,... | collective-permute-start | bytes 147464 | tf_op jit(solution)/shard_map/ppermute | solution.py:35
  40.2 3.5 %collective-permute-start.11 = (f32[48,128]{1,0:T(8,128)S(1)}, f32[48,128]{1,0:T(8,128)S(1)}, u32[]{:S(2)}, u32[]{:S(2)}) collective-permute-start(f32[48,128]{1,0:T(8,128)S(1)} %gram.1), channel_id=1, source_target_pairs={{0,12},{1,13},{2,14},{3,15},{4,8},{5,9},{6,10},{7,11},{8,4},{9,5},... | collective-permute-start | bytes 73736 | tf_op jit(solution)/shard_map/ppermute | solution.py:35
  43.8 1.2 %collective-permute-start.12 = (f32[48,128]{1,0:T(8,128)S(1)}, f32[48,128]{1,0:T(8,128)S(1)}, u32[]{:S(2)}, u32[]{:S(2)}) collective-permute-start(f32[48,128]{1,0:T(8,128)S(1)} %add.27.one_ref), channel_id=1, source_target_pairs={{0,4},{1,5},{2,6},{3,7},{4,0},{5,1},{6,2},{7,3},{8,12},{9,13},{10,... | collective-permute-start | bytes 73736 | tf_op jit(solution)/shard_map/ppermute | solution.py:35

commit v11 on v9

--- a/solution.py
+++ b/solution.py
@@ -49,7 +49,7 @@
     for side in (1, 0):
         train, query, buf, weight, held = sides[side]
         wide = buf.shape[1]
-        first = wide if side else 4 * tile
+        first = wide if side else 6 * tile
         second = (wide - first + tile) // (2 * tile) * tile
         for start, size in ((0, first), (first, second), (first + second, wide - first - second)):
             if not size:

time: 46.1 us -> 46.1 us (level)
  transfers between devices with their start and end apart: 13 -> 13, of which waited for: 6 -> 6; matrix products, arithmetic and copies ran while one was open for 0% -> 0% of each run, Pallas kernels for 13% -> 14%
where the time goes in v11:
time: 46.1 us; the launch traced here: 45.9 us
  starting transfers between devices  17.5 us (38%)
  waiting for transfers between devices  17.3 us (38%)
  Pallas kernels  10.8 us (23%)
    ppermute x13, starting transfers between devices, swap(): lax.ppermute(value, ('dp', 'tensor'), [(i, i ^ flip) for i in range(group...  17.5 us
    ppermute x13, waiting for transfers between devices, swap(): lax.ppermute(value, ('dp', 'tensor'), [(i, i ^ flip) for i in range(group...  17.3 us
    pallas_call x3, Pallas kernels, project(): call(functools.partial(project_kernel, mesh, parts, hops, tile), [jax.Sha...  8.6 us
    pallas_call x1, Pallas kernels, per_device(): call(functools.partial(solve_kernel, ntrain, rank * rank, share), jax.Sha...  1.29 us
  transfers between devices with their start and end apart: 13, of which 6 were waited for; matrix products, arithmetic and copies ran while one was open for 0% of the time, Pallas kernels for 14%

profile of v11, /device:TPU:0, one launch (start us, length us, event | category | flops | bytes accessed | tf_op | source)
XLA Modules:
  0.0 45.9 jit_solution(15040611834927359246)
XLA Ops:
  0.0 2.5 %project_3.1 = f32[320,128]{1,0:T(8,128)S(1)} custom-call(s32[1]{0:T(128)} %bitcast.1.at_ref, bf16[1024,3584]{1,0:T(8,128)(2,1)} %bitcast.16, bf16[1024,1024]{1,0:T(8,128)(2,1)} %bitcast.19, bf16[256,3584]{1,0:T(8,128)(2,1)} %bitcast.22, bf16[256,1024]{1,0:T(8,128)(2,1)} %bitcast.25, bf16[64,3584]{1,0:T(8,128)(2,1)} %bitcast.28, bf16[64,1024]{1,0:T(8,128)(2,1)} %bitcast.31), custom_call_target="tpu_custom_call" | custom-call | flops 188743680 | bytes 3538944 | tf_op jit(solution)/shard_map/project_3/pallas_call | solution.py:137
  2.5 5.1 %collective-permute-start = (f32[320,128]{1,0:T(8,128)S(1)}, f32[320,128]{1,0:T(8,128)S(1)}, u32[]{:S(2)}, u32[]{:S(2)}) collective-permute-start(f32[320,128]{1,0:T(8,128)S(1)} %project_3.1), channel_id=1, source_target_pairs={{0,3},{1,2},{2,1},{3,0},{4,7},{5,6},{6,5},{7,4},{8,11},{9,10},{10,... | collective-permute-start | bytes 491528 | tf_op jit(solution)/shard_map/ppermute | solution.py:35
  7.6 3.7 %project_2_1.1 = (f32[320,128]{1,0:T(8,128)S(1)}, f32[320,128]{1,0:T(8,128)S(1)}) custom-call(s32[1]{0:T(128)} %bitcast.1.at_ref, bf16[1024,3584]{1,0:T(8,128)(2,1)} %bitcast.17, bf16[1024,1024]{1,0:T(8,128)(2,1)} %bitcast.20, bf16[256,3584]{1,0:T(8,128)(2,1)} %bitcast.23, bf16[256,1024]{1,0:T(8,128)(2,1)} %bitcast.26, bf16[64,3584]{1,0:T(8,128)(2,1)} %bitcast.29, ...), custom_call_target="tpu_custom_call" | custom-call | flops 377487360 | bytes 6488064 | tf_op jit(solution)/shard_map/project_2_1/pallas_call | solution.py:137
  11.3 0.1 collective-permute-start.1
  11.3 0.6 %collective-permute-start.2 = (f32[320,128]{1,0:T(8,128)S(1)}, f32[320,128]{1,0:T(8,128)S(1)}, u32[]{:S(2)}, u32[]{:S(2)}) collective-permute-start(f32[320,128]{1,0:T(8,128)S(1)} %get-tuple-element.23), channel_id=1, source_target_pairs={{0,1},{1,0},{2,3},{3,2},{4,5},{5,4},{6,7},{7,6},{8,9},{9,8},{10,11... | collective-permute-start | bytes 491528 | tf_op jit(solution)/shard_map/ppermute | solution.py:35
  11.9 0.0 copy-start
  11.9 0.0 copy-start.1
  11.9 2.5 %project_0.1 = f32[320,128]{1,0:T(8,128)S(1)} custom-call(s32[1]{0:T(128)} %bitcast.1.at_ref, bf16[1024,3584]{1,0:T(8,128)(2,1)} %bitcast.18, bf16[1024,1024]{1,0:T(8,128)(2,1)} %bitcast.21, bf16[256,3584]{1,0:T(8,128)(2,1)} %bitcast.24, bf16[256,1024]{1,0:T(8,128)(2,1)} %bitcast.27, bf16[64,3584]{1,0:T(8,128)(2,1)} %bitcast.30, bf16[64,1024]{1,0:T(8,128)(2,1)} %bitcast.33), custom_call_target="tpu_custom_call" | custom-call | flops 188743680 | bytes 3538944 | tf_op jit(solution)/shard_map/project_0/pallas_call | solution.py:137
  14.4 0.0 collective-permute-done
  14.4 7.0 %collective-permute-done.1.refs_1_ = f32[320,128]{1,0:T(8,128)S(1)} collective-permute-done((f32[320,128]{1,0:T(8,128)S(1)}, f32[320,128]{1,0:T(8,128)S(1)}, u32[]{:S(2)}, u32[]{:S(2)}) %collective-permute-start.1) | collective-permute-done | bytes 163872 | tf_op jit(solution)/shard_map/ppermute | solution.py:35
  21.5 0.0 collective-permute-done.2.refs_2_
  21.5 0.0 copy-done
  21.5 0.0 copy-done.1
  21.5 0.4 outer.1
  21.9 0.1 collective-permute-start.3
  22.0 1.2 %collective-permute-done.3 = f32[2,7,8,128]{3,2,1,0:T(8,128)S(1)} collective-permute-done((f32[2,7,8,128]{3,2,1,0:T(8,128)S(1)}, f32[2,7,8,128]{3,2,1,0:T(8,128)S(1)}, u32[]{:S(2)}, u32[]{:S(2)}) %collective-permute-start.3) | collective-permute-done | bytes 57376 | tf_op jit(solution)/shard_map/ppermute | solution.py:35
  23.3 1.3 %collective-permute-start.4 = (f32[9,8,128]{2,1,0:T(8,128)S(1)}, f32[9,8,128]{2,1,0:T(8,128)S(1)}, u32[]{:S(2)}, u32[]{:S(2)}) collective-permute-start(f32[9,8,128]{2,1,0:T(8,128)S(1)} %get-tuple-element.32), channel_id=1, source_target_pairs={{0,12},{1,13},{2,14},{3,15},{4,8},{5,9},{6,10},{7,11},{8,4},{9,5},... | collective-permute-start | bytes 110600 | tf_op jit(solution)/shard_map/ppermute | solution.py:35
  24.6 2.2 %collective-permute-done.4 = f32[9,8,128]{2,1,0:T(8,128)S(1)} collective-permute-done((f32[9,8,128]{2,1,0:T(8,128)S(1)}, f32[9,8,128]{2,1,0:T(8,128)S(1)}, u32[]{:S(2)}, u32[]{:S(2)}) %collective-permute-start.4) | collective-permute-done | bytes 36896 | tf_op jit(solution)/shard_map/ppermute | solution.py:35
  26.8 1.3 %collective-permute-start.5 = (f32[13,8,128]{2,1,0:T(8,128)S(1)}, f32[13,8,128]{2,1,0:T(8,128)S(1)}, u32[]{:S(2)}, u32[]{:S(2)}) collective-permute-start(f32[13,8,128]{2,1,0:T(8,128)S(1)} %pad_maximum_fusion.2), channel_id=1, source_target_pairs={{0,20},{1,21},{2,22},{3,23},{4,16},{5,17},{6,18},{7,19},{8,28},{9,... | collective-permute-start | bytes 159752 | tf_op jit(solution)/shard_map/ppermute | solution.py:35
  28.2 0.0 collective-permute-start.6
  28.2 3.0 %collective-permute-start.7 = (f32[8,8,128]{2,1,0:T(8,128)S(1)}, f32[8,8,128]{2,1,0:T(8,128)S(1)}, u32[]{:S(2)}, u32[]{:S(2)}) collective-permute-start(f32[8,8,128]{2,1,0:T(8,128)S(1)} %pad_maximum_fusion.4), channel_id=1, source_target_pairs={{0,2},{1,3},{2,0},{3,1},{4,6},{5,7},{6,4},{7,5},{8,10},{9,11},{10,... | collective-permute-start | bytes 98312 | tf_op jit(solution)/shard_map/ppermute | solution.py:35
  31.2 0.0 collective-permute-done.5
  31.3 2.0 %collective-permute-start.9 = (f32[20,8,128]{2,1,0:T(8,128)S(1)}, f32[20,8,128]{2,1,0:T(8,128)S(1)}, u32[]{:S(2)}, u32[]{:S(2)}) collective-permute-start(f32[20,8,128]{2,1,0:T(8,128)S(1)} %pad_maximum_fusion.whole_ref.refs_0_), channel_id=1, source_target_pairs={{0,3},{1,2},{2,1},{3,0},{4,7},{5,6},{6,5},{7,4},{8,11},{9,10},{10,... | collective-permute-start | bytes 245768 | tf_op jit(solution)/shard_map/ppermute | solution.py:35
  33.3 0.0 collective-permute-start.8
  33.3 0.0 collective-permute-done.6.refs_0_
  33.3 0.0 collective-permute-done.7.refs_1_
  33.3 2.8 %collective-permute-start.10 = (f32[12,8,128]{2,1,0:T(8,128)S(1)}, f32[12,8,128]{2,1,0:T(8,128)S(1)}, u32[]{:S(2)}, u32[]{:S(2)}) collective-permute-start(f32[12,8,128]{2,1,0:T(8,128)S(1)} %pad_maximum_fusion.3), channel_id=1, source_target_pairs={{0,2},{1,3},{2,0},{3,1},{4,6},{5,7},{6,4},{7,5},{8,10},{9,11},{10,... | collective-permute-start | bytes 147464 | tf_op jit(solution)/shard_map/ppermute | solution.py:35
  36.1 0.1 rows.1.first_ref
  36.2 3.3 %collective-permute-done.8.refs_1_ = f32[12,8,128]{2,1,0:T(8,128)S(1)} collective-permute-done((f32[12,8,128]{2,1,0:T(8,128)S(1)}, f32[12,8,128]{2,1,0:T(8,128)S(1)}, u32[]{:S(2)}, u32[]{:S(2)}) %collective-permute-start.8) | collective-permute-done | bytes 49184 | tf_op jit(solution)/shard_map/ppermute | solution.py:35
  39.5 0.0 collective-permute-done.10.refs_3_
  39.5 0.0 collective-permute-done.9.refs_2_
  39.5 0.4 gram.1
  39.9 1.0 %collective-permute-start.11 = (f32[48,128]{1,0:T(8,128)S(1)}, f32[48,128]{1,0:T(8,128)S(1)}, u32[]{:S(2)}, u32[]{:S(2)}) collective-permute-start(f32[48,128]{1,0:T(8,128)S(1)} %gram.1), channel_id=1, source_target_pairs={{0,12},{1,13},{2,14},{3,15},{4,8},{5,9},{6,10},{7,11},{8,4},{9,5},... | collective-permute-start | bytes 73736 | tf_op jit(solution)/shard_map/ppermute | solution.py:35
  41.0 2.5 %collective-permute-done.11 = f32[48,128]{1,0:T(8,128)S(1)} collective-permute-done((f32[48,128]{1,0:T(8,128)S(1)}, f32[48,128]{1,0:T(8,128)S(1)}, u32[]{:S(2)}, u32[]{:S(2)}) %collective-permute-start.11) | collective-permute-done | bytes 24608 | tf_op jit(solution)/shard_map/ppermute | solution.py:35
  43.5 0.1 collective-permute-start.12
  43.6 1.1 %collective-permute-done.12.two_ref = f32[48,128]{1,0:T(8,128)S(1)} collective-permute-done((f32[48,128]{1,0:T(8,128)S(1)}, f32[48,128]{1,0:T(8,128)S(1)}, u32[]{:S(2)}, u32[]{:S(2)}) %collective-permute-start.12) | collective-permute-done | bytes 24608 | tf_op jit(solution)/shard_map/ppermute | solution.py:35
  44.7 1.3 %solve.1 = f32[2,16]{1,0:T(2,128)} custom-call(s32[1]{0:T(128)} %bitcast.low_ref, f32[48,128]{1,0:T(8,128)S(1)} %add.27.one_ref, f32[48,128]{1,0:T(8,128)S(1)} %collective-permute-done.12.two_ref), custom_call_target="tpu_custom_call" | custom-call | tf_op jit(solution)/shard_map/solve/pallas_call | solution.py:423
  (16 shorter events, 0.1 us)
Async XLA Ops:
  2.5 11.9 %collective-permute-start = (f32[320,128]{1,0:T(8,128)S(1)}, f32[320,128]{1,0:T(8,128)S(1)}, u32[]{:S(2)}, u32[]{:S(2)}) collective-permute-start(f32[320,128]{1,0:T(8,128)S(1)} %project_3.1), channel_id=1, source_target_pairs={{0,3},{1,2},{2,1},{3,0},{4,7},{5,6},{6,5},{7,4},{8,11},{9,10},{10,... | collective-permute-start | bytes 491528 | tf_op jit(solution)/shard_map/ppermute | solution.py:35
  11.3 10.2 %collective-permute-start.1 = (f32[320,128]{1,0:T(8,128)S(1)}, f32[320,128]{1,0:T(8,128)S(1)}, u32[]{:S(2)}, u32[]{:S(2)}) collective-permute-start(f32[320,128]{1,0:T(8,128)S(1)} %get-tuple-element.22), channel_id=1, source_target_pairs={{0,2},{1,3},{2,0},{3,1},{4,6},{5,7},{6,4},{7,5},{8,10},{9,11},{10,... | collective-permute-start | bytes 491528 | tf_op jit(solution)/shard_map/ppermute | solution.py:35
  11.3 10.1 %collective-permute-start.2 = (f32[320,128]{1,0:T(8,128)S(1)}, f32[320,128]{1,0:T(8,128)S(1)}, u32[]{:S(2)}, u32[]{:S(2)}) collective-permute-start(f32[320,128]{1,0:T(8,128)S(1)} %get-tuple-element.23), channel_id=1, source_target_pairs={{0,1},{1,0},{2,3},{3,2},{4,5},{5,4},{6,7},{7,6},{8,9},{9,8},{10,11... | collective-permute-start | bytes 491528 | tf_op jit(solution)/shard_map/ppermute | solution.py:35
  11.9 9.6 %copy-start = (s32[16,16]{1,0:T(8,128)S(1)}, s32[16,16]{1,0:T(8,128)}, u32[]{:S(2)}) copy-start(s32[16,16]{1,0:T(8,128)} %qids_ref.1) | copy-start | bytes 3076
  11.9 9.6 %copy-start.1 = (s32[8,128]{1,0:T(8,128)S(1)}, s32[8,128]{1,0:T(8,128)}, u32[]{:S(2)}) copy-start(s32[8,128]{1,0:T(8,128)} %ids_ref.1) | copy-start | bytes 12292
  21.9 1.3 %collective-permute-start.3 = (f32[2,7,8,128]{3,2,1,0:T(8,128)S(1)}, f32[2,7,8,128]{3,2,1,0:T(8,128)S(1)}, u32[]{:S(2)}, u32[]{:S(2)}) collective-permute-start(f32[2,7,8,128]{3,2,1,0:T(8,128)S(1)} %get-tuple-element.25), channel_id=1, source_target_pairs={{0,4},{1,5},{2,6},{3,7},{4,0},{5,1},{6,2},{7,3},{8,12},{9,13},{10,... | collective-permute-start | bytes 172040 | tf_op jit(solution)/shard_map/ppermute | solution.py:35
  23.3 3.5 %collective-permute-start.4 = (f32[9,8,128]{2,1,0:T(8,128)S(1)}, f32[9,8,128]{2,1,0:T(8,128)S(1)}, u32[]{:S(2)}, u32[]{:S(2)}) collective-permute-start(f32[9,8,128]{2,1,0:T(8,128)S(1)} %get-tuple-element.32), channel_id=1, source_target_pairs={{0,12},{1,13},{2,14},{3,15},{4,8},{5,9},{6,10},{7,11},{8,4},{9,5},... | collective-permute-start | bytes 110600 | tf_op jit(solution)/shard_map/ppermute | solution.py:35
  26.8 4.4 %collective-permute-start.5 = (f32[13,8,128]{2,1,0:T(8,128)S(1)}, f32[13,8,128]{2,1,0:T(8,128)S(1)}, u32[]{:S(2)}, u32[]{:S(2)}) collective-permute-start(f32[13,8,128]{2,1,0:T(8,128)S(1)} %pad_maximum_fusion.2), channel_id=1, source_target_pairs={{0,20},{1,21},{2,22},{3,23},{4,16},{5,17},{6,18},{7,19},{8,28},{9,... | collective-permute-start | bytes 159752 | tf_op jit(solution)/shard_map/ppermute | solution.py:35
  28.2 5.1 %collective-permute-start.6 = (f32[8,8,128]{2,1,0:T(8,128)S(1)}, f32[8,8,128]{2,1,0:T(8,128)S(1)}, u32[]{:S(2)}, u32[]{:S(2)}) collective-permute-start(f32[8,8,128]{2,1,0:T(8,128)S(1)} %pad_maximum_fusion.4), channel_id=1, source_target_pairs={{0,1},{1,0},{2,3},{3,2},{4,5},{5,4},{6,7},{7,6},{8,9},{9,8},{10,11... | collective-permute-start | bytes 98312 | tf_op jit(solution)/shard_map/ppermute | solution.py:35
  28.2 5.1 %collective-permute-start.7 = (f32[8,8,128]{2,1,0:T(8,128)S(1)}, f32[8,8,128]{2,1,0:T(8,128)S(1)}, u32[]{:S(2)}, u32[]{:S(2)}) collective-permute-start(f32[8,8,128]{2,1,0:T(8,128)S(1)} %pad_maximum_fusion.4), channel_id=1, source_target_pairs={{0,2},{1,3},{2,0},{3,1},{4,6},{5,7},{6,4},{7,5},{8,10},{9,11},{10,... | collective-permute-start | bytes 98312 | tf_op jit(solution)/shard_map/ppermute | solution.py:35
  31.3 8.2 %collective-permute-start.9 = (f32[20,8,128]{2,1,0:T(8,128)S(1)}, f32[20,8,128]{2,1,0:T(8,128)S(1)}, u32[]{:S(2)}, u32[]{:S(2)}) collective-permute-start(f32[20,8,128]{2,1,0:T(8,128)S(1)} %pad_maximum_fusion.whole_ref.refs_0_), channel_id=1, source_target_pairs={{0,3},{1,2},{2,1},{3,0},{4,7},{5,6},{6,5},{7,4},{8,11},{9,10},{10,... | collective-permute-start | bytes 245768 | tf_op jit(solution)/shard_map/ppermute | solution.py:35
  33.3 6.2 %collective-permute-start.8 = (f32[12,8,128]{2,1,0:T(8,128)S(1)}, f32[12,8,128]{2,1,0:T(8,128)S(1)}, u32[]{:S(2)}, u32[]{:S(2)}) collective-permute-start(f32[12,8,128]{2,1,0:T(8,128)S(1)} %pad_maximum_fusion.3), channel_id=1, source_target_pairs={{0,1},{1,0},{2,3},{3,2},{4,5},{5,4},{6,7},{7,6},{8,9},{9,8},{10,11... | collective-permute-start | bytes 147464 | tf_op jit(solution)/shard_map/ppermute | solution.py:35
  33.3 6.2 %collective-permute-start.10 = (f32[12,8,128]{2,1,0:T(8,128)S(1)}, f32[12,8,128]{2,1,0:T(8,128)S(1)}, u32[]{:S(2)}, u32[]{:S(2)}) collective-permute-start(f32[12,8,128]{2,1,0:T(8,128)S(1)} %pad_maximum_fusion.3), channel_id=1, source_target_pairs={{0,2},{1,3},{2,0},{3,1},{4,6},{5,7},{6,4},{7,5},{8,10},{9,11},{10,... | collective-permute-start | bytes 147464 | tf_op jit(solution)/shard_map/ppermute | solution.py:35
  39.9 3.5 %collective-permute-start.11 = (f32[48,128]{1,0:T(8,128)S(1)}, f32[48,128]{1,0:T(8,128)S(1)}, u32[]{:S(2)}, u32[]{:S(2)}) collective-permute-start(f32[48,128]{1,0:T(8,128)S(1)} %gram.1), channel_id=1, source_target_pairs={{0,12},{1,13},{2,14},{3,15},{4,8},{5,9},{6,10},{7,11},{8,4},{9,5},... | collective-permute-start | bytes 73736 | tf_op jit(solution)/shard_map/ppermute | solution.py:35
  43.5 1.2 %collective-permute-start.12 = (f32[48,128]{1,0:T(8,128)S(1)}, f32[48,128]{1,0:T(8,128)S(1)}, u32[]{:S(2)}, u32[]{:S(2)}) collective-permute-start(f32[48,128]{1,0:T(8,128)S(1)} %add.27.one_ref), channel_id=1, source_target_pairs={{0,4},{1,5},{2,6},{3,7},{4,0},{5,1},{6,2},{7,3},{8,12},{9,13},{10,... | collective-permute-start | bytes 73736 | tf_op jit(solution)/shard_map/ppermute | solution.py:35
